TPU v7x, 32 devices: a whole 2x2x4 slice. The times are simulated.
32 devices in a mesh: dp: 16 (over z, y, x), seq: 2 (over core).
Axes of the slice: x: 2, y: 2, z: 4, core: 2. Of those that a mesh axis runs over, the one named last changes fastest.
Arguments:
- hidden_in: bfloat16 [16, 512, 768], P('dp', 'seq'), may hold values from -6 to 6
- w_qkv: bfloat16 [768, 2304], replicated, may hold values from -0.21875 to 0.21875
- b_qv: bfloat16 [2, 768], replicated, may hold values from -3 to 3
- w_o: bfloat16 [768, 768], replicated, may hold values from -2.5 to 2.5
- b_o: bfloat16 [768], replicated, may hold values from -3 to 3
- ln1_gain: bfloat16 [768], replicated, may hold values from 0.099609375 to 1.8984375
- ln1_bias: bfloat16 [768], replicated, may hold values from -3 to 3
- w_in: bfloat16 [768, 3072], replicated, may hold values from -0.21875 to 0.21875
- b_in: bfloat16 [3072], replicated, may hold values from -3 to 3
- w_out: bfloat16 [3072, 768], replicated, may hold values from -0.109375 to 0.109375
- b_out: bfloat16 [768], replicated, may hold values from -3 to 3
- ln2_gain: bfloat16 [768], replicated, may hold values from 0.099609375 to 1.8984375
- ln2_bias: bfloat16 [768], replicated, may hold values from -3 to 3
- seg_lengths: int32 [16, 4], P('dp'), may hold values from 1 to 509, as said below
- cotangent: bfloat16 [16, 512, 768], P('dp', 'seq'), may hold values from -6 to 6
Outputs:
- output: bfloat16 [16, 512, 768], P('dp', 'seq')
- pooled: float32 [16, 4, 768], P('dp')
- d_input: float32 [16, 512, 768], P('dp', 'seq')
- d_w_qkv: float32 [1769472], P(('dp', 'seq'))
- d_w_o: float32 [589824], P(('dp', 'seq'))
- d_w_in: float32 [2359296], P(('dp', 'seq'))
- d_w_out: float32 [2359296], P(('dp', 'seq'))
- d_b_qv: float32 [2, 768], replicated
- d_b_o: float32 [768], replicated
- d_ln1_gain: float32 [768], replicated
- d_ln1_bias: float32 [768], replicated
- d_b_in: float32 [3072], replicated
- d_b_out: float32 [768], replicated
- d_ln2_gain: float32 [768], replicated
- d_ln2_bias: float32 [768], replicated
Inputs may be any that keep to these rules, and one draw needn't show every extreme that they name: `seg_lengths`: each row's 4 lengths add up to 512; no text ends at position 255, so some text of every row covers positions 255 and 256.
All inputs are finite; a program needn't handle non-finite values.
Results may differ from a plain program's by a relative error of at most 0.012.
Values may be sent and summed in bfloat16 or wider, within the bound.
No kernel may reach another device: no remote copies, remote signals or barrier semaphores. Data moves between devices by JAX's collectives and lax.ppermute only.
A program may use at most 192 MiB of HBM per device.

v0:
```python
import math

import jax
import jax.numpy as jnp
from jax import lax
from jax.sharding import PartitionSpec as P

HEADS = 12


EPSILON = 1e-12


def norm_forward(total, gain_vec, shift_vec):
    centered = total - jnp.mean(total, axis=-1, keepdims=True)
    inverse = lax.rsqrt(jnp.mean(centered * centered, axis=-1, keepdims=True) + EPSILON)
    normal = centered * inverse
    return (normal * gain_vec.astype(jnp.float32) + shift_vec.astype(jnp.float32), normal, inverse)


def norm_backward(grad_in, normal, inverse, gain_vec):
    d_gain = jnp.sum(grad_in * normal, axis=0)
    d_shift = jnp.sum(grad_in, axis=0)
    scaled = grad_in * gain_vec.astype(jnp.float32)
    grad_total = inverse * (
        scaled
        - jnp.mean(scaled, axis=-1, keepdims=True)
        - normal * jnp.mean(scaled * normal, axis=-1, keepdims=True)
    )
    return (grad_total, d_gain, d_shift)


def column_sums(matrix):
    return jnp.sum(matrix.astype(jnp.float32), axis=0)


def transposed_dot(left, right):
    return lax.dot_general(
        left, right, (((0,), (0,)), ((), ())), preferred_element_type=jnp.float32
    )


def segment_ids(lengths_in, positions):
    end_points = jnp.cumsum(lengths_in, axis=-1, dtype=jnp.int32)
    return jnp.sum((positions[None, :, None] >= end_points[:, None, :]).astype(jnp.int32), axis=-1)


def on_device(
    hidden_in,
    w_qkv,
    b_qv,
    w_o,
    b_o,
    ln1_gain,
    ln1_bias,
    w_in,
    b_in,
    w_out,
    b_out,
    ln2_gain,
    ln2_bias,
    seg_lengths,
    cotangent,
):
    row_count, half_len, model_width = hidden_in.shape
    length = half_len * lax.axis_size("seq")
    head_dim = model_width // HEADS
    scaling = 1.0 / math.sqrt(head_dim)
    local_pos = lax.axis_index("seq") * half_len + jnp.arange(half_len, dtype=jnp.int32)
    row_pos = jnp.arange(length, dtype=jnp.int32)
    local_ids = segment_ids(seg_lengths, local_pos)
    row_ids = segment_ids(seg_lengths, row_pos)
    same_seg = local_ids[:, :, None] == row_ids[:, None, :]
    flat_in = hidden_in.reshape(-1, model_width)
    qkv_lin = jnp.dot(flat_in, w_qkv, preferred_element_type=jnp.float32)
    bias_qv = b_qv.astype(jnp.float32)
    queries = (qkv_lin[:, :model_width] + bias_qv[0]).astype(jnp.bfloat16)
    keys_loc = qkv_lin[:, model_width : 2 * model_width].astype(jnp.bfloat16)
    values_loc = (qkv_lin[:, 2 * model_width :] + bias_qv[1]).astype(jnp.bfloat16)
    keys_row, values_row = (
        lax.all_gather(
            keys_loc.reshape(row_count, half_len, model_width), "seq", axis=1, tiled=True
        ),
        lax.all_gather(
            values_loc.reshape(row_count, half_len, model_width), "seq", axis=1, tiled=True
        ),
    )
    query_heads = queries.reshape(row_count, half_len, HEADS, head_dim)
    key_heads = keys_row.reshape(row_count, length, HEADS, head_dim)
    value_heads = values_row.reshape(row_count, length, HEADS, head_dim)
    raw = jnp.einsum("rphe,rqhe->rhpq", query_heads, key_heads, preferred_element_type=jnp.float32)
    scores = jnp.where(same_seg[:, None], raw * scaling, -1e30)
    row_max = jnp.max(scores, axis=-1, keepdims=True)
    expons = jnp.exp(scores - row_max)
    row_sum = jnp.sum(expons, axis=-1, keepdims=True)
    logsum = row_max + jnp.log(row_sum)
    probs_low = (expons / row_sum).astype(jnp.bfloat16)
    attended = jnp.einsum(
        "rhpq,rqhe->rphe", probs_low, value_heads, preferred_element_type=jnp.float32
    )
    attended = attended.reshape(-1, model_width).astype(jnp.bfloat16)
    branch = jnp.dot(attended, w_o, preferred_element_type=jnp.float32) + b_o.astype(jnp.float32)
    middle, normal_one, inverse_one = norm_forward(
        flat_in.astype(jnp.float32) + branch, ln1_gain, ln1_bias
    )
    middle_low = middle.astype(jnp.bfloat16)
    upper = jnp.dot(middle_low, w_in, preferred_element_type=jnp.float32) + b_in.astype(jnp.float32)
    active = jax.nn.gelu(upper, approximate=False).astype(jnp.bfloat16)
    down = jnp.dot(active, w_out, preferred_element_type=jnp.float32) + b_out.astype(jnp.float32)
    final, normal_two, inverse_two = norm_forward(middle + down, ln2_gain, ln2_bias)
    output = final.astype(jnp.bfloat16).reshape(row_count, half_len, model_width)
    slots = jnp.arange(seg_lengths.shape[1], dtype=jnp.int32)
    member = (local_ids[:, None, :] == slots[None, :, None]).astype(jnp.float32)
    partial_pool = jnp.einsum(
        "rsp,rpd->rsd",
        member,
        final.reshape(row_count, half_len, model_width),
        precision=lax.Precision.HIGHEST,
    )
    pooled_total = lax.psum(partial_pool, "seq")
    pooled = pooled_total / seg_lengths[:, :, None].astype(jnp.float32)
    grad_out = cotangent.reshape(-1, model_width).astype(jnp.float32)
    grad_sum2, d_ln2_gain, d_ln2_bias = norm_backward(grad_out, normal_two, inverse_two, ln2_gain)
    grad_down = grad_sum2.astype(jnp.bfloat16)
    d_b_out = column_sums(grad_down)
    d_w_out = transposed_dot(active, grad_down)
    grad_active = lax.dot_general(
        grad_down, w_out, (((1,), (1,)), ((), ())), preferred_element_type=jnp.float32
    )
    gelu_value, gelu_pull = jax.vjp(lambda inner: jax.nn.gelu(inner, approximate=False), upper)
    grad_upper = gelu_pull(grad_active)[0].astype(jnp.bfloat16)
    d_b_in = column_sums(grad_upper)
    d_w_in = transposed_dot(middle_low, grad_upper)
    grad_mid = grad_sum2 + lax.dot_general(
        grad_upper, w_in, (((1,), (1,)), ((), ())), preferred_element_type=jnp.float32
    )
    grad_sum1, d_ln1_gain, d_ln1_bias = norm_backward(grad_mid, normal_one, inverse_one, ln1_gain)
    grad_branch = grad_sum1.astype(jnp.bfloat16)
    d_b_o = column_sums(grad_branch)
    d_w_o = transposed_dot(attended, grad_branch)
    grad_att = lax.dot_general(
        grad_branch, w_o, (((1,), (1,)), ((), ())), preferred_element_type=jnp.float32
    )
    grad_att = grad_att.astype(jnp.bfloat16).reshape(row_count, half_len, HEADS, head_dim)
    raw_again = jnp.einsum(
        "rphe,rqhe->rhpq", query_heads, key_heads, preferred_element_type=jnp.float32
    )
    probs_again = jnp.exp(jnp.where(same_seg[:, None], raw_again * scaling, -1e30) - logsum)
    grad_probs = jnp.einsum(
        "rphe,rqhe->rhpq", grad_att, value_heads, preferred_element_type=jnp.float32
    )
    inner_sum = jnp.sum(probs_again * grad_probs, axis=-1, keepdims=True)
    grad_raw = (probs_again * (grad_probs - inner_sum) * scaling).astype(jnp.bfloat16)
    grad_query = jnp.einsum(
        "rhpq,rqhe->rphe", grad_raw, key_heads, preferred_element_type=jnp.float32
    )
    grad_query = grad_query.reshape(-1, model_width).astype(jnp.bfloat16)
    key_part = jnp.einsum(
        "rhpq,rphe->rqhe", grad_raw, query_heads, preferred_element_type=jnp.float32
    )
    value_part = jnp.einsum(
        "rhpq,rphe->rqhe",
        probs_again.astype(jnp.bfloat16),
        grad_att,
        preferred_element_type=jnp.float32,
    )
    grad_key, grad_value = (
        lax.psum_scatter(
            key_part.reshape(row_count, length, model_width), "seq", scatter_dimension=1, tiled=True
        ),
        lax.psum_scatter(
            value_part.reshape(row_count, length, model_width),
            "seq",
            scatter_dimension=1,
            tiled=True,
        ),
    )
    grad_key = grad_key.reshape(-1, model_width).astype(jnp.bfloat16)
    grad_value = grad_value.reshape(-1, model_width).astype(jnp.bfloat16)
    grad_qkv = jnp.concatenate([grad_query, grad_key, grad_value], axis=1)
    d_w_qkv = transposed_dot(flat_in, grad_qkv)
    d_b_qv = jnp.stack([column_sums(grad_query), column_sums(grad_value)])
    grad_input = grad_sum1 + lax.dot_general(
        grad_qkv, w_qkv, (((1,), (1,)), ((), ())), preferred_element_type=jnp.float32
    )
    d_input = grad_input.reshape(row_count, half_len, model_width)
    flat_qkv = d_w_qkv.reshape(-1)
    flat_o = d_w_o.reshape(-1)
    flat_in_w = d_w_in.reshape(-1)
    flat_out_w = d_w_out.reshape(-1)
    sum_qkv, sum_o, sum_in, sum_out = (
        lax.psum_scatter(flat_qkv, ("dp", "seq"), scatter_dimension=0, tiled=True),
        lax.psum_scatter(flat_o, ("dp", "seq"), scatter_dimension=0, tiled=True),
        lax.psum_scatter(flat_in_w, ("dp", "seq"), scatter_dimension=0, tiled=True),
        lax.psum_scatter(flat_out_w, ("dp", "seq"), scatter_dimension=0, tiled=True),
    )
    vec_qv, vec_o, vec_g1, vec_c1, vec_in, vec_out, vec_g2, vec_c2 = lax.psum(
        (d_b_qv, d_b_o, d_ln1_gain, d_ln1_bias, d_b_in, d_b_out, d_ln2_gain, d_ln2_bias),
        ("dp", "seq"),
    )
    return (
        output,
        pooled,
        d_input,
        sum_qkv,
        sum_o,
        sum_in,
        sum_out,
        vec_qv,
        vec_o,
        vec_g1,
        vec_c1,
        vec_in,
        vec_out,
        vec_g2,
        vec_c2,
    )


def solution(mesh):
    in_specs = (
        P("dp", "seq", None),
        P(),
        P(),
        P(),
        P(),
        P(),
        P(),
        P(),
        P(),
        P(),
        P(),
        P(),
        P(),
        P("dp", None),
        P("dp", "seq", None),
    )
    out_specs = (
        P("dp", "seq", None),
        P("dp", None, None),
        P("dp", "seq", None),
        P(("dp", "seq")),
        P(("dp", "seq")),
        P(("dp", "seq")),
        P(("dp", "seq")),
        P(),
        P(),
        P(),
        P(),
        P(),
        P(),
        P(),
        P(),
    )
    return jax.shard_map(
        on_device, mesh=mesh, in_specs=in_specs, out_specs=out_specs, check_vma=False
    )
```

profile of v0, /device:TPU:0, one launch (start us, length us, event | category | flops | bytes accessed | tf_op | source)
XLA Modules:
  0.0 634.1 jit_solution(13062739199785483457)
XLA Ops:
  22.6 4.4 all-gather.1
  29.3 4.0 all-gather
  36.5 2.5 fusion.76
  42.3 2.4 fusion.34
  45.7 8.1 %multiply_convert_fusion.1 = (bf16[256,3072]{1,0:T(8,128)(2,1)S(1)}, f32[256,3072]{1,0:T(8,128)S(1)}, f32[256,3072]{1,0:T(8,128)S(1)}) fusion(f32[3072]{0:T(1024)S(1)} %copy-done.23, bf16[768,3072]{1,0:T(8,128)(2,1)S(1)} %bitcast.113, f32[256,768]{1,0:T(8,128)S(1)} %get-tuple-element.50, f32[768]{0:T(1024)S(1)} %convert_element_type.179, ...), kind=kOutput, calls=%fused_computation.23 | convolution fusion | flops 1260847104 | bytes 13389824 | tf_op jit(solution)/shard_map/dot_general | solution.py:107
  58.4 3.0 convert_reduce_fusion
  68.6 5.1 fusion.12
  73.8 4.9 fusion.81
  78.7 24.2 %fusion.7 = f32[12,64,512]{2,1,0:T(8,128)} fusion(bf16[256,12,64]{0,2,1:T(8,128)(2,1)} %bitcast.105, f32[12,256,512]{2,1,0:T(8,128)} %fusion.81, f32[12,256,512]{2,1,0:T(8,128)} %copy-done.1, f32[12,256]{1,0:T(8,128)} %log_add_fusion), kind=kOutput, calls=%fused_computation.13 | convolution fusion | flops 212340224 | bytes 14561280 | tf_op jit(solution)/shard_map/rhpq,rphe->rqhe/dot_general | solution.py:158
  102.9 3.2 fusion.61
  106.1 3.5 reshape.421
  109.6 3.3 convolution_bitcast_fusion.1
  112.8 5.8 copy.53
  118.7 5.2 fusion.64
  123.9 10.8 %reshape.423 = f32[2359296]{0:T(1024)} reshape(f32[3072,768]{1,0:T(8,128)} %fusion.64) | data formatting | bytes 18874368 | tf_op jit(solution)/shard_map/reshape | solution.py:190
  134.6 23.9 %convert_reduce_fusion.5 = (f32[12,64]{1,0:T(8,128)}, bf16[12,64,256]{2,1,0:T(8,128)(2,1)}) fusion(bf16[512,12,64]{0,2,1:T(8,128)(2,1)} %bitcast.98, f32[12,256,512]{2,1,0:T(8,128)} %fusion.81, f32[12,256,512]{2,1,0:T(8,128)} %copy-done.1, f32[12,256]{1,0:T(8,128)} %log_add_fusion), kind=kOutput, calls=%fused_computation.72 | convolution fusion | flops 212929280 | bytes 13777920 | tf_op jit(solution)/shard_map/rhpq,rqhe->rphe/dot_general | solution.py:154
  158.5 2.5 convert_reduce_fusion.4
  163.0 5.2 convolution_bitcast_fusion
  168.2 8.0 %copy.52 = f32[768,2304]{1,0:T(8,128)} copy(f32[768,2304]{0,1:T(8,128)} %convolution_bitcast_fusion) | data formatting | bytes 14155776 | tf_op jit(solution)/shard_map/dot_general | solution.py:38
  176.2 7.9 %reshape.420 = f32[1769472]{0:T(1024)} reshape(f32[768,2304]{1,0:T(8,128)} %copy.52) | data formatting | bytes 14155776 | tf_op jit(solution)/shard_map/reshape | solution.py:187
  187.8 4.2 psum.63
  195.9 45.8 %all-reduce.4 = (f32[2,768]{1,0:T(2,128)}, f32[768]{0:T(1024)}, f32[768]{0:T(1024)}, f32[768]{0:T(1024)}, f32[3072]{0:T(1024)}, /*index=5*/f32[768]{0:T(1024)}, f32[768]{0:T(1024)}, f32[768]{0:T(1024)}) all-reduce(f32[2,768]{1,0:T(2,128)S(1)} %pad_maximum_fusion.3, ...), channel_id=1, replica_groups=mesh['dp'=16,'seq'=2] {'dp','seq'}, use_global_device_ids=true, to_apply=%region_23.24 | all-reduce | flops 9216 | bytes 73728 | tf_op jit(solution)/shard_map/psum | solution.py:197
  241.8 3.9 fusion.29
  245.6 375.0 %all-reduce.8.cloned.1.call-done = (f32[1769472]{0:T(1024)}, f32[589824]{0:T(1024)}, f32[2359296]{0:T(1024)}, f32[2359296]{0:T(1024)}) async-done(((f32[1769472]{0:T(1024)}, f32[589824]{0:T(1024)}, f32[2359296]{0:T(1024)}, f32[2359296]{0:T(1024)}), (f32[1769472]{0:T(1024)}, f32[589824]{0:T(1024)}, f32[2359296]{0:T(1024)}, f32[2359296]{0:T(1024)})) %all-reduce.8.cloned.1.call-update) | async-done | bytes 28311568
  (119 shorter events, 52.8 us)
Async XLA Ops:
  7.2 9.7 %copy-start = (bf16[768,2304]{1,0:T(8,128)(2,1)S(1)}, bf16[768,2304]{1,0:T(8,128)(2,1)}, u32[]{:S(2)}) copy-start(bf16[768,2304]{1,0:T(8,128)(2,1)} %param.16) | copy-start | bytes 10616836
  7.2 151.3 %reduce-scatter.5.cloned.1.call-start = ((), (), s32[]{:S(2)}) async-start(), calls=%async_computation.3 | async-start | bytes 2359296 | tf_op jit(solution)/shard_map/reduce_scatter | solution.py:171
  39.0 3.2 copy-start.1
  39.0 3.2 copy-start.10
  39.1 6.5 %slice-start.2 = ((s8[4718592]{0:T(1024)(128)(4,1)}), s8[4194304]{0:T(1024)(128)(4,1)S(1)}, s32[]{:S(2)}) async-start(s8[4718592]{0:T(1024)(128)(4,1)} %bitcast.112), calls=%async_computation.7 | async-start | bytes 8388608
  42.3 2.4 copy-start.5
  42.3 2.4 copy-start.6
  42.3 2.4 copy-start.21
  42.3 3.3 slice-start.3
  44.7 9.1 %copy-start.14 = (bf16[12,64,256]{2,1,0:T(8,128)(2,1)}, bf16[12,64,256]{2,1,0:T(8,128)(2,1)S(1)}, u32[]{:S(2)}) copy-start(bf16[12,64,256]{2,1,0:T(8,128)(2,1)S(1)} %fusion.34) | copy-start | bytes 1179652
  44.7 9.1 %slice-start = ((s8[4718592]{0:T(1024)(128)(4,1)}), s8[4194304]{0:T(1024)(128)(4,1)S(1)}, s32[]{:S(2)}) async-start(s8[4718592]{0:T(1024)(128)(4,1)} %bitcast.110), calls=%async_computation.5 | async-start | bytes 8388608
  45.3 18.3 %copy-start.3 = (f32[256,768]{1,0:T(8,128)}, f32[256,768]{1,0:T(8,128)S(1)}, u32[]{:S(2)}) copy-start(f32[256,768]{1,0:T(8,128)S(1)} %get-tuple-element.50) | copy-start | bytes 2359300
  45.3 18.3 %copy-start.18 = (f32[256]{0:T(256)}, f32[256]{0:T(256)S(1)}, u32[]{:S(2)}) copy-start(f32[256]{0:T(256)S(1)} %broadcast_multiply_fusion.5) | copy-start | bytes 3076
  45.6 18.0 %copy-start.22 = (f32[256]{0:T(256)}, f32[256]{0:T(256)S(1)}, u32[]{:S(2)}) copy-start(f32[256]{0:T(256)S(1)} %add_rsqrt_fusion.1) | copy-start | bytes 3076
  45.6 8.2 %copy-start.24 = (f32[768]{0:T(1024)S(1)}, f32[768]{0:T(1024)}, u32[]{:S(2)}) copy-start(f32[768]{0:T(1024)} %convert_element_type.183) | copy-start | bytes 9220
  45.6 8.2 %slice-start.1 = ((s8[4718592]{0:T(1024)(128)(4,1)}), s8[524288]{0:T(1024)(128)(4,1)S(1)}, s32[]{:S(2)}) async-start(s8[4718592]{0:T(1024)(128)(4,1)} %bitcast.110), calls=%async_computation.6 | async-start | bytes 1048576
  55.4 2.9 copy-start.16
  55.7 2.7 copy-start.19
  58.3 3.0 copy-start.8
  61.4 2.2 copy-start.15
  73.7 87.3 %reduce-scatter.3.cloned.1.call-start = ((), (), s32[]{:S(2)}) async-start(), calls=%async_computation.2 | async-start | bytes 2359296 | tf_op jit(solution)/shard_map/reduce_scatter | solution.py:168
  102.9 517.7 %all-reduce.8.cloned.1.call-start = ((), (), s32[]{:S(2)}) async-start(), calls=%async_computation.4 | async-start | bytes 56623104
  112.8 5.9 copy-start.9
  112.8 5.8 copy-start.12
  (8 other events, 10.1 us)
Sparse Core Ops, SparseCore 0:
  73.9 11.6 reduce-scatter.4
  103.0 11.8 reduce-scatter.2
  184.3 436.3 all-reduce.7
where the time goes:
time: 640 us; the launch traced here: 634 us
  waiting for transfers between devices  375 us (59%)
  matrix products  105 us (16%)
  blocking collectives  58.4 us (9%)
  local copies, waits for them, and re-layouts  56.6 us (9%)
  other arithmetic  24.5 us (4%)
  between operations  14.6 us (2%)
    unnamed x4, waiting for transfers between devices  375 us
    psum x1, blocking collectives, on_device(): lax.psum((d_b_qv, d_b_o, d_ln1_gain, d_ln1_bias, d_b_in, d_b_out, d_ln2_g...  45.8 us
    dot_general x1, matrix products, on_device(): jnp.einsum('rhpq,rphe->rqhe', grad_raw, query_heads, preferred_element_ty...  24.2 us
    dot_general x1, matrix products, on_device(): jnp.einsum('rhpq,rqhe->rphe', grad_raw, key_heads, preferred_element_type...  23.9 us
    dot_general x4, matrix products, transposed_dot(): lax.dot_general(left, right, (((0,), (0,)), ((), ())), preferred_element_...  16.8 us
    unnamed x63, local copies, waits for them, and re-layouts  15.1 us
  transfers between devices with their start and end apart: 3, of which 1 were waited for; matrix products, arithmetic and copies ran while one was open for 16% of the time, Pallas kernels for 0%

commit v1 on v0

v1 whole, which is shorter than its diff:
```python
import functools
import math

import jax
import jax.numpy as jnp
from jax import lax
from jax.experimental import pallas as pl
from jax.experimental.pallas import tpu as pltpu
from jax.sharding import PartitionSpec as P

HEADS = 12
EPSILON = 1e-12
HIDE = -1e30
GROUPS = 16
BF = jnp.bfloat16
F32 = jnp.float32
VMEM_BYTES = 56 * 2**20


def sds(shape, dtype):
    return jax.ShapeDtypeStruct(shape, dtype)


def nn(left, right):
    return jnp.dot(left, right, preferred_element_type=F32)


def nt(left, right):
    return lax.dot_general(left, right, (((1,), (1,)), ((), ())), preferred_element_type=F32)


def tn(left, right):
    return lax.dot_general(left, right, (((0,), (0,)), ((), ())), preferred_element_type=F32)


def call(kernel, outs, *args, scratch=(), hbm=(), smem=(), flops=0, name=None):
    specs = []
    total = 0
    for i, arg in enumerate(args):
        total += arg.size * arg.dtype.itemsize
        if i in hbm:
            specs.append(pl.BlockSpec(memory_space=pl.ANY))
        elif i in smem:
            specs.append(pl.BlockSpec(memory_space=pltpu.SMEM))
        else:
            specs.append(pl.BlockSpec(memory_space=pltpu.VMEM))
    total += sum(math.prod(o.shape) * o.dtype.itemsize for o in outs)
    return pl.pallas_call(
        kernel,
        out_shape=list(outs),
        in_specs=specs,
        out_specs=[pl.BlockSpec(memory_space=pltpu.VMEM) for _ in outs],
        scratch_shapes=list(scratch),
        compiler_params=pltpu.CompilerParams(vmem_limit_bytes=VMEM_BYTES),
        cost_estimate=pl.CostEstimate(flops=flops, bytes_accessed=total, transcendentals=0),
        name=name,
    )(*args)


def segment_of(positions, lens_ref):
    ids = jnp.zeros_like(positions)
    end = jnp.int32(0)
    for j in range(lens_ref.shape[1]):
        end = end + lens_ref[0, j]
        ids = ids + (positions >= end).astype(jnp.int32)
    return ids


def own_first(index, half, s):
    return jnp.where(index < half, index + s * half, index - half + (1 - s) * half)


def normalise(total):
    centered = total - jnp.mean(total, axis=-1, keepdims=True)
    inverse = lax.rsqrt(jnp.mean(centered * centered, axis=-1, keepdims=True) + EPSILON)
    return centered * inverse, inverse


def norm_pull(grad, normal, inverse, gain):
    scaled = grad * gain
    return inverse * (
        scaled
        - jnp.mean(scaled, axis=-1, keepdims=True)
        - normal * jnp.mean(scaled * normal, axis=-1, keepdims=True)
    )


def column_sum(matrix):
    return jnp.sum(matrix, axis=0, keepdims=True)


def attend_kernel(
    lens, own, other, w_hbm, b_qv, q_out, k_out, v_out, kt_out, probs_out, att_out, w_buf, sems
):
    half, width = own.shape
    length = 2 * half
    mine = width // 2
    pair = 2 * (width // HEADS)
    head = pair // 2
    s = lax.axis_index("seq")
    copies = []
    for c in range(3):
        start = pl.multiple_of(c * width + s * mine, 128)
        copies.append(pltpu.make_async_copy(w_hbm.at[:, pl.ds(start, mine)], w_buf.at[c], sems.at[c]))
        copies[-1].start()
    column = pl.ds(pl.multiple_of(s * mine, 128), mine)
    bias = (b_qv[0:1, column].astype(F32), None, b_qv[1:2, column].astype(F32))
    parts = []
    for c in range(3):
        copies[c].wait()
        whole = []
        for tokens in (own, other):
            lin = nn(tokens[...], w_buf[c])
            if bias[c] is not None:
                lin = lin + bias[c]
            whole.append(lin)
        parts.append(jnp.concatenate(whole, axis=0))
    q_all, k_all, v_all = parts
    q_all = q_all.astype(BF).astype(F32) * (1.0 / math.sqrt(head))
    q_out[...] = q_all.astype(BF)
    k_out[...] = k_all.astype(BF)
    v_out[...] = v_all.astype(BF)
    kt_out[...] = k_all.T.astype(BF)
    vt = v_all.T.astype(BF)
    rows = own_first(lax.broadcasted_iota(jnp.int32, (length, pair), 0), half, s)
    lane = lax.broadcasted_iota(jnp.int32, (length, pair), 1)
    same = segment_of(rows, lens) == lane % head
    in_range = lane % head < lens.shape[1]
    mark_k = jnp.where(same, 1.0, 0.0)
    mark_q = jnp.where(jnp.logical_and(in_range, jnp.logical_not(same)), HIDE, 0.0)
    first = lane < head
    for j in range(mine // pair):
        cols = slice(j * pair, (j + 1) * pair)
        q2, k2 = q_all[:, cols], k_all[:, cols]
        pieces = []
        for a in range(2):
            keep = first if a == 0 else jnp.logical_not(first)
            k_m = jnp.where(keep, k2, mark_k).astype(BF)
            q_m = jnp.where(keep, q2, mark_q).astype(BF)
            scores = nt(k_m, q_m)
            top = jnp.max(scores, axis=0, keepdims=True)
            expo = jnp.exp(scores - top)
            total = jnp.sum(expo, axis=0, keepdims=True)
            probs = (expo * (1.0 / total)).astype(BF)
            h = 2 * j + a
            probs_out[h] = probs
            pieces.append(nn(vt[h * head : (h + 1) * head, :], probs))
        att_out[:, cols] = jnp.concatenate(pieces, axis=0).T.astype(BF)


def forward_kernel(
    lens,
    own,
    att_mine,
    att_got,
    w_o,
    b_o,
    gain1,
    shift1,
    w_in,
    b_in,
    w_out,
    b_out,
    gain2,
    shift2,
    cot,
    mid_out,
    active_out,
    pull_out,
    normal_out,
    inverse_out,
    sum2_out,
    down_keep,
    down_send,
    out_out,
    pool_out,
    vec_out,
    down_acc,
):
    half, width = own.shape
    mine = width // 2
    ff = w_in.shape[1]
    s = lax.axis_index("seq")
    row_a = pl.ds(pl.multiple_of(s * mine, 128), mine)
    row_b = pl.ds(pl.multiple_of((1 - s) * mine, 128), mine)
    branch = nn(att_mine[0:half, :], w_o[row_a, :]) + nn(att_got[half:, :], w_o[row_b, :])
    normal, inverse = normalise(own[...].astype(F32) + (branch + b_o[...].astype(F32)))
    middle = normal * gain1[...].astype(F32) + shift1[...].astype(F32)
    low = middle.astype(BF)
    mid_out[...] = low
    normal_out[...] = normal
    inverse_out[...] = inverse
    down_acc[...] = middle + b_out[...].astype(F32)
    step = 512
    for c in range(0, ff, step):
        cols = slice(c, c + step)
        upper = nn(low, w_in[:, cols]) + b_in[:, cols].astype(F32)
        cdf = 0.5 + 0.5 * lax.erf(upper * (1.0 / math.sqrt(2.0)))
        density = jnp.exp(-0.5 * upper * upper) * (1.0 / math.sqrt(2.0 * math.pi))
        act = (upper * cdf).astype(BF)
        active_out[:, cols] = act
        pull_out[:, cols] = cdf + upper * density
        down_acc[...] += nn(act, w_out[cols, :])
    normal2, inverse2 = normalise(down_acc[...])
    gain = gain2[...].astype(F32)
    final = normal2 * gain + shift2[...].astype(F32)
    out_out[...] = final.astype(BF)
    rows = lax.broadcasted_iota(jnp.int32, (half, width), 0) + s * half
    ids = segment_of(rows, lens)
    pool_out[...] = jnp.zeros_like(pool_out)
    for t in range(lens.shape[1]):
        pool_out[t : t + 1, :] = column_sum(jnp.where(ids == t, final, 0.0))
    grad = cot[...].astype(F32)
    sum2 = norm_pull(grad, normal2, inverse2, gain)
    sum2_out[...] = sum2
    down = sum2.astype(BF)
    down_acc[...] = sum2
    down_keep[...] = down_acc[:, row_a].astype(BF)
    down_send[...] = down_acc[:, row_b].astype(BF)
    vec_out[...] = jnp.zeros_like(vec_out)
    vec_out[0:1, :] = column_sum(grad * normal2)
    vec_out[1:2, :] = column_sum(grad)
    vec_out[2:3, :] = column_sum(down.astype(F32))


def backward_kernel(
    sum2, pull, normal, inverse, gain1, w_in, w_out,
    up_keep, up_send, sum1_out, branch_out, vec_out, mid_acc,
):
    width, ff = w_in.shape
    s = lax.axis_index("seq")
    step = 512
    per = ff // 2 // step
    mid_acc[...] = sum2[...]
    low = sum2[...].astype(BF)
    vec_out[...] = jnp.zeros_like(vec_out)
    sums = []
    for i in range(2 * per):
        block = (i // per + s) % 2
        start = pl.multiple_of(block * (ff // 2) + (i % per) * step, 128)
        cols = pl.ds(start, step)
        grad_upper = (nt(low, w_out[cols, :]) * pull[:, cols]).astype(BF)
        place = up_keep if i < per else up_send
        place[:, (i % per) * step : (i % per + 1) * step] = grad_upper
        sums.append(column_sum(grad_upper.astype(F32)))
        mid_acc[...] += nt(grad_upper, w_in[:, cols])
    ups = [jnp.concatenate(sums[:per], axis=1), jnp.concatenate(sums[per:], axis=1)]
    for b in range(2):
        line = jnp.where(s == b, ups[0], ups[1])
        for r in range(ff // 2 // width):
            row = b * (ff // 2 // width) + r
            vec_out[row : row + 1, :] = line[:, r * width : (r + 1) * width]
    base = ff // width
    grad_mid = mid_acc[...]
    vec_out[base : base + 1, :] = column_sum(grad_mid * normal[...])
    vec_out[base + 1 : base + 2, :] = column_sum(grad_mid)
    sum1 = norm_pull(grad_mid, normal[...], inverse[...], gain1[...].astype(F32))
    sum1_out[...] = sum1
    branch = sum1.astype(BF)
    branch_out[...] = branch
    vec_out[base + 2 : base + 3, :] = column_sum(branch.astype(F32))


def attend_back_kernel(
    branch_own, branch_got, w_o, q, k, v, kt, probs, grad_out, vec_out
):
    length, mine = q.shape
    width = w_o.shape[1]
    head = width // HEADS
    pair = 2 * head
    s = lax.axis_index("seq")
    w_mine = w_o[pl.ds(pl.multiple_of(s * mine, 128), mine), :]
    att_t = jnp.concatenate(
        [nt(w_mine, branch_own[...]).astype(BF), nt(w_mine, branch_got[...]).astype(BF)], axis=1
    )
    lane = lax.broadcasted_iota(jnp.int32, (length, pair), 1)
    first = lane < head
    vec_out[...] = jnp.zeros_like(vec_out)
    for j in range(mine // pair):
        cols = slice(j * pair, (j + 1) * pair)
        q2 = q[:, cols]
        v2 = v[:, cols].astype(F32)
        a2 = att_t[cols, :]
        dq, dk, dv = [], [], []
        for a in range(2):
            h = 2 * j + a
            keep = first if a == 0 else jnp.logical_not(first)
            v_m = jnp.where(keep, v2, 0.0).astype(BF)
            grad_p = nn(v_m, a2)
            low = probs[h]
            prob = low.astype(F32)
            inner = jnp.sum(prob * grad_p, axis=0, keepdims=True)
            raw = (prob * (grad_p - inner)).astype(BF)
            dk.append(nn(raw, q2))
            dv.append(nt(low, a2))
            dq.append(nn(kt[h * head : (h + 1) * head, :], raw))
        dq_low = (jnp.concatenate(dq, axis=0) * (1.0 / math.sqrt(head))).T.astype(BF)
        dk_low = jnp.where(first, dk[0], dk[1]).astype(BF)
        dv_low = jnp.where(first, dv[0], dv[1]).astype(BF)
        grad_out[:, cols] = dq_low
        grad_out[:, mine + j * pair : mine + (j + 1) * pair] = dk_low
        grad_out[:, 2 * mine + j * pair : 2 * mine + (j + 1) * pair] = dv_low
        vec_out[0:1, cols] = column_sum(dq_low.astype(F32))
        vec_out[1:2, cols] = column_sum(dv_low.astype(F32))


def slot_of(chunk, order):
    if order is None:
        return jnp.int32(chunk)
    rel = jnp.bitwise_xor(jnp.int32(chunk), lax.axis_index("dp"))
    s = lax.axis_index("seq")
    slots = []
    for bits in order:
        slot = jnp.int32(0)
        for bit in bits:
            slot = slot * 2 + jnp.bitwise_and(lax.shift_right_logical(rel, jnp.int32(bit)), 1)
        slots.append(slot)
    return jnp.where(s == 0, slots[0], slots[1])


def place(values, chunk, order, keep, send, cols=None):
    half = GROUPS // 2
    slot = slot_of(chunk, order)
    rows = values.shape[0]
    if cols is None:
        cols = slice(0, values.shape[1])

    def at(index):
        return pl.ds(pl.multiple_of(index * rows, 16), rows)

    @pl.when(slot < half)
    def _():
        keep[at(slot), cols] = values

    @pl.when(slot >= half)
    def _():
        send[at(slot - half), cols] = values


def grad_out_kernel(order, active_own, active_got, down_own, down_got, keep, send):
    ff = active_own.shape[1]
    rows = ff // GROUPS
    block = 2 * rows
    for i in range(GROUPS // 2):
        cols = slice(i * block, (i + 1) * block)
        got = (
            tn(active_own[:, cols], down_own[...]) + tn(active_got[:, cols], down_got[...])
        ).astype(BF)
        for b in range(2):
            place(got[b * rows : (b + 1) * rows, :], 2 * i + b, order, keep, send)


def grad_in_kernel(order, mid_own, mid_got, up_own, up_got, keep, send):
    width = mid_own.shape[1]
    rows = width // GROUPS
    for i in range(2):
        cols = slice(i * width // 2, (i + 1) * width // 2)
        for n in range(0, up_own.shape[1], 512):
            out = slice(n, n + 512)
            got = (
                tn(mid_own[:, cols], up_own[:, out]) + tn(mid_got[:, cols], up_got[:, out])
            ).astype(BF)
            for b in range(GROUPS // 2):
                place(
                    got[b * rows : (b + 1) * rows, :], i * (GROUPS // 2) + b, order, keep, send, out
                )


def grad_qkv_kernel(
    order, own, other, grads, att_mine, att_got, branch_own, branch_got, vec_f, vec_b, vec_a,
    keep, send, vec_keep,
):
    half, width = own.shape
    mine = width // 2
    rows = width // GROUPS
    s = lax.axis_index("seq")
    column = pl.ds(pl.multiple_of(s * mine, 128), mine)
    for i in range(2):
        cols = slice(i * mine, (i + 1) * mine)
        for c in range(3):
            out = slice(c * mine, (c + 1) * mine)
            got = (tn(own[:, cols], grads[0:half, out]) + tn(other[:, cols], grads[half:, out])).astype(BF)
            for b in range(GROUPS // 2):
                place(got[b * rows : (b + 1) * rows, :], i * (GROUPS // 2) + b, order, keep, send, out)
    out = slice(3 * mine, 4 * mine)
    mine_o = tn(att_mine[0:half, :], branch_own[:, column]) + tn(att_mine[half:, :], branch_got[:, column])
    got_o = tn(att_got[half:, :], branch_own[:, column]) + tn(att_got[0:half, :], branch_got[:, column])
    for i in range(2):
        got = jnp.where(s == i, mine_o, got_o).astype(BF)
        for b in range(GROUPS // 2):
            place(got[b * rows : (b + 1) * rows, :], i * (GROUPS // 2) + b, order, keep, send, out)
    base = vec_b.shape[0]
    zero = jnp.zeros((1, mine), F32)
    lines = []
    for r in range(2):
        line = vec_a[r : r + 1, :]
        lines.append(
            jnp.concatenate([jnp.where(s == 0, line, zero), jnp.where(s == 0, zero, line)], axis=1)
        )
    table = jnp.concatenate(lines + [vec_b[0:7, :], vec_f[0:3, :], jnp.zeros((4, width), F32)], axis=0)
    high = table.astype(BF)
    rest = (table - high.astype(F32)).astype(BF)
    extra = slice(GROUPS // 2 * rows, GROUPS // 2 * rows + 16)
    send[extra, 0:width] = high
    send[extra, width:] = rest
    vec_keep[...] = high.astype(F32) + rest.astype(F32)


def merge_kernel(rows, got, keep, keep_out, send_out):
    total = keep[0:rows, :].astype(F32) + got[0:rows, :].astype(F32)
    keep_out[...] = total[0 : rows // 2, :].astype(BF)
    send_out[...] = total[rows // 2 :, :].astype(BF)


def merge_vec_kernel(rows, got, keep, vec, keep_out, send_out, vec_out):
    width = vec.shape[1]
    merge_kernel(rows, got, keep, keep_out, send_out.at[0 : rows // 2, :])
    table = vec[...] + (got[rows:, 0:width].astype(F32) + got[rows:, width:].astype(F32))
    high = table.astype(BF)
    rest = (table - high.astype(F32)).astype(BF)
    extra = slice(rows // 2, rows // 2 + 16)
    send_out[extra, 0:width] = high
    send_out[extra, width:] = rest
    vec_out[...] = high.astype(F32) + rest.astype(F32)


def last_kernel(got, keep, keep_out, send_out, acc):
    rows = keep.shape[0]
    s = lax.axis_index("seq")
    acc[...] = keep[...].astype(F32) + got[0:rows, :].astype(F32)
    keep_out[...] = acc[pl.ds(pl.multiple_of(s * (rows // 2), 8), rows // 2), :]
    send_out[...] = acc[pl.ds(pl.multiple_of((1 - s) * (rows // 2), 8), rows // 2), :]


def last_vec_kernel(got, keep, vec, keep_out, send_out, acc):
    rows = keep.shape[0]
    width = vec.shape[1]
    last_kernel(got, keep, keep_out, send_out.at[0 : rows // 2, :], acc)
    table = vec[...] + (got[rows:, 0:width].astype(F32) + got[rows:, width:].astype(F32))
    send_out[rows // 2 :, 0:width] = table
    send_out[rows // 2 :, width:] = jnp.zeros_like(table)


def swap(x, axis="seq"):
    return lax.ppermute(x, axis, [(0, 1), (1, 0)])


def send_to(x, phase, order, count):
    pairs = []
    for d in range(count):
        for s in range(2):
            pairs.append((2 * d + s, 2 * (d ^ (1 << order[s][phase])) + s))
    return lax.ppermute(x, ("dp", "seq"), pairs)


def reduce_rows(keep, send, order, count, name, vec=None):
    phases = len(order[0])
    rows = keep.shape[0]
    cols = keep.shape[1]
    for p in range(phases - 1):
        got = send_to(send, p, order, count)
        if vec is None:
            keep, send = call(
                functools.partial(merge_kernel, rows),
                [sds((rows // 2, cols), BF), sds((rows // 2, cols), BF)],
                got, keep, name=f"{name}_merge{p}",
            )
        else:
            keep, send, vec = call(
                functools.partial(merge_vec_kernel, rows),
                [sds((rows // 2, cols), BF), sds((rows // 2 + 16, cols), BF), sds(vec.shape, F32)],
                got, keep, vec, name=f"{name}_merge{p}",
            )
        rows //= 2
    got = send_to(send, phases - 1, order, count)
    scratch = [pltpu.VMEM((rows, cols), F32)]
    if vec is None:
        return call(
            last_kernel,
            [sds((rows // 2, cols), F32), sds((rows // 2, cols), F32)],
            got, keep, scratch=scratch, name=f"{name}_last",
        )
    return call(
        last_vec_kernel,
        [sds((rows // 2, cols), F32), sds((rows // 2 + 16, cols), F32)],
        got, keep, vec, scratch=scratch, name=f"{name}_last",
    )


def interleave(keep, got, s, pieces):
    size = keep.shape[1] // pieces
    outs = []
    for i in range(pieces):
        a, b = keep[:, i * size : (i + 1) * size], got[:, i * size : (i + 1) * size]
        outs += [jnp.where(s == 0, a, b), jnp.where(s == 0, b, a)]
    return outs


def on_device(
    orders, count,
    hidden_in, w_qkv, b_qv, w_o, b_o, ln1_gain, ln1_bias, w_in, b_in, w_out, b_out, ln2_gain, ln2_bias,
    seg_lengths, cotangent,
):
    row_count, half, width = hidden_in.shape
    length = 2 * half
    mine = width // 2
    heads = HEADS // 2
    ff = w_in.shape[1]
    s = lax.axis_index("seq")
    order_out, order_in, order_qkv = orders if orders else (None, None, None)
    own = hidden_in.reshape(half, width)
    cot = cotangent.reshape(half, width)
    line = lambda x: x.reshape(1, -1)
    other = swap(own)
    q, k, v, kt, probs, att_mine = call(
        attend_kernel,
        [sds((length, mine), BF)] * 3
        + [sds((mine, length), BF), sds((heads, length, length), BF), sds((length, mine), BF)],
        seg_lengths, own, other, w_qkv, b_qv,
        smem=(0,), hbm=(3,),
        scratch=[pltpu.VMEM((3, width, mine), BF), pltpu.SemaphoreType.DMA((3,))],
        flops=2 * length * width * 3 * mine + 4 * heads * length * length * 256,
        name="attend",
    )
    att_got = swap(att_mine)
    (mid_low, active, pull, normal, inverse, sum2, down_own, down_send, output, pool_part, vec_f) = call(
        forward_kernel,
        [
            sds((half, width), BF), sds((half, ff), BF), sds((half, ff), F32), sds((half, width), F32),
            sds((half, 1), F32), sds((half, width), F32), sds((half, mine), BF), sds((half, mine), BF),
            sds((half, width), BF), sds((8, width), F32), sds((8, width), F32),
        ],
        seg_lengths, own, att_mine, att_got, w_o, line(b_o), line(ln1_gain), line(ln1_bias), w_in, line(b_in),
        w_out, line(b_out), line(ln2_gain), line(ln2_bias), cot,
        smem=(0,), scratch=[pltpu.VMEM((half, width), F32)],
        flops=2 * half * (width * width + 2 * width * ff), name="forward",
    )
    active_got = swap(active)
    mid_got = swap(mid_low)
    down_got = swap(down_send)
    up_own, up_send, sum1, branch_own, vec_b = call(
        backward_kernel,
        [
            sds((half, ff // 2), BF), sds((half, ff // 2), BF), sds((half, width), F32),
            sds((half, width), BF), sds((8, width), F32),
        ],
        sum2, pull, normal, inverse, line(ln1_gain), w_in, w_out,
        scratch=[pltpu.VMEM((half, width), F32)],
        flops=4 * half * width * ff, name="backward",
    )
    branch_got = swap(branch_own)
    up_got = swap(up_send)
    rows_ff, rows_w = ff // GROUPS, width // GROUPS
    keep_out, send_out = call(
        functools.partial(grad_out_kernel, order_out),
        [sds((GROUPS // 2 * rows_ff, mine), BF)] * 2,
        active, active_got, down_own, down_got,
        flops=2 * length * ff * mine, name="grad_out",
    )
    keep_in, send_in = call(
        functools.partial(grad_in_kernel, order_in),
        [sds((GROUPS // 2 * rows_w, ff // 2), BF)] * 2,
        mid_low, mid_got, up_own, up_got,
        flops=2 * length * width * ff // 2, name="grad_in",
    )
    grads, vec_a = call(
        attend_back_kernel,
        [sds((length, 3 * mine), BF), sds((8, mine), F32)],
        branch_own, branch_got, w_o, q, k, v, kt, probs,
        flops=2 * length * width * mine + 10 * heads * length * length * 256, name="attend_back",
    )
    keep_qkv, send_qkv, vec = call(
        functools.partial(grad_qkv_kernel, order_qkv),
        [sds((GROUPS // 2 * rows_w, 4 * mine), BF), sds((GROUPS // 2 * rows_w + 16, 4 * mine), BF), sds((16, width), F32)],
        own, other, grads, att_mine, att_got, branch_own, branch_got, vec_f, vec_b, vec_a,
        flops=2 * length * width * 4 * mine, name="grad_qkv",
    )

    def grad_input_kernel(grads, w_hbm, sum1, pool, keep_ref, send_ref, w_buf, sems):
        core = lax.axis_index("seq")
        copies = []
        for c in range(3):
            start = pl.multiple_of(c * width + core * mine, 128)
            copies.append(
                pltpu.make_async_copy(w_hbm.at[:, pl.ds(start, mine)], w_buf.at[c], sems.at[c])
            )
            copies[-1].start()
        a, b = sum1[...], jnp.zeros((half, width), F32)
        for c in range(3):
            copies[c].wait()
            cols = slice(c * mine, (c + 1) * mine)
            a = a + nt(grads[0:half, cols], w_buf[c])
            b = b + nt(grads[half:, cols], w_buf[c])
        keep_ref[...] = a
        send_ref[0:half, :] = b
        send_ref[half:, :] = pool[...]

    input_keep, input_send = call(
        grad_input_kernel,
        [sds((half, width), F32), sds((half + 8, width), F32)],
        grads, w_qkv, sum1, pool_part,
        hbm=(1,), scratch=[pltpu.VMEM((3, width, mine), BF), pltpu.SemaphoreType.DMA((3,))],
        flops=2 * length * width * 3 * mine, name="grad_input",
    )
    input_got = swap(input_send)
    d_input = input_keep + input_got[:half]
    pool_sum = (pool_part + input_got[half:])[: seg_lengths.shape[1]]
    pooled = pool_sum / seg_lengths.reshape(-1, 1).astype(F32)

    if orders:
        out_keep, out_send = reduce_rows(keep_out, send_out, order_out, count, "out")
        in_keep, in_send = reduce_rows(keep_in, send_in, order_in, count, "in")
        qkv_keep, qkv_send = reduce_rows(keep_qkv, send_qkv, order_qkv, count, "qkv", vec)
        out_got, in_got, qkv_got = swap(out_send), swap(in_send), swap(qkv_send)
        rows = qkv_keep.shape[0]
        vec = qkv_send[rows:, :width] + qkv_got[rows:, :width]
        qkv_got = qkv_got[:rows]
    else:
        done = []
        for keep, send in ((keep_out, send_out), (keep_in, send_in), (keep_qkv, send_qkv)):
            both = jnp.concatenate([keep, send[: keep.shape[0]]], axis=0)
            total = lax.psum_scatter(both, "dp", scatter_dimension=0, tiled=True).astype(F32)
            parts = total.reshape(2, -1, total.shape[1])
            done.append((jnp.where(s == 0, parts[0], parts[1]), swap(jnp.where(s == 0, parts[1], parts[0]))))
        (out_keep, out_got), (in_keep, in_got), (qkv_keep, qkv_got) = done
        vec = lax.psum(vec, ("dp", "seq"))
    flat_out = jnp.concatenate(interleave(out_keep, out_got, s, 1), axis=1).reshape(-1)
    flat_in = jnp.concatenate(interleave(in_keep, in_got, s, 1), axis=1).reshape(-1)
    pieces = interleave(qkv_keep, qkv_got, s, 4)
    flat_qkv = jnp.concatenate(pieces[:6], axis=1).reshape(-1)
    flat_o = jnp.concatenate(pieces[6:], axis=1).reshape(-1)
    base = ff // width
    return (
        output.reshape(row_count, half, width),
        pooled[None],
        d_input.reshape(row_count, half, width),
        flat_qkv,
        flat_o,
        flat_in,
        flat_out,
        vec[0:2],
        vec[2 + base + 2],
        vec[2 + base],
        vec[2 + base + 1],
        vec[2 : 2 + base].reshape(-1),
        vec[2 + base + 5],
        vec[2 + base + 3],
        vec[2 + base + 4],
    )


def solution(mesh):
    count = mesh.shape["dp"]
    orders = None
    if count == GROUPS:
        orders = (
            ((0, 2, 3, 1), (1, 2, 3, 0)),
            ((0, 1, 2, 3), (1, 0, 2, 3)),
            ((0, 1, 2, 3), (1, 0, 2, 3)),
        )
    in_specs = (P("dp", "seq", None),) + (P(),) * 12 + (P("dp", None), P("dp", "seq", None))
    out_specs = (
        P("dp", "seq", None),
        P("dp", None, None),
        P("dp", "seq", None),
    ) + (P(("dp", "seq")),) * 4 + (P(),) * 8
    return jax.shard_map(
        functools.partial(on_device, orders, count),
        mesh=mesh, in_specs=in_specs, out_specs=out_specs, check_vma=False,
    )
```

time: 640 us -> 205 us (0.32)
  waiting for transfers between devices: 375 us -> 63.1 us
  matrix products: 105 us -> 0 us
  Pallas kernels: 0 us -> 92.6 us
  blocking collectives: 58.4 us -> 0 us
  local copies, waits for them, and re-layouts: 56.6 us -> 23.2 us
  starting transfers between devices: 0.12 us -> 22.1 us
  other arithmetic: 24.5 us -> 2.67 us
  between operations: 14.6 us -> 0.95 us
    unnamed x4 -> x0, waiting for transfers between devices: 375 us -> none
    dot_general x19 -> x0, matrix products: 105 us -> none  [the longest x1 24.2 us: on_device(): jnp.einsum('rhpq,rphe->rqhe', grad_raw, query_heads, preferred_element_ty...]
    pallas_call x0 -> x20, Pallas kernels: none -> 92.6 us  [call(): pl.pallas_call(kernel, out_shape=list(outs), in_specs=specs, out_specs=[p...]
    ppermute x0 -> x23, waiting for transfers between devices: none -> 63.1 us  [the longest x12 59.5 us: send_to(): return lax.ppermute(x, ('dp', 'seq'), pairs)]
    psum x2 -> x0, blocking collectives: 50 us -> none  [the longest x1 45.8 us: on_device(): lax.psum((d_b_qv, d_b_o, d_ln1_gain, d_ln1_bias, d_b_in, d_b_out, d_ln2_g...]
    ppermute x0 -> x23, starting transfers between devices: none -> 22.1 us  [the longest x12 20.3 us: send_to(): return lax.ppermute(x, ('dp', 'seq'), pairs)]
    reshape x3 -> x11, local copies, waits for them, and re-layouts: 22.2 us -> 6.78 us  [the longest x7 4.1 us: on_device(): line = lambda x: x.reshape(1, -1)]
    reduce_sum x10 -> x0, other arithmetic: 10.6 us -> none  [the longest x3 5.11 us: column_sums(): return jnp.sum(matrix.astype(jnp.float32), axis=0)]
  transfers between devices with their start and end apart: 3 -> 23, of which waited for: 1 -> 11; matrix products, arithmetic and copies ran while one was open for 16% -> 5% of each run, Pallas kernels for 0% -> 30%
where the time goes in v1:
time: 205 us
  Pallas kernels  92.6 us (45%)
  waiting for transfers between devices  63.1 us (31%)
  local copies, waits for them, and re-layouts  23.2 us (11%)
  starting transfers between devices  22.1 us (11%)
  other arithmetic  2.67 us (1%)
    pallas_call x20, Pallas kernels, call(): pl.pallas_call(kernel, out_shape=list(outs), in_specs=specs, out_specs=[p...  92.6 us
    ppermute x12, waiting for transfers between devices, send_to(): return lax.ppermute(x, ('dp', 'seq'), pairs)  59.5 us
    ppermute x12, starting transfers between devices, send_to(): return lax.ppermute(x, ('dp', 'seq'), pairs)  20.3 us
    unnamed x71, local copies, waits for them, and re-layouts  15.2 us
  transfers between devices with their start and end apart: 23, of which 11 were waited for; matrix products, arithmetic and copies ran while one was open for 5% of the time, Pallas kernels for 30%

profile of v1, /device:TPU:0, one launch (start us, length us, event | category | flops | bytes accessed | tf_op | source)
XLA Modules:
  0.0 204.7 jit_solution(4516864051908481621)
XLA Ops:
  3.5 9.6 %attend.1 = (bf16[512,384]{1,0:T(8,128)(2,1)}, bf16[512,384]{1,0:T(8,128)(2,1)}, bf16[512,384]{1,0:T(8,128)(2,1)}, bf16[384,512]{1,0:T(8,128)(2,1)}, bf16[6,512,...) custom-call(s32[1,4]{1,0:T(1,128)} %lens.3, bf16[256,768]{1,0:T(8,128)(2,1)} %bitcast.14, bf16[256,768]{1,0:T(8,128)(2,1)} %copy-done.29, ...), custom_call_target="tpu_custom_call" | custom-call | flops 2516582400 | bytes 9440272 | tf_op jit(solution)/shard_map/attend/pallas_call | solution.py:48
  18.5 12.4 %forward.1 = (bf16[256,768]{1,0:T(8,128)(2,1)}, bf16[256,3072]{1,0:T(8,128)(2,1)}, f32[256,3072]{1,0:T(8,128)}, f32[256,768]{1,0:T(8,128)}, f32[256,1]{1,0:T(8,1...) custom-call(s32[1,4]{1,0:T(1,128)} %lens.3, ...), custom_call_target="tpu_custom_call" | custom-call | flops 2717908992 | bytes 19726352 | tf_op jit(solution)/shard_map/forward/pallas_call | solution.py:48
  30.8 10.0 %backward.1 = (bf16[256,1536]{1,0:T(8,128)(2,1)}, bf16[256,1536]{1,0:T(8,128)(2,1)}, f32[256,768]{1,0:T(8,128)}, bf16[256,768]{1,0:T(8,128)(2,1)}, f32[8,768]{1,0:T(8,128)}) custom-call(f32[256,768]{1,0:T(8,128)} %get-tuple-element.78.sum2, f32[256,3072]{1,0:T(8,128)} %get-tuple-element.79.pull, f32[256,768]{1,0:T(8,128)} %get-tuple-element.80.normal, ...), custom_call_target="tpu_custom_call" | custom-call | flops 2415919104 | bytes 16935424 | tf_op jit(solution)/shard_map/backward/pallas_call | solution.py:48
  43.5 9.0 %attend_back.1 = (bf16[512,1152]{1,0:T(8,128)(2,1)}, f32[8,384]{1,0:T(8,128)}) custom-call(bf16[256,768]{1,0:T(8,128)(2,1)} %get-tuple-element.82.branch_own, bf16[256,768]{1,0:T(8,128)(2,1)} %copy-done.32, bf16[768,768]{1,0:T(8,128)(2,1)} %w_o.3, bf16[512,384]{1,0:T(8,128)(2,1)} %get-tuple-element.83.q, bf16[512,384]{1,0:T(8,128)(2,1)} %get-tuple-element.84.k, ...), custom_call_target="tpu_custom_call" | custom-call | flops 4328521728 | bytes 7876608 | tf_op jit(solution)/shard_map/attend_back/pallas_call | solution.py:48
  52.5 7.4 %grad_qkv.1 = (bf16[384,1536]{1,0:T(8,128)(2,1)}, bf16[400,1536]{1,0:T(8,128)(2,1)}, f32[16,768]{1,0:T(8,128)}) custom-call(bf16[256,768]{1,0:T(8,128)(2,1)} %bitcast.16, bf16[256,768]{1,0:T(8,128)(2,1)} %copy-done.29, bf16[512,1152]{1,0:T(8,128)(2,1)} %get-tuple-element.88.grads, bf16[512,384]{1,0:T(8,128)(2,1)} %get-tuple-element.75.att_mine, ...), custom_call_target="tpu_custom_call" | custom-call | flops 1207959552 | bytes 6057984 | tf_op jit(solution)/shard_map/grad_qkv/pallas_call | solution.py:48
  59.8 2.6 %collective-permute-start.4 = (bf16[400,1536]{1,0:T(8,128)(2,1)}, bf16[400,1536]{1,0:T(8,128)(2,1)S(1)}, u32[]{:S(2)}, u32[]{:S(2)}) collective-permute-start(bf16[400,1536]{1,0:T(8,128)(2,1)} %get-tuple-element.95), channel_id=1, source_target_pairs={{0,2},{1,5},{2,0},{3,7},{4,6},{5,1},{6,4},{7,3},{8,10},{9,13},{10,... | collective-permute-start | bytes 3686408 | tf_op jit(solution)/shard_map/ppermute | solution.py:453
  63.6 6.3 %grad_in.1 = (bf16[384,1536]{1,0:T(8,128)(2,1)}, bf16[384,1536]{1,0:T(8,128)(2,1)}) custom-call(bf16[256,768]{1,0:T(8,128)(2,1)} %get-tuple-element.109.mid_own, bf16[256,768]{1,0:T(8,128)(2,1)} %copy-done.31, bf16[256,1536]{1,0:T(8,128)(2,1)} %get-tuple-element.110.up_own, bf16[256,1536]{1,0:T(8,128)(2,1)} %copy-done.28), custom_call_target="tpu_custom_call" | custom-call | flops 1207959552 | bytes 4718592 | tf_op jit(solution)/shard_map/grad_in/pallas_call | solution.py:48
  71.4 6.0 %collective-permute-done.4.got = bf16[400,1536]{1,0:T(8,128)(2,1)S(1)} collective-permute-done((bf16[400,1536]{1,0:T(8,128)(2,1)}, bf16[400,1536]{1,0:T(8,128)(2,1)S(1)}, u32[]{:S(2)}, u32[]{:S(2)}) %collective-permute-start.4) | collective-permute-done | bytes 1228832 | tf_op jit(solution)/shard_map/ppermute | solution.py:453
  78.5 2.9 %qkv_merge0.1 = (bf16[192,1536]{1,0:T(8,128)(2,1)}, bf16[208,1536]{1,0:T(8,128)(2,1)}, f32[16,768]{1,0:T(8,128)}) custom-call(bf16[400,1536]{1,0:T(8,128)(2,1)} %copy-done, bf16[384,1536]{1,0:T(8,128)(2,1)} %get-tuple-element.96.keep, f32[16,768]{1,0:T(8,128)} %get-tuple-element.97.vec), custom_call_target="tpu_custom_call" | custom-call | bytes 3735552 | tf_op jit(solution)/shard_map/qkv_merge0/pallas_call | solution.py:48
  83.4 12.5 %collective-permute-done.11.got = bf16[384,1536]{1,0:T(8,128)(2,1)S(1)} collective-permute-done((bf16[384,1536]{1,0:T(8,128)(2,1)}, bf16[384,1536]{1,0:T(8,128)(2,1)S(1)}, u32[]{:S(2)}, u32[]{:S(2)}) %collective-permute-start.11) | collective-permute-done | bytes 1179680 | tf_op jit(solution)/shard_map/ppermute | solution.py:453
  97.0 2.8 %in_merge0.1 = (bf16[192,1536]{1,0:T(8,128)(2,1)}, bf16[192,1536]{1,0:T(8,128)(2,1)}) custom-call(bf16[384,1536]{1,0:T(8,128)(2,1)} %copy-done.2, bf16[384,1536]{1,0:T(8,128)(2,1)} %get-tuple-element.113.keep), custom_call_target="tpu_custom_call" | custom-call | bytes 3538944 | tf_op jit(solution)/shard_map/in_merge0/pallas_call | solution.py:48
  99.9 2.4 %collective-permute-start.12 = (bf16[192,1536]{1,0:T(8,128)(2,1)}, bf16[192,1536]{1,0:T(8,128)(2,1)S(1)}, u32[]{:S(2)}, u32[]{:S(2)}) collective-permute-start(bf16[192,1536]{1,0:T(8,128)(2,1)} %get-tuple-element.114), channel_id=1, source_target_pairs={{0,4},{1,3},{2,6},{3,1},{4,0},{5,7},{6,2},{7,5},{8,12},{9,11},{10,... | collective-permute-start | bytes 1769480 | tf_op jit(solution)/shard_map/ppermute | solution.py:453
  102.2 5.4 %grad_input.1 = (f32[256,768]{1,0:T(8,128)}, f32[264,768]{1,0:T(8,128)}) custom-call(bf16[512,1152]{1,0:T(8,128)(2,1)} %get-tuple-element.88.grads, bf16[768,2304]{1,0:T(8,128)(2,1)} %w_hbm.3, f32[256,768]{1,0:T(8,128)} %get-tuple-element.89.sum1, f32[8,768]{1,0:T(8,128)} %get-tuple-element.77.pool), custom_call_target="tpu_custom_call" | custom-call | flops 905969664 | bytes 7127040 | tf_op jit(solution)/shard_map/grad_input/pallas_call | solution.py:48
  108.9 6.9 %grad_out.1 = (bf16[1536,384]{1,0:T(8,128)(2,1)}, bf16[1536,384]{1,0:T(8,128)(2,1)}) custom-call(bf16[256,3072]{1,0:T(8,128)(2,1)} %get-tuple-element.122.active_own, bf16[256,3072]{1,0:T(8,128)(2,1)} %copy-done.27, bf16[256,384]{1,0:T(8,128)(2,1)} %get-tuple-element.123.down_own, bf16[256,384]{1,0:T(8,128)(2,1)} %copy-done.34), custom_call_target="tpu_custom_call" | custom-call | flops 1207959552 | bytes 5898240 | tf_op jit(solution)/shard_map/grad_out/pallas_call | solution.py:48
  118.2 2.2 %qkv_merge1.1 = (bf16[96,1536]{1,0:T(8,128)(2,1)}, bf16[112,1536]{1,0:T(8,128)(2,1)}, f32[16,768]{1,0:T(8,128)}) custom-call(bf16[208,1536]{1,0:T(8,128)(2,1)} %copy-done.4, bf16[192,1536]{1,0:T(8,128)(2,1)} %get-tuple-element.99.keep, f32[16,768]{1,0:T(8,128)} %get-tuple-element.100.vec), custom_call_target="tpu_custom_call" | custom-call | bytes 1966080 | tf_op jit(solution)/shard_map/qkv_merge1/pallas_call | solution.py:48
  125.4 6.2 %collective-permute-done.6.got = bf16[112,1536]{1,0:T(8,128)(2,1)S(1)} collective-permute-done((bf16[112,1536]{1,0:T(8,128)(2,1)}, bf16[112,1536]{1,0:T(8,128)(2,1)S(1)}, u32[]{:S(2)}, u32[]{:S(2)}) %collective-permute-start.6) | collective-permute-done | bytes 344096 | tf_op jit(solution)/shard_map/ppermute | solution.py:453
  134.2 2.6 %collective-permute-start.7 = (bf16[64,1536]{1,0:T(8,128)(2,1)}, bf16[64,1536]{1,0:T(8,128)(2,1)S(1)}, u32[]{:S(2)}, u32[]{:S(2)}) collective-permute-start(bf16[64,1536]{1,0:T(8,128)(2,1)} %get-tuple-element.104), channel_id=1, source_target_pairs={{0,16},{1,17},{2,18},{3,19},{4,20},{5,21},{6,22},{7,23},{8,24},{9,... | collective-permute-start | bytes 589832 | tf_op jit(solution)/shard_map/ppermute | solution.py:453
  136.8 7.1 %collective-permute-done.7.got = bf16[64,1536]{1,0:T(8,128)(2,1)S(1)} collective-permute-done((bf16[64,1536]{1,0:T(8,128)(2,1)}, bf16[64,1536]{1,0:T(8,128)(2,1)S(1)}, u32[]{:S(2)}, u32[]{:S(2)}) %collective-permute-start.7) | collective-permute-done | bytes 196640 | tf_op jit(solution)/shard_map/ppermute | solution.py:453
  151.7 2.8 %out_merge0.1 = (bf16[768,384]{1,0:T(8,128)(2,1)}, bf16[768,384]{1,0:T(8,128)(2,1)}) custom-call(bf16[1536,384]{1,0:T(8,128)(2,1)} %copy-done.1, bf16[1536,384]{1,0:T(8,128)(2,1)} %get-tuple-element.126.keep), custom_call_target="tpu_custom_call" | custom-call | bytes 3538944 | tf_op jit(solution)/shard_map/out_merge0/pallas_call | solution.py:48
  154.5 3.2 %collective-permute-start.19 = (bf16[768,384]{1,0:T(8,128)(2,1)}, bf16[768,384]{1,0:T(8,128)(2,1)S(1)}, u32[]{:S(2)}, u32[]{:S(2)}) collective-permute-start(bf16[768,384]{1,0:T(8,128)(2,1)} %get-tuple-element.127), channel_id=1, source_target_pairs={{0,8},{1,9},{2,10},{3,11},{4,12},{5,13},{6,14},{7,15},{8,0},{9,1},... | collective-permute-start | bytes 1769480 | tf_op jit(solution)/shard_map/ppermute | solution.py:453
  157.7 2.8 %collective-permute-done.14.got = bf16[48,1536]{1,0:T(8,128)(2,1)S(1)} collective-permute-done((bf16[48,1536]{1,0:T(8,128)(2,1)}, bf16[48,1536]{1,0:T(8,128)(2,1)S(1)}, u32[]{:S(2)}, u32[]{:S(2)}) %collective-permute-start.14) | collective-permute-done | bytes 147488 | tf_op jit(solution)/shard_map/ppermute | solution.py:453
  163.1 10.0 %collective-permute-done.19.got = bf16[768,384]{1,0:T(8,128)(2,1)S(1)} collective-permute-done((bf16[768,384]{1,0:T(8,128)(2,1)}, bf16[768,384]{1,0:T(8,128)(2,1)S(1)}, u32[]{:S(2)}, u32[]{:S(2)}) %collective-permute-start.19) | collective-permute-done | bytes 589856 | tf_op jit(solution)/shard_map/ppermute | solution.py:453
  176.9 14.6 %collective-permute-done.20.got = bf16[384,384]{1,0:T(8,128)(2,1)S(1)} collective-permute-done((bf16[384,384]{1,0:T(8,128)(2,1)}, bf16[384,384]{1,0:T(8,128)(2,1)S(1)}, u32[]{:S(2)}, u32[]{:S(2)}) %collective-permute-start.20) | collective-permute-done | bytes 294944 | tf_op jit(solution)/shard_map/ppermute | solution.py:453
  194.1 2.4 %collective-permute-start.21 = (bf16[192,384]{1,0:T(8,128)(2,1)}, bf16[192,384]{1,0:T(8,128)(2,1)S(1)}, u32[]{:S(2)}, u32[]{:S(2)}) collective-permute-start(bf16[192,384]{1,0:T(8,128)(2,1)} %get-tuple-element.131), channel_id=1, source_target_pairs={{0,4},{1,3},{2,6},{3,1},{4,0},{5,7},{6,2},{7,5},{8,12},{9,11},{10,... | collective-permute-start | bytes 442376 | tf_op jit(solution)/shard_map/ppermute | solution.py:453
  (143 shorter events, 53.5 us)
Async XLA Ops:
  0.7 2.1 %collective-permute-start = (bf16[256,768]{1,0:T(8,128)(2,1)}, bf16[256,768]{1,0:T(8,128)(2,1)S(1)}, u32[]{:S(2)}, u32[]{:S(2)}) collective-permute-start(bf16[256,768]{1,0:T(8,128)(2,1)} %bitcast.13), channel_id=1, source_target_pairs={{0,1},{1,0},{2,3},{3,2},{4,5},{5,4},{6,7},{7,6},{8,9},{9,8},{10,11... | collective-permute-start | bytes 1179656 | tf_op jit(solution)/shard_map/ppermute | solution.py:445
  13.1 4.6 %collective-permute-start.1 = (bf16[512,384]{1,0:T(8,128)(2,1)}, bf16[512,384]{1,0:T(8,128)(2,1)S(1)}, u32[]{:S(2)}, u32[]{:S(2)}) collective-permute-start(bf16[512,384]{1,0:T(8,128)(2,1)} %get-tuple-element.75.att_mine), channel_id=1, source_target_pairs={{0,1},{1,0},{2,3},{3,2},{4,5},{5,4},{6,7},{7,6},{8,9},{9,8},{10,11... | collective-permute-start | bytes 1179656 | tf_op jit(solution)/shard_map/ppermute | solution.py:445
  40.8 1.9 collective-permute-start.2
  41.0 21.6 %collective-permute-start.10 = (bf16[256,1536]{1,0:T(8,128)(2,1)}, bf16[256,1536]{1,0:T(8,128)(2,1)S(1)}, u32[]{:S(2)}, u32[]{:S(2)}) collective-permute-start(bf16[256,1536]{1,0:T(8,128)(2,1)} %get-tuple-element.111), channel_id=1, source_target_pairs={{0,1},{1,0},{2,3},{3,2},{4,5},{5,4},{6,7},{7,6},{8,9},{9,8},{10,11... | collective-permute-start | bytes 2359304 | tf_op jit(solution)/shard_map/ppermute | solution.py:445
  41.3 21.3 %collective-permute-start.9 = (bf16[256,768]{1,0:T(8,128)(2,1)S(1)}, bf16[256,768]{1,0:T(8,128)(2,1)S(1)}, u32[]{:S(2)}, u32[]{:S(2)}) collective-permute-start(bf16[256,768]{1,0:T(8,128)(2,1)S(1)} %copy-done.30), channel_id=1, source_target_pairs={{0,1},{1,0},{2,3},{3,2},{4,5},{5,4},{6,7},{7,6},{8,9},{9,8},{10,11... | collective-permute-start | bytes 1179656 | tf_op jit(solution)/shard_map/ppermute | solution.py:445
  59.8 17.6 %collective-permute-start.4 = (bf16[400,1536]{1,0:T(8,128)(2,1)}, bf16[400,1536]{1,0:T(8,128)(2,1)S(1)}, u32[]{:S(2)}, u32[]{:S(2)}) collective-permute-start(bf16[400,1536]{1,0:T(8,128)(2,1)} %get-tuple-element.95), channel_id=1, source_target_pairs={{0,2},{1,5},{2,0},{3,7},{4,6},{5,1},{6,4},{7,3},{8,10},{9,13},{10,... | collective-permute-start | bytes 3686408 | tf_op jit(solution)/shard_map/ppermute | solution.py:453
  62.5 45.2 %collective-permute-start.16 = (bf16[256,3072]{1,0:T(8,128)(2,1)S(1)}, bf16[256,3072]{1,0:T(8,128)(2,1)S(1)}, u32[]{:S(2)}, u32[]{:S(2)}) collective-permute-start(bf16[256,3072]{1,0:T(8,128)(2,1)S(1)} %copy-done.26), channel_id=1, source_target_pairs={{0,1},{1,0},{2,3},{3,2},{4,5},{5,4},{6,7},{7,6},{8,9},{9,8},{10,11... | collective-permute-start | bytes 4718600 | tf_op jit(solution)/shard_map/ppermute | solution.py:445
  69.9 26.1 %collective-permute-start.11 = (bf16[384,1536]{1,0:T(8,128)(2,1)}, bf16[384,1536]{1,0:T(8,128)(2,1)S(1)}, u32[]{:S(2)}, u32[]{:S(2)}) collective-permute-start(bf16[384,1536]{1,0:T(8,128)(2,1)} %get-tuple-element.112), channel_id=1, source_target_pairs={{0,2},{1,5},{2,0},{3,7},{4,6},{5,1},{6,4},{7,3},{8,10},{9,13},{10,... | collective-permute-start | bytes 3538952 | tf_op jit(solution)/shard_map/ppermute | solution.py:453
  81.4 36.0 %collective-permute-start.5 = (bf16[208,1536]{1,0:T(8,128)(2,1)}, bf16[208,1536]{1,0:T(8,128)(2,1)S(1)}, u32[]{:S(2)}, u32[]{:S(2)}) collective-permute-start(bf16[208,1536]{1,0:T(8,128)(2,1)} %get-tuple-element.98), channel_id=1, source_target_pairs={{0,4},{1,3},{2,6},{3,1},{4,0},{5,7},{6,2},{7,5},{8,12},{9,11},{10,... | collective-permute-start | bytes 1916936 | tf_op jit(solution)/shard_map/ppermute | solution.py:453
  83.4 24.2 %collective-permute-start.17 = (bf16[256,384]{1,0:T(8,128)(2,1)S(1)}, bf16[256,384]{1,0:T(8,128)(2,1)S(1)}, u32[]{:S(2)}, u32[]{:S(2)}) collective-permute-start(bf16[256,384]{1,0:T(8,128)(2,1)S(1)} %copy-done.33), channel_id=1, source_target_pairs={{0,1},{1,0},{2,3},{3,2},{4,5},{5,4},{6,7},{7,6},{8,9},{9,8},{10,11... | collective-permute-start | bytes 589832 | tf_op jit(solution)/shard_map/ppermute | solution.py:445
  99.9 22.1 %collective-permute-start.12 = (bf16[192,1536]{1,0:T(8,128)(2,1)}, bf16[192,1536]{1,0:T(8,128)(2,1)S(1)}, u32[]{:S(2)}, u32[]{:S(2)}) collective-permute-start(bf16[192,1536]{1,0:T(8,128)(2,1)} %get-tuple-element.114), channel_id=1, source_target_pairs={{0,4},{1,3},{2,6},{3,1},{4,0},{5,7},{6,2},{7,5},{8,12},{9,11},{10,... | collective-permute-start | bytes 1769480 | tf_op jit(solution)/shard_map/ppermute | solution.py:453
  107.6 38.8 %collective-permute-start.3 = (f32[264,768]{1,0:T(8,128)}, f32[264,768]{1,0:T(8,128)S(1)}, u32[]{:S(2)}, u32[]{:S(2)}) collective-permute-start(f32[264,768]{1,0:T(8,128)} %get-tuple-element.90), channel_id=1, source_target_pairs={{0,1},{1,0},{2,3},{3,2},{4,5},{5,4},{6,7},{7,6},{8,9},{9,8},{10,11... | collective-permute-start | bytes 2433032 | tf_op jit(solution)/shard_map/ppermute | solution.py:445
  115.9 34.8 %collective-permute-start.18 = (bf16[1536,384]{1,0:T(8,128)(2,1)}, bf16[1536,384]{1,0:T(8,128)(2,1)S(1)}, u32[]{:S(2)}, u32[]{:S(2)}) collective-permute-start(bf16[1536,384]{1,0:T(8,128)(2,1)} %get-tuple-element.125), channel_id=1, source_target_pairs={{0,2},{1,5},{2,0},{3,7},{4,6},{5,1},{6,4},{7,3},{8,10},{9,13},{10,... | collective-permute-start | bytes 3538952 | tf_op jit(solution)/shard_map/ppermute | solution.py:453
  120.4 11.2 %collective-permute-start.6 = (bf16[112,1536]{1,0:T(8,128)(2,1)}, bf16[112,1536]{1,0:T(8,128)(2,1)S(1)}, u32[]{:S(2)}, u32[]{:S(2)}) collective-permute-start(bf16[112,1536]{1,0:T(8,128)(2,1)} %get-tuple-element.101), channel_id=1, source_target_pairs={{0,8},{1,9},{2,10},{3,11},{4,12},{5,13},{6,14},{7,15},{8,0},{9,1},... | collective-permute-start | bytes 1032200 | tf_op jit(solution)/shard_map/ppermute | solution.py:453
  124.9 22.5 %collective-permute-start.13 = (bf16[96,1536]{1,0:T(8,128)(2,1)}, bf16[96,1536]{1,0:T(8,128)(2,1)S(1)}, u32[]{:S(2)}, u32[]{:S(2)}) collective-permute-start(bf16[96,1536]{1,0:T(8,128)(2,1)} %get-tuple-element.116), channel_id=1, source_target_pairs={{0,8},{1,9},{2,10},{3,11},{4,12},{5,13},{6,14},{7,15},{8,0},{9,1},... | collective-permute-start | bytes 884744 | tf_op jit(solution)/shard_map/ppermute | solution.py:453
  134.2 9.7 %collective-permute-start.7 = (bf16[64,1536]{1,0:T(8,128)(2,1)}, bf16[64,1536]{1,0:T(8,128)(2,1)S(1)}, u32[]{:S(2)}, u32[]{:S(2)}) collective-permute-start(bf16[64,1536]{1,0:T(8,128)(2,1)} %get-tuple-element.104), channel_id=1, source_target_pairs={{0,16},{1,17},{2,18},{3,19},{4,20},{5,21},{6,22},{7,23},{8,24},{9,... | collective-permute-start | bytes 589832 | tf_op jit(solution)/shard_map/ppermute | solution.py:453
  146.4 16.6 %collective-permute-start.8 = (f32[40,1536]{1,0:T(8,128)}, f32[40,1536]{1,0:T(8,128)S(1)}, u32[]{:S(2)}, u32[]{:S(2)}) collective-permute-start(f32[40,1536]{1,0:T(8,128)} %get-tuple-element.108), channel_id=1, source_target_pairs={{0,1},{1,0},{2,3},{3,2},{4,5},{5,4},{6,7},{7,6},{8,9},{9,8},{10,11... | collective-permute-start | bytes 737288 | tf_op jit(solution)/shard_map/ppermute | solution.py:445
  149.9 10.6 %collective-permute-start.14 = (bf16[48,1536]{1,0:T(8,128)(2,1)}, bf16[48,1536]{1,0:T(8,128)(2,1)S(1)}, u32[]{:S(2)}, u32[]{:S(2)}) collective-permute-start(bf16[48,1536]{1,0:T(8,128)(2,1)} %get-tuple-element.118), channel_id=1, source_target_pairs={{0,16},{1,17},{2,18},{3,19},{4,20},{5,21},{6,22},{7,23},{8,24},{9,... | collective-permute-start | bytes 442376 | tf_op jit(solution)/shard_map/ppermute | solution.py:453
  154.5 18.6 %collective-permute-start.19 = (bf16[768,384]{1,0:T(8,128)(2,1)}, bf16[768,384]{1,0:T(8,128)(2,1)S(1)}, u32[]{:S(2)}, u32[]{:S(2)}) collective-permute-start(bf16[768,384]{1,0:T(8,128)(2,1)} %get-tuple-element.127), channel_id=1, source_target_pairs={{0,8},{1,9},{2,10},{3,11},{4,12},{5,13},{6,14},{7,15},{8,0},{9,1},... | collective-permute-start | bytes 1769480 | tf_op jit(solution)/shard_map/ppermute | solution.py:453
  163.0 39.3 %collective-permute-start.15 = (f32[24,1536]{1,0:T(8,128)}, f32[24,1536]{1,0:T(8,128)S(1)}, u32[]{:S(2)}, u32[]{:S(2)}) collective-permute-start(f32[24,1536]{1,0:T(8,128)} %get-tuple-element.121), channel_id=1, source_target_pairs={{0,1},{1,0},{2,3},{3,2},{4,5},{5,4},{6,7},{7,6},{8,9},{9,8},{10,11... | collective-permute-start | bytes 442376 | tf_op jit(solution)/shard_map/ppermute | solution.py:445
  176.1 26.2 %copy-start.15 = (f32[24,1536]{1,0:T(8,128)S(1)}, f32[24,1536]{1,0:T(8,128)}, u32[]{:S(2)}) copy-start(f32[24,1536]{1,0:T(8,128)} %get-tuple-element.120) | copy-start | bytes 442372
  176.1 15.5 %collective-permute-start.20 = (bf16[384,384]{1,0:T(8,128)(2,1)}, bf16[384,384]{1,0:T(8,128)(2,1)S(1)}, u32[]{:S(2)}, u32[]{:S(2)}) collective-permute-start(bf16[384,384]{1,0:T(8,128)(2,1)} %get-tuple-element.129), channel_id=1, source_target_pairs={{0,16},{1,17},{2,18},{3,19},{4,20},{5,21},{6,22},{7,23},{8,24},{9,... | collective-permute-start | bytes 884744 | tf_op jit(solution)/shard_map/ppermute | solution.py:453
  194.1 5.8 %collective-permute-start.21 = (bf16[192,384]{1,0:T(8,128)(2,1)}, bf16[192,384]{1,0:T(8,128)(2,1)S(1)}, u32[]{:S(2)}, u32[]{:S(2)}) collective-permute-start(bf16[192,384]{1,0:T(8,128)(2,1)} %get-tuple-element.131), channel_id=1, source_target_pairs={{0,4},{1,3},{2,6},{3,1},{4,0},{5,7},{6,2},{7,5},{8,12},{9,11},{10,... | collective-permute-start | bytes 442376 | tf_op jit(solution)/shard_map/ppermute | solution.py:453
  202.3 1.6 collective-permute-start.22
  (34 other events, 202.9 us)

commit v2 on v1

v2 whole, which is shorter than its diff:
```python
import functools
import math

import jax
import jax.numpy as jnp
from jax import lax
from jax.experimental import pallas as pl
from jax.experimental.pallas import tpu as pltpu
from jax.sharding import PartitionSpec as P

HEADS = 12
EPSILON = 1e-12
HIDE = -1e30
GROUPS = 16
BF = jnp.bfloat16
F32 = jnp.float32
MIB = 2**20
MERGE_US = 0.3
KERNEL_US = 0.3
WEIGHTS = {"out": 1, "in": 1, "qkv": 3, "o": 1}
PARTS = {
    "a": ("out", 0, 384, "xy12"),
    "b": ("in", 0, 768, "xy12"),
    "c": ("in", 768, 1536, "1xy2"),
    "d": ("qkv", 0, 384, "12xy"),
    "e": ("qkv", 384, 1152, "yx12"),
}
WITH_O = "c"
WITH_VECTORS = "d"
PLAN = (
    "BWD", "OUT", "IN", "BACK", "out", "QKV", "INPUT", "in", "out", "qkv", "input", "in",
    "out", "qkv", "in", "out", "qkv", "in", "qkv",
)


def sds(shape, dtype):
    return jax.ShapeDtypeStruct(shape, dtype)


def nn(left, right):
    return jnp.dot(left, right, preferred_element_type=F32)


def nt(left, right):
    return lax.dot_general(left, right, (((1,), (1,)), ((), ())), preferred_element_type=F32)


def tn(left, right):
    return lax.dot_general(left, right, (((0,), (0,)), ((), ())), preferred_element_type=F32)


class Line:
    def __init__(self):
        self.last = None

    def call(self, kernel, outs, *args, scratch=(), hbm=(), smem=(), name=None, vmem=16, us=KERNEL_US, end=False):
        if end:
            outs = [sds((8, 128), F32), *outs]
        specs = []
        lead = len(args)
        for i in range(lead):
            space = pltpu.HBM if i in hbm else pltpu.SMEM if i in smem else pltpu.VMEM
            specs.append(pl.BlockSpec(memory_space=space))
        args = [
            pltpu.with_memory_space_constraint(arg, pltpu.HBM) if i in hbm else arg
            for i, arg in enumerate(args)
        ]
        after = () if self.last is None else (self.last,)
        specs += [pl.BlockSpec(memory_space=pl.ANY) for _ in after]

        def body(*refs):
            rest = refs[lead + len(after) :]
            if end:
                rest[0][...] = jnp.zeros((8, 128), F32)
                rest = rest[1:]
            kernel(*refs[:lead], *rest)

        made = pl.pallas_call(
            body,
            out_shape=list(outs),
            in_specs=specs,
            out_specs=[pl.BlockSpec(memory_space=pltpu.VMEM) for _ in outs],
            scratch_shapes=list(scratch),
            compiler_params=pltpu.CompilerParams(vmem_limit_bytes=vmem * MIB),
            cost_estimate=pl.CostEstimate(flops=int(us * 1.1e9), bytes_accessed=1024, transcendentals=0),
            name=name,
        )(*args, *after)
        self.last = made[0]
        return made[1:] if end else made


def segment_of(positions, lens_ref):
    ids = jnp.zeros_like(positions)
    end = jnp.int32(0)
    for j in range(lens_ref.shape[1]):
        end = end + lens_ref[0, j]
        ids = ids + (positions >= end).astype(jnp.int32)
    return ids


def own_first(index, half, s):
    return jnp.where(index < half, index + s * half, index - half + (1 - s) * half)


def normalise(total):
    centered = total - jnp.mean(total, axis=-1, keepdims=True)
    inverse = lax.rsqrt(jnp.mean(centered * centered, axis=-1, keepdims=True) + EPSILON)
    return centered * inverse, inverse


def norm_pull(grad, normal, inverse, gain):
    scaled = grad * gain
    return inverse * (
        scaled
        - jnp.mean(scaled, axis=-1, keepdims=True)
        - normal * jnp.mean(scaled * normal, axis=-1, keepdims=True)
    )


def column_sum(matrix):
    return jnp.sum(matrix, axis=0, keepdims=True)


def project_kernel(own_hbm, w_hbm, b_hbm, own, w_mine, bias, lin, b_buf, sems):
    width = own.shape[1]
    mine = width // 2
    s = lax.axis_index("seq")
    first = pltpu.make_async_copy(own_hbm, own, sems.at[3])
    first.start()
    copies = []
    for c in range(3):
        start = pl.multiple_of(c * width + s * mine, 128)
        copies.append(pltpu.make_async_copy(w_hbm.at[:, pl.ds(start, mine)], w_mine.at[c], sems.at[c]))
        copies[-1].start()
    second = pltpu.make_async_copy(b_hbm, b_buf, sems.at[4])
    second.start()
    second.wait()
    column = pl.ds(pl.multiple_of(s * mine, 128), mine)
    bias[...] = jnp.zeros_like(bias)
    bias[0:1, :] = b_buf[0:1, column].astype(F32)
    bias[2:3, :] = b_buf[1:2, column].astype(F32)
    first.wait()
    for c in range(3):
        copies[c].wait()
        lin[:, c * mine : (c + 1) * mine] = nn(own[...], w_mine[c]) + bias[c : c + 1, :]


def attend_kernel(
    lens, other, w_mine, bias, lin, w_o_hbm, w_in_hbm, w_out_hbm,
    q_out, k_out, v_out, kt_out, expo_out, scale_out, att_t, att_out, w_o, w_in, w_out, sems,
):
    half, width = other.shape
    length = 2 * half
    mine = width // 2
    pair = 2 * (width // HEADS)
    head = pair // 2
    s = lax.axis_index("seq")
    copies = [
        pltpu.make_async_copy(source, target, sems.at[i])
        for i, (source, target) in enumerate(((w_o_hbm, w_o), (w_in_hbm, w_in), (w_out_hbm, w_out)))
    ]
    for copy in copies:
        copy.start()
    parts = []
    for c in range(3):
        rest = nn(other[...], w_mine[c]) + bias[c : c + 1, :]
        parts.append(jnp.concatenate([lin[:, c * mine : (c + 1) * mine], rest], axis=0))
    q_all, k_all, v_all = parts
    q_all = q_all.astype(BF).astype(F32) * (1.0 / math.sqrt(head))
    q_out[...] = q_all.astype(BF)
    k_out[...] = k_all.astype(BF)
    v_out[...] = v_all.astype(BF)
    kt_out[...] = k_all.T.astype(BF)
    vt = v_all.T.astype(BF)
    rows = own_first(lax.broadcasted_iota(jnp.int32, (length, pair), 0), half, s)
    lane = lax.broadcasted_iota(jnp.int32, (length, pair), 1)
    same = segment_of(rows, lens) == lane % head
    in_range = lane % head < lens.shape[1]
    mark_k = jnp.where(same, 1.0, 0.0)
    mark_q = jnp.where(jnp.logical_and(in_range, jnp.logical_not(same)), HIDE, 0.0)
    first = lane < head
    for j in range(mine // pair):
        cols = slice(j * pair, (j + 1) * pair)
        q2, k2 = q_all[:, cols], k_all[:, cols]
        pieces = []
        for a in range(2):
            keep = first if a == 0 else jnp.logical_not(first)
            k_m = jnp.where(keep, k2, mark_k).astype(BF)
            q_m = jnp.where(keep, q2, mark_q).astype(BF)
            scores = nt(k_m, q_m)
            top = jnp.max(scores, axis=0, keepdims=True)
            expo = jnp.exp(scores - top)
            scale = 1.0 / jnp.sum(expo, axis=0, keepdims=True)
            low = expo.astype(BF)
            h = 2 * j + a
            expo_out[h] = low
            scale_out[h : h + 1, :] = scale
            pieces.append(nn(vt[h * head : (h + 1) * head, :], low) * scale)
        both = jnp.concatenate(pieces, axis=0)
        att_t[cols, :] = both
        att_out[:, cols] = both.T.astype(BF)
    for copy in copies:
        copy.wait()


def forward_kernel(
    lens,
    own,
    att_mine,
    att_got,
    w_o,
    b_o,
    gain1,
    shift1,
    w_in,
    b_in,
    w_out,
    b_out,
    gain2,
    shift2,
    cot,
    mid_out,
    active_out,
    pull_out,
    normal_out,
    inverse_out,
    sum2_out,
    down_keep,
    down_send,
    out_out,
    pool_out,
    vec_out,
    down_acc,
):
    half, width = own.shape
    mine = width // 2
    ff = w_in.shape[1]
    s = lax.axis_index("seq")
    row_a = pl.ds(pl.multiple_of(s * mine, 128), mine)
    row_b = pl.ds(pl.multiple_of((1 - s) * mine, 128), mine)
    branch = nn(att_mine[0:half, :], w_o[row_a, :]) + nn(att_got[half:, :], w_o[row_b, :])
    normal, inverse = normalise(own[...].astype(F32) + (branch + b_o[...].astype(F32)))
    middle = normal * gain1[...].astype(F32) + shift1[...].astype(F32)
    low = middle.astype(BF)
    mid_out[...] = low
    normal_out[...] = normal
    inverse_out[...] = inverse
    down_acc[...] = middle + b_out[...].astype(F32)
    step = 1024
    for c in range(0, ff, step):
        cols = slice(c, c + step)
        upper = nn(low, w_in[:, cols]) + b_in[:, cols].astype(F32)
        cdf = 0.5 + 0.5 * lax.erf(upper * (1.0 / math.sqrt(2.0)))
        density = jnp.exp(-0.5 * upper * upper) * (1.0 / math.sqrt(2.0 * math.pi))
        act = (upper * cdf).astype(BF)
        active_out[:, cols] = act
        pull_out[:, cols] = cdf + upper * density
        down_acc[...] += nn(act, w_out[cols, :])
    normal2, inverse2 = normalise(down_acc[...])
    gain = gain2[...].astype(F32)
    final = normal2 * gain + shift2[...].astype(F32)
    out_out[...] = final.astype(BF)
    rows = lax.broadcasted_iota(jnp.int32, (half, width), 0) + s * half
    ids = segment_of(rows, lens)
    pool_out[...] = jnp.zeros_like(pool_out)
    for t in range(lens.shape[1]):
        pool_out[t : t + 1, :] = column_sum(jnp.where(ids == t, final, 0.0))
    grad = cot[...].astype(F32)
    sum2 = norm_pull(grad, normal2, inverse2, gain)
    sum2_out[...] = sum2
    down = sum2.astype(BF)
    down_acc[...] = sum2
    down_keep[...] = down_acc[:, row_a].astype(BF)
    down_send[...] = down_acc[:, row_b].astype(BF)
    vec_out[...] = jnp.zeros_like(vec_out)
    vec_out[0:1, :] = column_sum(grad * normal2)
    vec_out[1:2, :] = column_sum(grad)
    vec_out[2:3, :] = column_sum(down.astype(F32))


def backward_kernel(
    sum2, pull, normal, inverse, gain1, w_in, w_out,
    up_keep, up_send, sum1_out, branch_out, vec_out, mid_acc,
):
    width, ff = w_in.shape
    s = lax.axis_index("seq")
    step = 768
    per = ff // 2 // step
    mid_acc[...] = sum2[...]
    low = sum2[...].astype(BF)
    vec_out[...] = jnp.zeros_like(vec_out)
    sums = []
    for i in range(2 * per):
        block = (i // per + s) % 2
        start = pl.multiple_of(block * (ff // 2) + (i % per) * step, 128)
        cols = pl.ds(start, step)
        grad_upper = (nt(low, w_out[cols, :]) * pull[:, cols]).astype(BF)
        place = up_keep if i < per else up_send
        place[:, (i % per) * step : (i % per + 1) * step] = grad_upper
        sums.append(column_sum(grad_upper.astype(F32)))
        mid_acc[...] += nt(grad_upper, w_in[:, cols])
    ups = [jnp.concatenate(sums[:per], axis=1), jnp.concatenate(sums[per:], axis=1)]
    for b in range(2):
        line = jnp.where(s == b, ups[0], ups[1])
        for r in range(ff // 2 // width):
            row = b * (ff // 2 // width) + r
            vec_out[row : row + 1, :] = line[:, r * width : (r + 1) * width]
    base = ff // width
    grad_mid = mid_acc[...]
    vec_out[base : base + 1, :] = column_sum(grad_mid * normal[...])
    vec_out[base + 1 : base + 2, :] = column_sum(grad_mid)
    sum1 = norm_pull(grad_mid, normal[...], inverse[...], gain1[...].astype(F32))
    sum1_out[...] = sum1
    branch = sum1.astype(BF)
    branch_out[...] = branch
    vec_out[base + 2 : base + 3, :] = column_sum(branch.astype(F32))


def attend_back_kernel(
    branch_own, branch_got, w_o, q, k, v, kt, expo, scale, att_t, grad_out, vec_out
):
    length, mine = q.shape
    width = w_o.shape[1]
    head = width // HEADS
    pair = 2 * head
    s = lax.axis_index("seq")
    w_mine = w_o[pl.ds(pl.multiple_of(s * mine, 128), mine), :]
    grad_t = jnp.concatenate([nt(w_mine, branch_own[...]), nt(w_mine, branch_got[...])], axis=1)
    lane = lax.broadcasted_iota(jnp.int32, (length, pair), 1)
    first = lane < head
    vec_out[...] = jnp.zeros_like(vec_out)
    for j in range(mine // pair):
        cols = slice(j * pair, (j + 1) * pair)
        q2 = q[:, cols]
        v2 = v[:, cols].astype(F32)
        scaled, inners = [], []
        for h in (2 * j, 2 * j + 1):
            part = slice(h * head, (h + 1) * head)
            times = scale[h : h + 1, :]
            scaled.append(grad_t[part, :] * times)
            inners.append(jnp.sum(att_t[part, :] * scaled[-1], axis=0, keepdims=True))
        a2 = jnp.concatenate(scaled, axis=0).astype(BF)
        dq, dk, dv = [], [], []
        for a in range(2):
            h = 2 * j + a
            keep = first if a == 0 else jnp.logical_not(first)
            v_m = jnp.where(keep, v2, 0.0).astype(BF)
            grad_p = nn(v_m, a2)
            low = expo[h]
            raw = (low.astype(F32) * (grad_p - inners[a])).astype(BF)
            dk.append(nn(raw, q2))
            dv.append(nt(low, a2))
            dq.append(nn(kt[h * head : (h + 1) * head, :], raw))
        dq_low = (jnp.concatenate(dq, axis=0) * (1.0 / math.sqrt(head))).T.astype(BF)
        dk_low = jnp.where(first, dk[0], dk[1]).astype(BF)
        dv_low = jnp.where(first, dv[0], dv[1]).astype(BF)
        grad_out[:, cols] = dq_low
        grad_out[:, mine + j * pair : mine + (j + 1) * pair] = dk_low
        grad_out[:, 2 * mine + j * pair : 2 * mine + (j + 1) * pair] = dv_low
        vec_out[0:1, cols] = column_sum(dq_low.astype(F32))
        vec_out[1:2, cols] = column_sum(dv_low.astype(F32))


def slot_of(chunk, order):
    if order is None:
        return jnp.int32(chunk)
    rel = jnp.bitwise_xor(jnp.int32(chunk), lax.axis_index("dp"))
    s = lax.axis_index("seq")
    slots = []
    for bits in order:
        slot = jnp.int32(0)
        for bit in bits:
            slot = slot * 2 + jnp.bitwise_and(lax.shift_right_logical(rel, jnp.int32(bit)), 1)
        slots.append(slot)
    return jnp.where(s == 0, slots[0], slots[1])


def place(values, chunk, order, keep, send, cols=None):
    half = GROUPS // 2
    slot = slot_of(chunk, order)
    rows = values.shape[0]
    if cols is None:
        cols = slice(0, values.shape[1])

    def at(index):
        return pl.ds(pl.multiple_of(index * rows, 16), rows)

    @pl.when(slot < half)
    def _():
        keep[at(slot), cols] = values

    @pl.when(slot >= half)
    def _():
        send[at(slot - half), cols] = values


def grad_out_kernel(parts, active_own, active_got, down_own, down_got, *outs):
    ff = active_own.shape[1]
    rows = ff // GROUPS
    block = 2 * rows
    for i in range(GROUPS // 2):
        cols = slice(i * block, (i + 1) * block)
        got = (
            tn(active_own[:, cols], down_own[...]) + tn(active_got[:, cols], down_got[...])
        ).astype(BF)
        for b in range(2):
            for p, (start, stop, order) in enumerate(parts):
                values = got[b * rows : (b + 1) * rows, start:stop]
                place(values, 2 * i + b, order, outs[2 * p], outs[2 * p + 1])


def grad_in_kernel(
    parts, with_o, mid_own, mid_got, up_own, up_got, att_mine, att_got, branch_own, branch_got, *outs
):
    half, width = mid_own.shape
    mine = width // 2
    rows = width // GROUPS
    for i in range(2):
        cols = slice(i * mine, (i + 1) * mine)
        for p, (start, stop, order) in enumerate(parts):
            for n in range(start, stop, 512):
                out = slice(n, min(n + 512, stop))
                got = (
                    tn(mid_own[:, cols], up_own[:, out]) + tn(mid_got[:, cols], up_got[:, out])
                ).astype(BF)
                to = slice(n - start, out.stop - start)
                for b in range(GROUPS // 2):
                    place(
                        got[b * rows : (b + 1) * rows, :], i * (GROUPS // 2) + b, order,
                        outs[2 * p], outs[2 * p + 1], to,
                    )
    s = lax.axis_index("seq")
    column = pl.ds(pl.multiple_of(s * mine, 128), mine)
    mine_o = tn(att_mine[0:half, :], branch_own[:, column]) + tn(att_mine[half:, :], branch_got[:, column])
    got_o = tn(att_got[half:, :], branch_own[:, column]) + tn(att_got[0:half, :], branch_got[:, column])
    start, stop, order = parts[with_o]
    to = slice(stop - start, stop - start + mine)
    for i in range(2):
        got = jnp.where(s == i, mine_o, got_o).astype(BF)
        for b in range(GROUPS // 2):
            place(
                got[b * rows : (b + 1) * rows, :], i * (GROUPS // 2) + b, order,
                outs[2 * with_o], outs[2 * with_o + 1], to,
            )


def pack_vectors(table, send, start):
    high = table.astype(BF)
    rest = (table - high.astype(F32)).astype(BF)
    width = min(table.shape[1], send.shape[1])
    row = start
    for piece in (high, rest):
        for c in range(0, table.shape[1], width):
            send[row : row + 16, 0:width] = piece[:, c : c + width]
            row += 16
    return high.astype(F32) + rest.astype(F32)


def unpack_vectors(got, start, total):
    width = min(total, got.shape[1])
    count = total // width
    parts = [got[start + 16 * i : start + 16 * (i + 1), 0:width].astype(F32) for i in range(2 * count)]
    return jnp.concatenate([parts[i] + parts[count + i] for i in range(count)], axis=1)


def vector_rows(total, cols):
    return 32 * (total // min(total, cols))


def grad_qkv_kernel(parts, with_vectors, own, other, grads, vec_f, vec_b, vec_a, *outs):
    half, width = own.shape
    mine = width // 2
    rows = width // GROUPS
    s = lax.axis_index("seq")
    for i in range(2):
        cols = slice(i * mine, (i + 1) * mine)
        for p, (start, stop, order) in enumerate(parts):
            for n in range(start, stop, mine):
                out = slice(n, n + mine)
                got = (
                    tn(own[:, cols], grads[0:half, out]) + tn(other[:, cols], grads[half:, out])
                ).astype(BF)
                to = slice(n - start, n - start + mine)
                for b in range(GROUPS // 2):
                    place(
                        got[b * rows : (b + 1) * rows, :], i * (GROUPS // 2) + b, order,
                        outs[2 * p], outs[2 * p + 1], to,
                    )
    zero = jnp.zeros((1, mine), F32)
    lines = []
    for r in range(2):
        line = vec_a[r : r + 1, :]
        lines.append(
            jnp.concatenate([jnp.where(s == 0, line, zero), jnp.where(s == 0, zero, line)], axis=1)
        )
    table = jnp.concatenate(lines + [vec_b[0:7, :], vec_f[0:3, :], jnp.zeros((4, width), F32)], axis=0)
    outs[-1][...] = pack_vectors(table, outs[2 * with_vectors + 1], GROUPS // 2 * rows)


def grad_input_kernel(grads, w_mine, sum1, pool, keep, send):
    half, width = sum1.shape
    mine = width // 2
    a, b = sum1[...], jnp.zeros((half, width), F32)
    for c in range(3):
        cols = slice(c * mine, (c + 1) * mine)
        a = a + nt(grads[0:half, cols], w_mine[c])
        b = b + nt(grads[half:, cols], w_mine[c])
    keep[...] = a
    send[0:half, :] = b
    send[half:, :] = pool[...]


def merge_kernel(rows, got, keep, keep_out, send_out):
    total = keep[0:rows, :].astype(F32) + got[0:rows, :].astype(F32)
    keep_out[...] = total[0 : rows // 2, :].astype(BF)
    send_out[...] = total[rows // 2 :, :].astype(BF)


def merge_vec_kernel(rows, got, keep, vec, keep_out, send_out, vec_out):
    merge_kernel(rows, got, keep, keep_out, send_out.at[0 : rows // 2, :])
    table = vec[...] + unpack_vectors(got, rows, vec.shape[1])
    vec_out[...] = pack_vectors(table, send_out, rows // 2)


def last_kernel(got, keep, keep_out, send_out, acc):
    rows = keep.shape[0]
    s = lax.axis_index("seq")
    acc[...] = keep[...].astype(F32) + got[0:rows, :].astype(F32)
    keep_out[...] = acc[pl.ds(pl.multiple_of(s * (rows // 2), 8), rows // 2), :]
    send_out[...] = acc[pl.ds(pl.multiple_of((1 - s) * (rows // 2), 8), rows // 2), :]


def last_vec_kernel(got, keep, vec, keep_out, send_out, acc):
    rows = keep.shape[0]
    last_kernel(got, keep, keep_out, send_out.at[0 : rows // 2, :], acc)
    table = vec[...] + unpack_vectors(got, rows, vec.shape[1])
    width = min(table.shape[1], keep.shape[1])
    for i, c in enumerate(range(0, table.shape[1], width)):
        send_out[rows // 2 + 16 * i : rows // 2 + 16 * (i + 1), 0:width] = table[:, c : c + width]


def finish_kernel(pieces, places, *refs):
    flat = refs[-1]
    count = len(places)
    per = count // pieces
    s = lax.axis_index("seq")
    for j, (p, lane) in enumerate(places):
        keep, got = refs[2 * p], refs[2 * p + 1]
        rows = keep.shape[0]
        cols = slice(lane, lane + 128)
        first, second = keep[:, cols], got[0:rows, cols]
        line = j // per * 2 * per + j % per
        flat[pl.ds(line, rows, stride=2 * count), :] = jnp.where(s == 0, first, second)
        flat[pl.ds(line + per, rows, stride=2 * count), :] = jnp.where(s == 0, second, first)


def finish_vectors_kernel(rows, width, sent, got, b_qv, b_o, gain1, shift1, b_in, b_out, gain2, shift2):
    half = min(width, sent.shape[1])
    count = width // half
    total = sent[rows:, 0:half] + got[rows:, 0:half]
    table = jnp.concatenate([total[16 * i : 16 * (i + 1), :] for i in range(count)], axis=1)
    b_qv[...] = table[0:2, :]
    base = b_in.shape[0] * 128 // width
    for r in range(base):
        for c in range(width // 128):
            line = r * (width // 128) + c
            b_in[line : line + 1, :] = table[2 + r : 3 + r, c * 128 : (c + 1) * 128]
    for i, ref in enumerate((gain1, shift1, b_o, gain2, shift2, b_out)):
        for c in range(width // 128):
            ref[c : c + 1, :] = table[2 + base + i : 3 + base + i, c * 128 : (c + 1) * 128]


def finish_input_kernel(lens, keep, sent, got, d_input, pooled):
    half = keep.shape[0]
    d_input[...] = keep[...] + got[0:half, :]
    total = sent[half:, :] + got[half:, :]
    for t in range(lens.shape[1]):
        pooled[t : t + 1, :] = total[t : t + 1, :] / lens[0, t].astype(F32)


def swap(x, axis="seq"):
    return lax.ppermute(x, axis, [(0, 1), (1, 0)])


def send_to(x, phase, order, count):
    pairs = []
    for d in range(count):
        for s in range(2):
            pairs.append((2 * d + s, 2 * (d ^ (1 << order[s][phase])) + s))
    return lax.ppermute(x, ("dp", "seq"), pairs)


class Part:
    def __init__(self, keep, send, order, vec):
        self.keep, self.sent, self.order, self.vec, self.got = keep, send, order, vec, None


class Sum:
    def __init__(self, line, parts, count, name):
        self.line, self.parts, self.count, self.name = line, parts, count, name
        self.phase = 0
        self.send()

    def send(self):
        for part in self.parts:
            if self.phase == len(part.order[0]):
                part.got = swap(part.sent)
            else:
                part.got = send_to(part.sent, self.phase, part.order, self.count)

    def step(self):
        last = self.phase == len(self.parts[0].order[0]) - 1
        dtype = F32 if last else BF
        args, outs, scratch, jobs = [], [], [], []
        for part in self.parts:
            rows, cols = part.keep.shape
            half = rows // 2
            extra = 0 if part.vec is None else vector_rows(part.vec.shape[1], cols)
            args += [part.got, part.keep]
            outs += [sds((half, cols), dtype), sds((half + (extra // 2 if last else extra), cols), dtype)]
            if last:
                scratch.append(pltpu.VMEM((rows, cols), F32))
            if part.vec is None:
                jobs.append((last_kernel if last else functools.partial(merge_kernel, rows), 2, 2))
            elif last:
                args.append(part.vec)
                jobs.append((last_vec_kernel, 3, 2))
            else:
                args.append(part.vec)
                outs.append(sds(part.vec.shape, F32))
                jobs.append((functools.partial(merge_vec_kernel, rows), 3, 3))

        def kernel(*refs):
            i, o, t = 0, len(args), len(args) + len(outs)
            for run, reads, writes in jobs:
                run(*refs[i : i + reads], *refs[o : o + writes], *([refs[t]] if last else []))
                i, o, t = i + reads, o + writes, t + 1

        made = self.line.call(
            kernel, outs, *args, scratch=scratch, name=f"sum_{self.name}_{self.phase}", vmem=10, us=MERGE_US
        )
        made = list(made)
        for part, (_, _, writes) in zip(self.parts, jobs):
            part.keep, part.sent = made[0], made[1]
            if writes == 3:
                part.vec = made[2]
            del made[:writes]
        self.phase += 1
        self.send()


def interleave(keep, got, s, pieces):
    size = keep.shape[1] // pieces
    outs = []
    for i in range(pieces):
        a, b = keep[:, i * size : (i + 1) * size], got[:, i * size : (i + 1) * size]
        outs += [jnp.where(s == 0, a, b), jnp.where(s == 0, b, a)]
    return outs


def on_device(
    spread, count,
    hidden_in, w_qkv, b_qv, w_o, b_o, ln1_gain, ln1_bias, w_in, b_in, w_out, b_out, ln2_gain, ln2_bias,
    seg_lengths, cotangent,
):
    row_count, half, width = hidden_in.shape
    length = 2 * half
    mine = width // 2
    heads = HEADS // 2
    ff = w_in.shape[1]
    s = lax.axis_index("seq")
    own = hidden_in.reshape(half, width)
    cot = cotangent.reshape(half, width)
    line = Line()
    call = line.call
    flat = lambda x: x.reshape(1, -1)
    rows_ff, rows_w = ff // GROUPS, width // GROUPS
    half_ff, half_w = GROUPS // 2 * rows_ff, GROUPS // 2 * rows_w
    made, sums, flats = {}, {}, {}

    def parts_of(weight):
        names = [n for n in PARTS if PARTS[n][0] == weight]
        return names, tuple(
            (PARTS[n][1], PARTS[n][2], both_cores(PARTS[n][3]) if spread else None) for n in names
        )

    def reduce(names, arrays):
        for i, name in enumerate(names):
            keep, send = arrays[2 * i], arrays[2 * i + 1]
            vec = made["table"] if name == WITH_VECTORS else None
            sums[name] = Part(keep, send, both_cores(PARTS[name][3]), vec)
        if spread:
            weight = PARTS[names[0]][0]
            sums[weight] = Sum(line, [sums[n] for n in names], count, weight)

    other = swap(own)
    own, w_mine, bias, lin = call(
        project_kernel,
        [sds((half, width), BF), sds((3, width, mine), BF), sds((8, mine), F32), sds((half, 3 * mine), F32)],
        own, w_qkv, b_qv,
        hbm=(0, 1, 2), scratch=[pltpu.VMEM(b_qv.shape, BF), pltpu.SemaphoreType.DMA((5,))],
        name="project", vmem=12,
    )
    q, k, v, kt, expo, scale, att_t, att_mine, w_o, w_in, w_out = call(
        attend_kernel,
        [sds((length, mine), BF)] * 3
        + [sds((mine, length), BF), sds((heads, length, length), BF), sds((8, length), F32)]
        + [sds((mine, length), F32), sds((length, mine), BF)]
        + [sds(w.shape, BF) for w in (w_o, w_in, w_out)],
        seg_lengths, other, w_mine, bias, lin, w_o, w_in, w_out,
        smem=(0,), hbm=(5, 6, 7), scratch=[pltpu.SemaphoreType.DMA((3,))], name="attend", vmem=16,
    )
    att_got = swap(att_mine)
    (mid_low, active, pull, normal, inverse, sum2, down_own, down_send, output, pool_part, vec_f) = call(
        forward_kernel,
        [
            sds((half, width), BF), sds((half, ff), BF), sds((half, ff), F32), sds((half, width), F32),
            sds((half, 1), F32), sds((half, width), F32), sds((half, mine), BF), sds((half, mine), BF),
            sds((half, width), BF), sds((8, width), F32), sds((8, width), F32),
        ],
        seg_lengths, own, att_mine, att_got, w_o, flat(b_o), flat(ln1_gain), flat(ln1_bias), w_in, flat(b_in),
        w_out, flat(b_out), flat(ln2_gain), flat(ln2_bias), cot,
        smem=(0,), scratch=[pltpu.VMEM((half, width), F32)], name="forward", vmem=16,
    )
    active_got = swap(active)
    mid_got = swap(mid_low)
    down_got = swap(down_send)

    def backward():
        made["up_own"], up_send, made["sum1"], branch, made["vec_b"] = call(
            backward_kernel,
            [
                sds((half, ff // 2), BF), sds((half, ff // 2), BF), sds((half, width), F32),
                sds((half, width), BF), sds((8, width), F32),
            ],
            sum2, pull, normal, inverse, flat(ln1_gain), w_in, w_out,
            scratch=[pltpu.VMEM((half, width), F32)], name="backward", vmem=12,
        )
        made["branch"] = branch, swap(branch)
        made["up_got"] = swap(up_send)

    def grad_out():
        names, parts = parts_of("out")
        outs = [sds((half_ff, stop - start), BF) for start, stop, _ in parts for _ in range(2)]
        arrays = call(
            functools.partial(grad_out_kernel, parts), outs,
            active, active_got, down_own, down_got, name="grad_out",
        )
        reduce(names, arrays)

    def grad_in():
        names, parts = parts_of("in")
        with_o = names.index(WITH_O)
        outs = []
        for i, (start, stop, _) in enumerate(parts):
            outs += [sds((half_w, stop - start + (mine if i == with_o else 0)), BF)] * 2
        arrays = call(
            functools.partial(grad_in_kernel, parts, with_o), outs,
            mid_low, mid_got, made["up_own"], made["up_got"], att_mine, att_got, *made["branch"], name="grad_in",
        )
        reduce(names, arrays)

    def attend_back():
        made["grads"], made["vec_a"] = call(
            attend_back_kernel, [sds((length, 3 * mine), BF), sds((8, mine), F32)],
            *made["branch"], w_o, q, k, v, kt, expo, scale, att_t, name="attend_back", vmem=16,
        )

    def grad_qkv():
        names, parts = parts_of("qkv")
        with_vectors = names.index(WITH_VECTORS)
        outs = []
        for i, (start, stop, _) in enumerate(parts):
            extra = vector_rows(width, stop - start) if i == with_vectors else 0
            outs += [sds((half_w, stop - start), BF), sds((half_w + extra, stop - start), BF)]
        outs.append(sds((16, width), F32))
        *arrays, made["table"] = call(
            functools.partial(grad_qkv_kernel, parts, with_vectors), outs,
            own, other, made["grads"], vec_f, made["vec_b"], made["vec_a"], name="grad_qkv",
        )
        reduce(names, arrays)

    def grad_input():
        made["keep"], made["send"] = call(
            grad_input_kernel, [sds((half, width), F32), sds((half + 8, width), F32)],
            made["grads"], w_mine, made["sum1"], pool_part, name="grad_input",
        )
        made["got"] = swap(made["send"])

    def finish_input():
        made["d_input"], made["pooled"] = call(
            finish_input_kernel, [sds((half, width), F32), sds((seg_lengths.shape[1], width), F32)],
            seg_lengths, made["keep"], made["send"], made["got"], smem=(0,), name="finish_input", end=True,
        )

    def places_of(weight, pieces):
        if weight == "o":
            _, start, stop, _ = PARTS[WITH_O]
            return [WITH_O], [(0, stop - start + c) for c in range(0, mine, 128)]
        names, parts = parts_of(weight)
        return names, [
            (i, c - start) for i, (start, stop, _) in enumerate(parts) for c in range(start, stop, 128)
        ]

    def finish_all():
        args, outs, jobs = [], [], []
        for weight, pieces in WEIGHTS.items():
            names, places = places_of(weight, pieces)
            first = len(args)
            args += [x for n in names for x in (sums[n].keep, sums[n].got)]
            outs.append(sds((2 * args[first].shape[0] * len(places), 128), F32))
            jobs.append((functools.partial(finish_kernel, pieces, places), first, len(args)))
        part = sums[WITH_VECTORS]
        one = sds((width // 128, 128), F32)
        args += [part.sent, part.got]
        outs += [sds((2, width), F32), one, one, one, sds((ff // 128, 128), F32), one, one, one]

        def kernel(*refs):
            results = refs[len(args) :]
            for job, (run, start, stop) in enumerate(jobs):
                run(*refs[start:stop], results[job])
            finish_vectors_kernel(
                part.keep.shape[0], width, refs[len(args) - 2], refs[len(args) - 1], *results[len(jobs) :]
            )

        done = call(kernel, outs, *args, name="finish", vmem=10)
        for weight, out in zip(WEIGHTS, done):
            flats[weight] = out.reshape(-1)
        made["vectors"] = done[len(jobs) :]

    work = {
        "BWD": backward, "OUT": grad_out, "IN": grad_in, "BACK": attend_back, "QKV": grad_qkv, "INPUT": grad_input,
        "input": finish_input,
    }
    for item in PLAN:
        if item in work:
            work[item]()
        elif spread:
            sums[item].step()
    if spread:
        finish_all()

    if spread:
        vectors = [v if v.shape[0] == 2 else v.reshape(-1) for v in made["vectors"]]
    else:
        for name in PARTS:
            part = sums[name]
            both = jnp.concatenate([part.keep, part.sent[: part.keep.shape[0]]], axis=0)
            total = lax.psum_scatter(both, "dp", scatter_dimension=0, tiled=True).astype(F32)
            half_rows = total.reshape(2, -1, total.shape[1])
            part.keep = jnp.where(s == 0, half_rows[0], half_rows[1])
            part.got = swap(jnp.where(s == 0, half_rows[1], half_rows[0]))
        for weight, pieces in WEIGHTS.items():
            names, places = places_of(weight, pieces)
            keep, got = (
                jnp.concatenate([getattr(sums[names[p]], k)[:, c : c + 128] for p, c in places], axis=1)
                for k in ("keep", "got")
            )
            flats[weight] = jnp.concatenate(interleave(keep, got, s, pieces), axis=1).reshape(-1)
        vec = lax.psum(made["table"], ("dp", "seq"))
        base = ff // width
        vectors = [vec[0:2]] + [vec[2 + base + i] for i in (2, 0, 1)] + [vec[2 : 2 + base].reshape(-1)]
        vectors += [vec[2 + base + i] for i in (5, 3, 4)]
    return (
        output.reshape(row_count, half, width),
        made["pooled"][None],
        made["d_input"].reshape(row_count, half, width),
        *(flats[n] for n in ("qkv", "o", "in", "out")),
        *vectors,
    )


def both_cores(letters):
    bits = {"x": 0, "y": 1, "1": 2, "2": 3}
    turned = {"x": "y", "y": "x"}
    return tuple(bits[c] for c in letters), tuple(bits[turned.get(c, c)] for c in letters)


def solution(mesh):
    count = mesh.shape["dp"]
    in_specs = (P("dp", "seq", None),) + (P(),) * 12 + (P("dp", None), P("dp", "seq", None))
    out_specs = (
        P("dp", "seq", None),
        P("dp", None, None),
        P("dp", "seq", None),
    ) + (P(("dp", "seq")),) * 4 + (P(),) * 8
    return jax.shard_map(
        functools.partial(on_device, count == GROUPS, count),
        mesh=mesh, in_specs=in_specs, out_specs=out_specs, check_vma=False,
    )
```

time: 205 us -> 101 us (0.49)
  Pallas kernels: 92.6 us -> 38.3 us
  waiting for transfers between devices: 63.1 us -> 25 us
  local copies, waits for them, and re-layouts: 23.2 us -> 0.1 us
  starting transfers between devices: 22.1 us -> 34.7 us
  other arithmetic: 2.67 us -> 0 us
    pallas_call x20 -> x23, Pallas kernels: 92.6 us -> 38.3 us  [call(): pl.pallas_call(body, out_shape=list(outs), in_specs=specs, out_specs=[pl....]
    ppermute x12 -> x20, waiting for transfers between devices: 59.5 us -> 20.5 us  [send_to(): return lax.ppermute(x, ('dp', 'seq'), pairs)]
    unnamed x71 -> x18, local copies, waits for them, and re-layouts: 15.2 us -> 0.05 us
    ppermute x12 -> x20, starting transfers between devices: 20.3 us -> 32 us  [send_to(): return lax.ppermute(x, ('dp', 'seq'), pairs)]
    reshape x11 -> x7, local copies, waits for them, and re-layouts: 6.78 us -> 0.04 us  [on_device(): flat = lambda x: x.reshape(1, -1)]
    ppermute x11 -> x13, waiting for transfers between devices: 3.58 us -> 4.47 us  [swap(): return lax.ppermute(x, axis, [(0, 1), (1, 0)])]
  transfers between devices with their start and end apart: 23 -> 33, of which waited for: 11 -> 14; matrix products, arithmetic and copies ran while one was open for 5% -> 0% of each run, Pallas kernels for 30% -> 27%
where the time goes in v2:
time: 101 us; the launch traced here: 99.2 us
  Pallas kernels  38.3 us (38%)
  starting transfers between devices  34.7 us (34%)
  waiting for transfers between devices  25 us (25%)
  between operations  1.18 us (1%)
    pallas_call x23, Pallas kernels, call(): pl.pallas_call(body, out_shape=list(outs), in_specs=specs, out_specs=[pl....  38.3 us
    ppermute x20, starting transfers between devices, send_to(): return lax.ppermute(x, ('dp', 'seq'), pairs)  32 us
    ppermute x20, waiting for transfers between devices, send_to(): return lax.ppermute(x, ('dp', 'seq'), pairs)  20.5 us
    ppermute x13, waiting for transfers between devices, swap(): return lax.ppermute(x, axis, [(0, 1), (1, 0)])  4.47 us
    ppermute x13, starting transfers between devices, swap(): return lax.ppermute(x, axis, [(0, 1), (1, 0)])  2.66 us
  transfers between devices with their start and end apart: 33, of which 14 were waited for; matrix products, arithmetic and copies ran while one was open for 0% of the time, Pallas kernels for 27%

profile of v2, /device:TPU:0, one launch (start us, length us, event | category | flops | bytes accessed | tf_op | source)
XLA Modules:
  0.0 99.2 jit_solution(9476838915225853538)
XLA Ops:
  1.2 2.6 %project.1 = (bf16[256,768]{1,0:T(8,128)(2,1)S(1)}, bf16[3,768,384]{2,1,0:T(8,128)(2,1)S(1)}, f32[8,384]{1,0:T(8,128)S(1)}, f32[256,1152]{1,0:T(8,128)S(1)}) custom-call(bf16[256,768]{1,0:T(8,128)(2,1)} %bitcast.18, bf16[768,2304]{1,0:T(8,128)(2,1)} %refs_1_.1, bf16[2,768]{1,0:T(2,128)(2,1)} %refs_2_.1), custom_call_target="tpu_custom_call" | custom-call | flops 330000000 | bytes 1024 | tf_op jit(solution)/shard_map/project/pallas_call | solution.py:78
  3.9 4.8 %attend.1 = (bf16[512,384]{1,0:T(8,128)(2,1)S(1)}, bf16[512,384]{1,0:T(8,128)(2,1)S(1)}, bf16[512,384]{1,0:T(8,128)(2,1)S(1)}, bf16[384,512]{1,0:T(8,128)(2,1)S(...) custom-call(s32[1,4]{1,0:T(1,128)S(1)} %copy-done.1, ...), custom_call_target="tpu_custom_call" | custom-call | flops 330000000 | bytes 1024 | tf_op jit(solution)/shard_map/attend/pallas_call | solution.py:78
  10.5 6.0 %forward.1 = (bf16[256,768]{1,0:T(8,128)(2,1)S(1)}, bf16[256,3072]{1,0:T(8,128)(2,1)S(1)}, f32[256,3072]{1,0:T(8,128)S(1)}, f32[256,768]{1,0:T(8,128)S(1)}, f32[...) custom-call(s32[1,4]{1,0:T(1,128)S(1)} %copy-done.1, ...), custom_call_target="tpu_custom_call" | custom-call | flops 330000000 | bytes 1024 | tf_op jit(solution)/shard_map/forward/pallas_call | solution.py:78
  17.0 3.3 %backward.1 = (bf16[256,1536]{1,0:T(8,128)(2,1)S(1)}, bf16[256,1536]{1,0:T(8,128)(2,1)S(1)}, f32[256,768]{1,0:T(8,128)S(1)}, bf16[256,768]{1,0:T(8,128)(2,1)S(1)}, f32[8,768]{1,0:T(8,128)S(1)}) custom-call(f32[256,768]{1,0:T(8,128)S(1)} %get-tuple-element.129.refs_0_, f32[256,3072]{1,0:T(8,128)S(1)} %get-tuple-element.130.refs_1_, ...), custom_call_target="tpu_custom_call" | custom-call | flops 330000000 | bytes 1024 | tf_op jit(solution)/shard_map/backward/pallas_call | solution.py:78
  20.5 3.6 %grad_out.1 = (bf16[1536,384]{1,0:T(8,128)(2,1)S(1)}, bf16[1536,384]{1,0:T(8,128)(2,1)S(1)}) custom-call(bf16[256,3072]{1,0:T(8,128)(2,1)S(1)} %get-tuple-element.143.refs_0_, bf16[256,3072]{1,0:T(8,128)(2,1)S(1)} %collective-permute-done.5.refs_1_, bf16[256,384]{1,0:T(8,128)(2,1)S(1)} %get-tuple-element.144.refs_2_, ...), custom_call_target="tpu_custom_call" | custom-call | flops 330000000 | bytes 1024 | tf_op jit(solution)/shard_map/grad_out/pallas_call | solution.py:78
  24.2 3.0 %collective-permute-start.7 = (bf16[1536,384]{1,0:T(8,128)(2,1)S(1)}, bf16[1536,384]{1,0:T(8,128)(2,1)S(1)}, u32[]{:S(2)}, u32[]{:S(2)}) collective-permute-start(bf16[1536,384]{1,0:T(8,128)(2,1)S(1)} %get-tuple-element.154), channel_id=1, source_target_pairs={{0,2},{1,5},{2,0},{3,7},{4,6},{5,1},{6,4},{7,3},{8,10},{9,13},{10,... | collective-permute-start | bytes 3538952 | tf_op jit(solution)/shard_map/ppermute | solution.py:590
  29.4 5.2 %grad_in.1 = (bf16[384,768]{1,0:T(8,128)(2,1)S(1)}, bf16[384,768]{1,0:T(8,128)(2,1)S(1)}, bf16[384,1152]{1,0:T(8,128)(2,1)S(1)}, bf16[384,1152]{1,0:T(8,128)(2,1)S(1)}) custom-call(bf16[256,768]{1,0:T(8,128)(2,1)S(1)} %get-tuple-element.133.refs_7_.refs_0_, bf16[256,768]{1,0:T(8,128)(2,1)S(1)} %collective-permute-done.3.refs_1_, ...), custom_call_target="tpu_custom_call" | custom-call | flops 330000000 | bytes 1024 | tf_op jit(solution)/shard_map/grad_in/pallas_call | solution.py:78
  34.7 1.6 %collective-permute-start.13 = (bf16[384,1152]{1,0:T(8,128)(2,1)S(1)}, bf16[384,1152]{1,0:T(8,128)(2,1)S(1)}, u32[]{:S(2)}, u32[]{:S(2)}) collective-permute-start(bf16[384,1152]{1,0:T(8,128)(2,1)S(1)} %get-tuple-element.165), channel_id=1, source_target_pairs={{0,8},{1,9},{2,10},{3,11},{4,12},{5,13},{6,14},{7,15},{8,0},{9,1},... | collective-permute-start | bytes 2654216 | tf_op jit(solution)/shard_map/ppermute | solution.py:590
  37.3 3.6 %attend_back.1 = (bf16[512,1152]{1,0:T(8,128)(2,1)S(1)}, f32[8,384]{1,0:T(8,128)S(1)}) custom-call(bf16[256,768]{1,0:T(8,128)(2,1)S(1)} %get-tuple-element.134.refs_6_.refs_0_, bf16[256,768]{1,0:T(8,128)(2,1)S(1)} %collective-permute-done.2.refs_7_.refs_1_, bf16[768,768]{1,0:T(8,128)(2,1)S(1)} %get-tuple-element.124.refs_4_.refs_2_, ...), custom_call_target="tpu_custom_call" | custom-call | flops 330000000 | bytes 1024 | tf_op jit(solution)/shard_map/attend_back/pallas_call | solution.py:78
  41.6 2.1 %collective-permute-start.11 = (bf16[768,384]{1,0:T(8,128)(2,1)S(1)}, bf16[768,384]{1,0:T(8,128)(2,1)S(1)}, u32[]{:S(2)}, u32[]{:S(2)}) collective-permute-start(bf16[768,384]{1,0:T(8,128)(2,1)S(1)} %get-tuple-element.163), channel_id=1, source_target_pairs={{0,4},{1,3},{2,6},{3,1},{4,0},{5,7},{6,2},{7,5},{8,12},{9,11},{10,... | collective-permute-start | bytes 1769480 | tf_op jit(solution)/shard_map/ppermute | solution.py:590
  43.7 3.4 %grad_qkv.1 = (bf16[384,384]{1,0:T(8,128)(2,1)S(1)}, bf16[448,384]{1,0:T(8,128)(2,1)S(1)}, bf16[384,768]{1,0:T(8,128)(2,1)S(1)}, bf16[384,768]{1,0:T(8,128)(2,1)S(1)}, f32[16,768]{1,0:T(8,128)S(1)}) custom-call(bf16[256,768]{1,0:T(8,128)(2,1)S(1)} %get-tuple-element.119.refs_8_.refs_1_.refs_0_, bf16[256,768]{1,0:T(8,128)(2,1)S(1)} %collective-permute-done.refs_1_, ...), custom_call_target="tpu_custom_call" | custom-call | flops 330000000 | bytes 1024 | tf_op jit(solution)/shard_map/grad_qkv/pallas_call | solution.py:78
  49.2 2.1 %collective-permute-done.12.refs_0_ = bf16[384,768]{1,0:T(8,128)(2,1)S(1)} collective-permute-done((bf16[384,768]{1,0:T(8,128)(2,1)S(1)}, bf16[384,768]{1,0:T(8,128)(2,1)S(1)}, u32[]{:S(2)}, u32[]{:S(2)}) %collective-permute-start.12) | collective-permute-done | bytes 589856 | tf_op jit(solution)/shard_map/ppermute | solution.py:590
  51.3 2.5 %collective-permute-start.9 = (bf16[448,384]{1,0:T(8,128)(2,1)S(1)}, bf16[448,384]{1,0:T(8,128)(2,1)S(1)}, u32[]{:S(2)}, u32[]{:S(2)}) collective-permute-start(bf16[448,384]{1,0:T(8,128)(2,1)S(1)} %get-tuple-element.159), channel_id=1, source_target_pairs={{0,8},{1,9},{2,10},{3,11},{4,12},{5,13},{6,14},{7,15},{8,0},{9,1},... | collective-permute-start | bytes 1032200 | tf_op jit(solution)/shard_map/ppermute | solution.py:590
  53.8 3.4 %collective-permute-done.13.refs_2_ = bf16[384,1152]{1,0:T(8,128)(2,1)S(1)} collective-permute-done((bf16[384,1152]{1,0:T(8,128)(2,1)S(1)}, bf16[384,1152]{1,0:T(8,128)(2,1)S(1)}, u32[]{:S(2)}, u32[]{:S(2)}) %collective-permute-start.13) | collective-permute-done | bytes 884768 | tf_op jit(solution)/shard_map/ppermute | solution.py:590
  59.8 4.0 %collective-permute-done.9.refs_0_ = bf16[448,384]{1,0:T(8,128)(2,1)S(1)} collective-permute-done((bf16[448,384]{1,0:T(8,128)(2,1)S(1)}, bf16[448,384]{1,0:T(8,128)(2,1)S(1)}, u32[]{:S(2)}, u32[]{:S(2)}) %collective-permute-start.9) | collective-permute-done | bytes 344096 | tf_op jit(solution)/shard_map/ppermute | solution.py:590
  63.8 1.6 %collective-permute-start.14 = (bf16[384,384]{1,0:T(8,128)(2,1)S(1)}, bf16[384,384]{1,0:T(8,128)(2,1)S(1)}, u32[]{:S(2)}, u32[]{:S(2)}) collective-permute-start(bf16[384,384]{1,0:T(8,128)(2,1)S(1)} %get-tuple-element.172), channel_id=1, source_target_pairs={{0,8},{1,9},{2,10},{3,11},{4,12},{5,13},{6,14},{7,15},{8,0},{9,1},... | collective-permute-start | bytes 884744 | tf_op jit(solution)/shard_map/ppermute | solution.py:590
  66.9 2.6 %collective-permute-start.20 = (bf16[256,384]{1,0:T(8,128)(2,1)S(1)}, bf16[256,384]{1,0:T(8,128)(2,1)S(1)}, u32[]{:S(2)}, u32[]{:S(2)}) collective-permute-start(bf16[256,384]{1,0:T(8,128)(2,1)S(1)} %get-tuple-element.183), channel_id=1, source_target_pairs={{0,16},{1,17},{2,18},{3,19},{4,20},{5,21},{6,22},{7,23},{8,24},{9,... | collective-permute-start | bytes 589832 | tf_op jit(solution)/shard_map/ppermute | solution.py:590
  72.5 5.5 %collective-permute-done.14.refs_0_ = bf16[384,384]{1,0:T(8,128)(2,1)S(1)} collective-permute-done((bf16[384,384]{1,0:T(8,128)(2,1)S(1)}, bf16[384,384]{1,0:T(8,128)(2,1)S(1)}, u32[]{:S(2)}, u32[]{:S(2)}) %collective-permute-start.14) | collective-permute-done | bytes 294944 | tf_op jit(solution)/shard_map/ppermute | solution.py:590
  78.0 1.7 %collective-permute-start.17 = (bf16[192,384]{1,0:T(8,128)(2,1)S(1)}, bf16[192,384]{1,0:T(8,128)(2,1)S(1)}, u32[]{:S(2)}, u32[]{:S(2)}) collective-permute-start(bf16[192,384]{1,0:T(8,128)(2,1)S(1)} %get-tuple-element.178), channel_id=1, source_target_pairs={{0,16},{1,17},{2,18},{3,19},{4,20},{5,21},{6,22},{7,23},{8,24},{9,... | collective-permute-start | bytes 442376 | tf_op jit(solution)/shard_map/ppermute | solution.py:590
  79.9 2.8 %collective-permute-start.26 = (bf16[96,768]{1,0:T(8,128)(2,1)S(1)}, bf16[96,768]{1,0:T(8,128)(2,1)S(1)}, u32[]{:S(2)}, u32[]{:S(2)}) collective-permute-start(bf16[96,768]{1,0:T(8,128)(2,1)S(1)} %get-tuple-element.196), channel_id=1, source_target_pairs={{0,8},{1,9},{2,10},{3,11},{4,12},{5,13},{6,14},{7,15},{8,0},{9,1},... | collective-permute-start | bytes 442376 | tf_op jit(solution)/shard_map/ppermute | solution.py:590
  83.8 1.6 %collective-permute-start.23 = (bf16[48,768]{1,0:T(8,128)(2,1)S(1)}, bf16[48,768]{1,0:T(8,128)(2,1)S(1)}, u32[]{:S(2)}, u32[]{:S(2)}) collective-permute-start(bf16[48,768]{1,0:T(8,128)(2,1)S(1)} %get-tuple-element.191), channel_id=1, source_target_pairs={{0,16},{1,17},{2,18},{3,19},{4,20},{5,21},{6,22},{7,23},{8,24},{9,... | collective-permute-start | bytes 221192 | tf_op jit(solution)/shard_map/ppermute | solution.py:590
  88.0 2.7 %collective-permute-start.29 = (bf16[112,384]{1,0:T(8,128)(2,1)S(1)}, bf16[112,384]{1,0:T(8,128)(2,1)S(1)}, u32[]{:S(2)}, u32[]{:S(2)}) collective-permute-start(bf16[112,384]{1,0:T(8,128)(2,1)S(1)} %get-tuple-element.203), channel_id=1, source_target_pairs={{0,4},{1,3},{2,6},{3,1},{4,0},{5,7},{6,2},{7,5},{8,12},{9,11},{10,... | collective-permute-start | bytes 258056 | tf_op jit(solution)/shard_map/ppermute | solution.py:590
  91.8 1.5 %collective-permute-done.23.refs_0_ = bf16[48,768]{1,0:T(8,128)(2,1)S(1)} collective-permute-done((bf16[48,768]{1,0:T(8,128)(2,1)S(1)}, bf16[48,768]{1,0:T(8,128)(2,1)S(1)}, u32[]{:S(2)}, u32[]{:S(2)}) %collective-permute-start.23) | collective-permute-done | bytes 73760 | tf_op jit(solution)/shard_map/ppermute | solution.py:590
  93.4 2.0 %collective-permute-done.24.refs_2_ = bf16[48,1152]{1,0:T(8,128)(2,1)S(1)} collective-permute-done((bf16[48,1152]{1,0:T(8,128)(2,1)S(1)}, bf16[48,1152]{1,0:T(8,128)(2,1)S(1)}, u32[]{:S(2)}, u32[]{:S(2)}) %collective-permute-start.24) | collective-permute-done | bytes 110624 | tf_op jit(solution)/shard_map/ppermute | solution.py:590
  (90 shorter events, 24.9 us)
Async XLA Ops:
  16.5 4.0 %collective-permute-start.5 = (bf16[256,3072]{1,0:T(8,128)(2,1)S(1)}, bf16[256,3072]{1,0:T(8,128)(2,1)S(1)}, u32[]{:S(2)}, u32[]{:S(2)}) collective-permute-start(bf16[256,3072]{1,0:T(8,128)(2,1)S(1)} %get-tuple-element.143.refs_0_), channel_id=1, source_target_pairs={{0,1},{1,0},{2,3},{3,2},{4,5},{5,4},{6,7},{7,6},{8,9},{9,8},{10,11... | collective-permute-start | bytes 4718600 | tf_op jit(solution)/shard_map/ppermute | solution.py:582
  20.3 9.1 %collective-permute-start.4 = (bf16[256,1536]{1,0:T(8,128)(2,1)S(1)}, bf16[256,1536]{1,0:T(8,128)(2,1)S(1)}, u32[]{:S(2)}, u32[]{:S(2)}) collective-permute-start(bf16[256,1536]{1,0:T(8,128)(2,1)S(1)} %get-tuple-element.142), channel_id=1, source_target_pairs={{0,1},{1,0},{2,3},{3,2},{4,5},{5,4},{6,7},{7,6},{8,9},{9,8},{10,11... | collective-permute-start | bytes 2359304 | tf_op jit(solution)/shard_map/ppermute | solution.py:582
  24.2 17.1 %collective-permute-start.7 = (bf16[1536,384]{1,0:T(8,128)(2,1)S(1)}, bf16[1536,384]{1,0:T(8,128)(2,1)S(1)}, u32[]{:S(2)}, u32[]{:S(2)}) collective-permute-start(bf16[1536,384]{1,0:T(8,128)(2,1)S(1)} %get-tuple-element.154), channel_id=1, source_target_pairs={{0,2},{1,5},{2,0},{3,7},{4,6},{5,1},{6,4},{7,3},{8,10},{9,13},{10,... | collective-permute-start | bytes 3538952 | tf_op jit(solution)/shard_map/ppermute | solution.py:590
  34.7 22.6 %collective-permute-start.13 = (bf16[384,1152]{1,0:T(8,128)(2,1)S(1)}, bf16[384,1152]{1,0:T(8,128)(2,1)S(1)}, u32[]{:S(2)}, u32[]{:S(2)}) collective-permute-start(bf16[384,1152]{1,0:T(8,128)(2,1)S(1)} %get-tuple-element.165), channel_id=1, source_target_pairs={{0,8},{1,9},{2,10},{3,11},{4,12},{5,13},{6,14},{7,15},{8,0},{9,1},... | collective-permute-start | bytes 2654216 | tf_op jit(solution)/shard_map/ppermute | solution.py:590
  36.3 15.0 %collective-permute-start.12 = (bf16[384,768]{1,0:T(8,128)(2,1)S(1)}, bf16[384,768]{1,0:T(8,128)(2,1)S(1)}, u32[]{:S(2)}, u32[]{:S(2)}) collective-permute-start(bf16[384,768]{1,0:T(8,128)(2,1)S(1)} %get-tuple-element.164), channel_id=1, source_target_pairs={{0,2},{1,5},{2,0},{3,7},{4,6},{5,1},{6,4},{7,3},{8,10},{9,13},{10,... | collective-permute-start | bytes 1769480 | tf_op jit(solution)/shard_map/ppermute | solution.py:590
  41.6 17.0 %collective-permute-start.11 = (bf16[768,384]{1,0:T(8,128)(2,1)S(1)}, bf16[768,384]{1,0:T(8,128)(2,1)S(1)}, u32[]{:S(2)}, u32[]{:S(2)}) collective-permute-start(bf16[768,384]{1,0:T(8,128)(2,1)S(1)} %get-tuple-element.163), channel_id=1, source_target_pairs={{0,4},{1,3},{2,6},{3,1},{4,0},{5,7},{6,2},{7,5},{8,12},{9,11},{10,... | collective-permute-start | bytes 1769480 | tf_op jit(solution)/shard_map/ppermute | solution.py:590
  48.6 18.3 %collective-permute-start.8 = (f32[264,768]{1,0:T(8,128)S(1)}, f32[264,768]{1,0:T(8,128)S(1)}, u32[]{:S(2)}, u32[]{:S(2)}) collective-permute-start(f32[264,768]{1,0:T(8,128)S(1)} %get-tuple-element.158.refs_2_), channel_id=1, source_target_pairs={{0,1},{1,0},{2,3},{3,2},{4,5},{5,4},{6,7},{7,6},{8,9},{9,8},{10,11... | collective-permute-start | bytes 2433032 | tf_op jit(solution)/shard_map/ppermute | solution.py:582
  48.7 16.7 %collective-permute-start.10 = (bf16[384,768]{1,0:T(8,128)(2,1)S(1)}, bf16[384,768]{1,0:T(8,128)(2,1)S(1)}, u32[]{:S(2)}, u32[]{:S(2)}) collective-permute-start(bf16[384,768]{1,0:T(8,128)(2,1)S(1)} %get-tuple-element.161), channel_id=1, source_target_pairs={{0,4},{1,3},{2,6},{3,1},{4,0},{5,7},{6,2},{7,5},{8,12},{9,11},{10,... | collective-permute-start | bytes 1769480 | tf_op jit(solution)/shard_map/ppermute | solution.py:590
  51.3 12.5 %collective-permute-start.9 = (bf16[448,384]{1,0:T(8,128)(2,1)S(1)}, bf16[448,384]{1,0:T(8,128)(2,1)S(1)}, u32[]{:S(2)}, u32[]{:S(2)}) collective-permute-start(bf16[448,384]{1,0:T(8,128)(2,1)S(1)} %get-tuple-element.159), channel_id=1, source_target_pairs={{0,8},{1,9},{2,10},{3,11},{4,12},{5,13},{6,14},{7,15},{8,0},{9,1},... | collective-permute-start | bytes 1032200 | tf_op jit(solution)/shard_map/ppermute | solution.py:590
  57.6 13.5 %collective-permute-start.16 = (bf16[192,1152]{1,0:T(8,128)(2,1)S(1)}, bf16[192,1152]{1,0:T(8,128)(2,1)S(1)}, u32[]{:S(2)}, u32[]{:S(2)}) collective-permute-start(bf16[192,1152]{1,0:T(8,128)(2,1)S(1)} %get-tuple-element.174), channel_id=1, source_target_pairs={{0,2},{1,5},{2,0},{3,7},{4,6},{5,1},{6,4},{7,3},{8,10},{9,13},{10,... | collective-permute-start | bytes 1327112 | tf_op jit(solution)/shard_map/ppermute | solution.py:590
  58.6 12.4 %collective-permute-start.15 = (bf16[192,768]{1,0:T(8,128)(2,1)S(1)}, bf16[192,768]{1,0:T(8,128)(2,1)S(1)}, u32[]{:S(2)}, u32[]{:S(2)}) collective-permute-start(bf16[192,768]{1,0:T(8,128)(2,1)S(1)} %get-tuple-element.173), channel_id=1, source_target_pairs={{0,4},{1,3},{2,6},{3,1},{4,0},{5,7},{6,2},{7,5},{8,12},{9,11},{10,... | collective-permute-start | bytes 884744 | tf_op jit(solution)/shard_map/ppermute | solution.py:590
  63.8 14.2 %collective-permute-start.14 = (bf16[384,384]{1,0:T(8,128)(2,1)S(1)}, bf16[384,384]{1,0:T(8,128)(2,1)S(1)}, u32[]{:S(2)}, u32[]{:S(2)}) collective-permute-start(bf16[384,384]{1,0:T(8,128)(2,1)S(1)} %get-tuple-element.172), channel_id=1, source_target_pairs={{0,8},{1,9},{2,10},{3,11},{4,12},{5,13},{6,14},{7,15},{8,0},{9,1},... | collective-permute-start | bytes 884744 | tf_op jit(solution)/shard_map/ppermute | solution.py:590
  65.6 14.2 %collective-permute-start.21 = (bf16[192,768]{1,0:T(8,128)(2,1)S(1)}, bf16[192,768]{1,0:T(8,128)(2,1)S(1)}, u32[]{:S(2)}, u32[]{:S(2)}) collective-permute-start(bf16[192,768]{1,0:T(8,128)(2,1)S(1)} %get-tuple-element.185), channel_id=1, source_target_pairs={{0,2},{1,5},{2,0},{3,7},{4,6},{5,1},{6,4},{7,3},{8,10},{9,13},{10,... | collective-permute-start | bytes 884744 | tf_op jit(solution)/shard_map/ppermute | solution.py:590
  66.9 12.8 %collective-permute-start.20 = (bf16[256,384]{1,0:T(8,128)(2,1)S(1)}, bf16[256,384]{1,0:T(8,128)(2,1)S(1)}, u32[]{:S(2)}, u32[]{:S(2)}) collective-permute-start(bf16[256,384]{1,0:T(8,128)(2,1)S(1)} %get-tuple-element.183), channel_id=1, source_target_pairs={{0,16},{1,17},{2,18},{3,19},{4,20},{5,21},{6,22},{7,23},{8,24},{9,... | collective-permute-start | bytes 589832 | tf_op jit(solution)/shard_map/ppermute | solution.py:590
  71.2 12.5 %collective-permute-start.19 = (bf16[96,1152]{1,0:T(8,128)(2,1)S(1)}, bf16[96,1152]{1,0:T(8,128)(2,1)S(1)}, u32[]{:S(2)}, u32[]{:S(2)}) collective-permute-start(bf16[96,1152]{1,0:T(8,128)(2,1)S(1)} %get-tuple-element.181), channel_id=1, source_target_pairs={{0,4},{1,3},{2,6},{3,1},{4,0},{5,7},{6,2},{7,5},{8,12},{9,11},{10,... | collective-permute-start | bytes 663560 | tf_op jit(solution)/shard_map/ppermute | solution.py:590
  72.1 11.7 %collective-permute-start.18 = (bf16[96,768]{1,0:T(8,128)(2,1)S(1)}, bf16[96,768]{1,0:T(8,128)(2,1)S(1)}, u32[]{:S(2)}, u32[]{:S(2)}) collective-permute-start(bf16[96,768]{1,0:T(8,128)(2,1)S(1)} %get-tuple-element.180), channel_id=1, source_target_pairs={{0,8},{1,9},{2,10},{3,11},{4,12},{5,13},{6,14},{7,15},{8,0},{9,1},... | collective-permute-start | bytes 442376 | tf_op jit(solution)/shard_map/ppermute | solution.py:590
  78.0 9.7 %collective-permute-start.17 = (bf16[192,384]{1,0:T(8,128)(2,1)S(1)}, bf16[192,384]{1,0:T(8,128)(2,1)S(1)}, u32[]{:S(2)}, u32[]{:S(2)}) collective-permute-start(bf16[192,384]{1,0:T(8,128)(2,1)S(1)} %get-tuple-element.178), channel_id=1, source_target_pairs={{0,16},{1,17},{2,18},{3,19},{4,20},{5,21},{6,22},{7,23},{8,24},{9,... | collective-permute-start | bytes 442376 | tf_op jit(solution)/shard_map/ppermute | solution.py:590
  79.9 8.0 %collective-permute-start.26 = (bf16[96,768]{1,0:T(8,128)(2,1)S(1)}, bf16[96,768]{1,0:T(8,128)(2,1)S(1)}, u32[]{:S(2)}, u32[]{:S(2)}) collective-permute-start(bf16[96,768]{1,0:T(8,128)(2,1)S(1)} %get-tuple-element.196), channel_id=1, source_target_pairs={{0,8},{1,9},{2,10},{3,11},{4,12},{5,13},{6,14},{7,15},{8,0},{9,1},... | collective-permute-start | bytes 442376 | tf_op jit(solution)/shard_map/ppermute | solution.py:590
  82.7 5.2 %collective-permute-start.25 = (bf16[160,384]{1,0:T(8,128)(2,1)S(1)}, bf16[160,384]{1,0:T(8,128)(2,1)S(1)}, u32[]{:S(2)}, u32[]{:S(2)}) collective-permute-start(bf16[160,384]{1,0:T(8,128)(2,1)S(1)} %get-tuple-element.194), channel_id=1, source_target_pairs={{0,2},{1,5},{2,0},{3,7},{4,6},{5,1},{6,4},{7,3},{8,10},{9,13},{10,... | collective-permute-start | bytes 368648 | tf_op jit(solution)/shard_map/ppermute | solution.py:590
  83.8 9.6 %collective-permute-start.23 = (bf16[48,768]{1,0:T(8,128)(2,1)S(1)}, bf16[48,768]{1,0:T(8,128)(2,1)S(1)}, u32[]{:S(2)}, u32[]{:S(2)}) collective-permute-start(bf16[48,768]{1,0:T(8,128)(2,1)S(1)} %get-tuple-element.191), channel_id=1, source_target_pairs={{0,16},{1,17},{2,18},{3,19},{4,20},{5,21},{6,22},{7,23},{8,24},{9,... | collective-permute-start | bytes 221192 | tf_op jit(solution)/shard_map/ppermute | solution.py:590
  85.4 9.9 %collective-permute-start.24 = (bf16[48,1152]{1,0:T(8,128)(2,1)S(1)}, bf16[48,1152]{1,0:T(8,128)(2,1)S(1)}, u32[]{:S(2)}, u32[]{:S(2)}) collective-permute-start(bf16[48,1152]{1,0:T(8,128)(2,1)S(1)} %get-tuple-element.192), channel_id=1, source_target_pairs={{0,16},{1,17},{2,18},{3,19},{4,20},{5,21},{6,22},{7,23},{8,24},{9,... | collective-permute-start | bytes 331784 | tf_op jit(solution)/shard_map/ppermute | solution.py:590
  88.0 8.2 %collective-permute-start.29 = (bf16[112,384]{1,0:T(8,128)(2,1)S(1)}, bf16[112,384]{1,0:T(8,128)(2,1)S(1)}, u32[]{:S(2)}, u32[]{:S(2)}) collective-permute-start(bf16[112,384]{1,0:T(8,128)(2,1)S(1)} %get-tuple-element.203), channel_id=1, source_target_pairs={{0,4},{1,3},{2,6},{3,1},{4,0},{5,7},{6,2},{7,5},{8,12},{9,11},{10,... | collective-permute-start | bytes 258056 | tf_op jit(solution)/shard_map/ppermute | solution.py:590
  90.6 5.5 %collective-permute-start.30 = (bf16[48,768]{1,0:T(8,128)(2,1)S(1)}, bf16[48,768]{1,0:T(8,128)(2,1)S(1)}, u32[]{:S(2)}, u32[]{:S(2)}) collective-permute-start(bf16[48,768]{1,0:T(8,128)(2,1)S(1)} %get-tuple-element.205), channel_id=1, source_target_pairs={{0,16},{1,17},{2,18},{3,19},{4,20},{5,21},{6,22},{7,23},{8,24},{9,... | collective-permute-start | bytes 221192 | tf_op jit(solution)/shard_map/ppermute | solution.py:590
  91.8 5.0 %collective-permute-start.22 = (f32[96,384]{1,0:T(8,128)S(1)}, f32[96,384]{1,0:T(8,128)S(1)}, u32[]{:S(2)}, u32[]{:S(2)}) collective-permute-start(f32[96,384]{1,0:T(8,128)S(1)} %get-tuple-element.190), channel_id=1, source_target_pairs={{0,1},{1,0},{2,3},{3,2},{4,5},{5,4},{6,7},{7,6},{8,9},{9,8},{10,11... | collective-permute-start | bytes 442376 | tf_op jit(solution)/shard_map/ppermute | solution.py:582
  (18 other events, 65.2 us)

commit v3 on v2

--- a/solution.py
+++ b/solution.py
@@ -15,21 +15,21 @@
 BF = jnp.bfloat16
 F32 = jnp.float32
 MIB = 2**20
-MERGE_US = 0.3
-KERNEL_US = 0.3
+PIECES = 1
+MERGE_US = 1.0
+KERNEL_US = 1.0
 WEIGHTS = {"out": 1, "in": 1, "qkv": 3, "o": 1}
 PARTS = {
-    "a": ("out", 0, 384, "xy12"),
-    "b": ("in", 0, 768, "xy12"),
-    "c": ("in", 768, 1536, "1xy2"),
-    "d": ("qkv", 0, 384, "12xy"),
-    "e": ("qkv", 384, 1152, "yx12"),
+    "a": ("out", 0, 384, "y1x2", "12xy"),
+    "b": ("in", 0, 1024, "y1x2", "xy12"),
+    "c": ("in", 1024, 1536, "1yx2", "yx21"),
+    "d": ("qkv", 0, 1152, "x2y1", "xy12"),
 }
 WITH_O = "c"
 WITH_VECTORS = "d"
 PLAN = (
-    "BWD", "OUT", "IN", "BACK", "out", "QKV", "INPUT", "in", "out", "qkv", "input", "in",
-    "out", "qkv", "in", "out", "qkv", "in", "qkv",
+    "BWD", "OUT", "BACK", "QKV", "IN", "INPUT", "out", "qkv", "in", "input", "out", "qkv",
+    "in", "out", "qkv", "in", "out", "qkv", "in",
 )
 
 
@@ -121,18 +121,29 @@
     return jnp.sum(matrix, axis=0, keepdims=True)
 
 
+def copies_of(source, target, sems, first, pieces):
+    rows = target.shape[0] // pieces
+    return [
+        pltpu.make_async_copy(
+            source.at[i * rows : (i + 1) * rows, :], target.at[i * rows : (i + 1) * rows, :], sems.at[first + i]
+        )
+        for i in range(pieces)
+    ]
+
+
 def project_kernel(own_hbm, w_hbm, b_hbm, own, w_mine, bias, lin, b_buf, sems):
     width = own.shape[1]
     mine = width // 2
     s = lax.axis_index("seq")
-    first = pltpu.make_async_copy(own_hbm, own, sems.at[3])
+    first = pltpu.make_async_copy(own_hbm, own, sems.at[3 * PIECES])
     first.start()
     copies = []
     for c in range(3):
         start = pl.multiple_of(c * width + s * mine, 128)
-        copies.append(pltpu.make_async_copy(w_hbm.at[:, pl.ds(start, mine)], w_mine.at[c], sems.at[c]))
-        copies[-1].start()
-    second = pltpu.make_async_copy(b_hbm, b_buf, sems.at[4])
+        copies.append(copies_of(w_hbm.at[:, pl.ds(start, mine)], w_mine.at[c], sems, c * PIECES, PIECES))
+        for copy in copies[-1]:
+            copy.start()
+    second = pltpu.make_async_copy(b_hbm, b_buf, sems.at[3 * PIECES + 1])
     second.start()
     second.wait()
     column = pl.ds(pl.multiple_of(s * mine, 128), mine)
@@ -141,7 +152,8 @@
     bias[2:3, :] = b_buf[1:2, column].astype(F32)
     first.wait()
     for c in range(3):
-        copies[c].wait()
+        for copy in copies[c]:
+            copy.wait()
         lin[:, c * mine : (c + 1) * mine] = nn(own[...], w_mine[c]) + bias[c : c + 1, :]
 
 
@@ -155,10 +167,9 @@
     pair = 2 * (width // HEADS)
     head = pair // 2
     s = lax.axis_index("seq")
-    copies = [
-        pltpu.make_async_copy(source, target, sems.at[i])
-        for i, (source, target) in enumerate(((w_o_hbm, w_o), (w_in_hbm, w_in), (w_out_hbm, w_out)))
-    ]
+    copies = []
+    for source, target in ((w_o_hbm, w_o), (w_in_hbm, w_in), (w_out_hbm, w_out)):
+        copies += copies_of(source, target, sems, len(copies), PIECES)
     for copy in copies:
         copy.start()
     parts = []
@@ -351,7 +362,7 @@
             dk.append(nn(raw, q2))
             dv.append(nt(low, a2))
             dq.append(nn(kt[h * head : (h + 1) * head, :], raw))
-        dq_low = (jnp.concatenate(dq, axis=0) * (1.0 / math.sqrt(head))).T.astype(BF)
+        dq_low = (jnp.concatenate(dq, axis=0) * (1.0 / math.sqrt(head))).astype(BF).T
         dk_low = jnp.where(first, dk[0], dk[1]).astype(BF)
         dv_low = jnp.where(first, dv[0], dv[1]).astype(BF)
         grad_out[:, cols] = dq_low
@@ -361,87 +372,63 @@
         vec_out[1:2, cols] = column_sum(dv_low.astype(F32))
 
 
-def slot_of(chunk, order):
+def chunk_of(slot, order):
     if order is None:
-        return jnp.int32(chunk)
-    rel = jnp.bitwise_xor(jnp.int32(chunk), lax.axis_index("dp"))
-    s = lax.axis_index("seq")
-    slots = []
+        return slot
+    chunks = []
     for bits in order:
-        slot = jnp.int32(0)
-        for bit in bits:
-            slot = slot * 2 + jnp.bitwise_and(lax.shift_right_logical(rel, jnp.int32(bit)), 1)
-        slots.append(slot)
-    return jnp.where(s == 0, slots[0], slots[1])
-
-
-def place(values, chunk, order, keep, send, cols=None):
-    half = GROUPS // 2
-    slot = slot_of(chunk, order)
-    rows = values.shape[0]
-    if cols is None:
-        cols = slice(0, values.shape[1])
-
-    def at(index):
-        return pl.ds(pl.multiple_of(index * rows, 16), rows)
-
-    @pl.when(slot < half)
-    def _():
-        keep[at(slot), cols] = values
-
-    @pl.when(slot >= half)
-    def _():
-        send[at(slot - half), cols] = values
+        rel = 0
+        for i, bit in enumerate(bits):
+            rel |= (slot >> (len(bits) - 1 - i) & 1) << bit
+        chunks.append(rel)
+    rel = jnp.where(lax.axis_index("seq") == 0, jnp.int32(chunks[0]), jnp.int32(chunks[1]))
+    return jnp.bitwise_xor(rel, lax.axis_index("dp"))
+
+
+def spread_rows(whole, order, keep, send, cols, to):
+    rows = whole.shape[0] // GROUPS
+    for slot in range(GROUPS):
+        chunk = chunk_of(slot, order)
+        target = keep if slot < GROUPS // 2 else send
+        place = slot % (GROUPS // 2) * rows
+        target[place : place + rows, to] = whole[pl.ds(pl.multiple_of(chunk * rows, 16), rows), cols]
 
 
 def grad_out_kernel(parts, active_own, active_got, down_own, down_got, *outs):
-    ff = active_own.shape[1]
-    rows = ff // GROUPS
-    block = 2 * rows
-    for i in range(GROUPS // 2):
-        cols = slice(i * block, (i + 1) * block)
-        got = (
+    *outs, whole = outs
+    block = 512
+    for i in range(0, active_own.shape[1], block):
+        cols = slice(i, i + block)
+        whole[cols, :] = (
             tn(active_own[:, cols], down_own[...]) + tn(active_got[:, cols], down_got[...])
         ).astype(BF)
-        for b in range(2):
-            for p, (start, stop, order) in enumerate(parts):
-                values = got[b * rows : (b + 1) * rows, start:stop]
-                place(values, 2 * i + b, order, outs[2 * p], outs[2 * p + 1])
+    for p, (start, stop, order) in enumerate(parts):
+        spread_rows(whole, order, outs[2 * p], outs[2 * p + 1], slice(start, stop), slice(0, stop - start))
 
 
 def grad_in_kernel(
     parts, with_o, mid_own, mid_got, up_own, up_got, att_mine, att_got, branch_own, branch_got, *outs
 ):
+    *outs, whole, whole_o = outs
     half, width = mid_own.shape
     mine = width // 2
-    rows = width // GROUPS
     for i in range(2):
         cols = slice(i * mine, (i + 1) * mine)
-        for p, (start, stop, order) in enumerate(parts):
-            for n in range(start, stop, 512):
-                out = slice(n, min(n + 512, stop))
-                got = (
-                    tn(mid_own[:, cols], up_own[:, out]) + tn(mid_got[:, cols], up_got[:, out])
-                ).astype(BF)
-                to = slice(n - start, out.stop - start)
-                for b in range(GROUPS // 2):
-                    place(
-                        got[b * rows : (b + 1) * rows, :], i * (GROUPS // 2) + b, order,
-                        outs[2 * p], outs[2 * p + 1], to,
-                    )
+        own_t, got_t = mid_own[:, cols].T, mid_got[:, cols].T
+        for n in range(0, up_own.shape[1], 512):
+            out = slice(n, n + 512)
+            whole[cols, out] = (nn(own_t, up_own[:, out]) + nn(got_t, up_got[:, out])).astype(BF)
     s = lax.axis_index("seq")
     column = pl.ds(pl.multiple_of(s * mine, 128), mine)
     mine_o = tn(att_mine[0:half, :], branch_own[:, column]) + tn(att_mine[half:, :], branch_got[:, column])
     got_o = tn(att_got[half:, :], branch_own[:, column]) + tn(att_got[0:half, :], branch_got[:, column])
-    start, stop, order = parts[with_o]
-    to = slice(stop - start, stop - start + mine)
     for i in range(2):
-        got = jnp.where(s == i, mine_o, got_o).astype(BF)
-        for b in range(GROUPS // 2):
-            place(
-                got[b * rows : (b + 1) * rows, :], i * (GROUPS // 2) + b, order,
-                outs[2 * with_o], outs[2 * with_o + 1], to,
-            )
+        whole_o[i * mine : (i + 1) * mine, :] = jnp.where(s == i, mine_o, got_o).astype(BF)
+    for p, (start, stop, order) in enumerate(parts):
+        spread_rows(whole, order, outs[2 * p], outs[2 * p + 1], slice(start, stop), slice(0, stop - start))
+        if p == with_o:
+            to = slice(stop - start, stop - start + mine)
+            spread_rows(whole_o, order, outs[2 * p], outs[2 * p + 1], slice(0, mine), to)
 
 
 def pack_vectors(table, send, start):
@@ -468,24 +455,19 @@
 
 
 def grad_qkv_kernel(parts, with_vectors, own, other, grads, vec_f, vec_b, vec_a, *outs):
+    *outs, whole = outs
     half, width = own.shape
     mine = width // 2
     rows = width // GROUPS
     s = lax.axis_index("seq")
     for i in range(2):
         cols = slice(i * mine, (i + 1) * mine)
-        for p, (start, stop, order) in enumerate(parts):
-            for n in range(start, stop, mine):
-                out = slice(n, n + mine)
-                got = (
-                    tn(own[:, cols], grads[0:half, out]) + tn(other[:, cols], grads[half:, out])
-                ).astype(BF)
-                to = slice(n - start, n - start + mine)
-                for b in range(GROUPS // 2):
-                    place(
-                        got[b * rows : (b + 1) * rows, :], i * (GROUPS // 2) + b, order,
-                        outs[2 * p], outs[2 * p + 1], to,
-                    )
+        both_t = jnp.concatenate([own[:, cols].T, other[:, cols].T], axis=1)
+        for c in range(3):
+            out = slice(c * mine, (c + 1) * mine)
+            whole[cols, out] = nn(both_t, grads[:, out]).astype(BF)
+    for p, (start, stop, order) in enumerate(parts):
+        spread_rows(whole, order, outs[2 * p], outs[2 * p + 1], slice(start, stop), slice(0, stop - start))
     zero = jnp.zeros((1, mine), F32)
     lines = []
     for r in range(2):
@@ -570,8 +552,9 @@
             ref[c : c + 1, :] = table[2 + base + i : 3 + base + i, c * 128 : (c + 1) * 128]
 
 
-def finish_input_kernel(lens, keep, sent, got, d_input, pooled):
+def finish_input_kernel(lens, keep, sent, got, final, d_input, pooled, output):
     half = keep.shape[0]
+    output[...] = final[...]
     d_input[...] = keep[...] + got[0:half, :]
     total = sent[half:, :] + got[half:, :]
     for t in range(lens.shape[1]):
@@ -681,14 +664,14 @@
     def parts_of(weight):
         names = [n for n in PARTS if PARTS[n][0] == weight]
         return names, tuple(
-            (PARTS[n][1], PARTS[n][2], both_cores(PARTS[n][3]) if spread else None) for n in names
+            (PARTS[n][1], PARTS[n][2], as_bits(*PARTS[n][3:]) if spread else None) for n in names
         )
 
     def reduce(names, arrays):
         for i, name in enumerate(names):
             keep, send = arrays[2 * i], arrays[2 * i + 1]
             vec = made["table"] if name == WITH_VECTORS else None
-            sums[name] = Part(keep, send, both_cores(PARTS[name][3]), vec)
+            sums[name] = Part(keep, send, as_bits(*PARTS[name][3:]), vec)
         if spread:
             weight = PARTS[names[0]][0]
             sums[weight] = Sum(line, [sums[n] for n in names], count, weight)
@@ -698,7 +681,7 @@
         project_kernel,
         [sds((half, width), BF), sds((3, width, mine), BF), sds((8, mine), F32), sds((half, 3 * mine), F32)],
         own, w_qkv, b_qv,
-        hbm=(0, 1, 2), scratch=[pltpu.VMEM(b_qv.shape, BF), pltpu.SemaphoreType.DMA((5,))],
+        hbm=(0, 1, 2), scratch=[pltpu.VMEM(b_qv.shape, BF), pltpu.SemaphoreType.DMA((3 * PIECES + 2,))],
         name="project", vmem=12,
     )
     q, k, v, kt, expo, scale, att_t, att_mine, w_o, w_in, w_out = call(
@@ -708,7 +691,7 @@
         + [sds((mine, length), F32), sds((length, mine), BF)]
         + [sds(w.shape, BF) for w in (w_o, w_in, w_out)],
         seg_lengths, other, w_mine, bias, lin, w_o, w_in, w_out,
-        smem=(0,), hbm=(5, 6, 7), scratch=[pltpu.SemaphoreType.DMA((3,))], name="attend", vmem=16,
+        smem=(0,), hbm=(5, 6, 7), scratch=[pltpu.SemaphoreType.DMA((3 * PIECES,))], name="attend", vmem=16,
     )
     att_got = swap(att_mine)
     (mid_low, active, pull, normal, inverse, sum2, down_own, down_send, output, pool_part, vec_f) = call(
@@ -745,6 +728,7 @@
         arrays = call(
             functools.partial(grad_out_kernel, parts), outs,
             active, active_got, down_own, down_got, name="grad_out",
+            scratch=[pltpu.VMEM((ff, mine), BF)],
         )
         reduce(names, arrays)
 
@@ -757,6 +741,7 @@
         arrays = call(
             functools.partial(grad_in_kernel, parts, with_o), outs,
             mid_low, mid_got, made["up_own"], made["up_got"], att_mine, att_got, *made["branch"], name="grad_in",
+            scratch=[pltpu.VMEM((width, ff // 2), BF), pltpu.VMEM((width, mine), BF)],
         )
         reduce(names, arrays)
 
@@ -777,6 +762,7 @@
         *arrays, made["table"] = call(
             functools.partial(grad_qkv_kernel, parts, with_vectors), outs,
             own, other, made["grads"], vec_f, made["vec_b"], made["vec_a"], name="grad_qkv",
+            scratch=[pltpu.VMEM((width, 3 * mine), BF)],
         )
         reduce(names, arrays)
 
@@ -788,14 +774,15 @@
         made["got"] = swap(made["send"])
 
     def finish_input():
-        made["d_input"], made["pooled"] = call(
-            finish_input_kernel, [sds((half, width), F32), sds((seg_lengths.shape[1], width), F32)],
-            seg_lengths, made["keep"], made["send"], made["got"], smem=(0,), name="finish_input", end=True,
+        made["d_input"], made["pooled"], made["output"] = call(
+            finish_input_kernel,
+            [sds((half, width), F32), sds((seg_lengths.shape[1], width), F32), sds((half, width), BF)],
+            seg_lengths, made["keep"], made["send"], made["got"], output, smem=(0,), name="finish_input", end=True,
         )
 
     def places_of(weight, pieces):
         if weight == "o":
-            _, start, stop, _ = PARTS[WITH_O]
+            start, stop = PARTS[WITH_O][1:3]
             return [WITH_O], [(0, stop - start + c) for c in range(0, mine, 128)]
         names, parts = parts_of(weight)
         return names, [
@@ -817,11 +804,10 @@
 
         def kernel(*refs):
             results = refs[len(args) :]
+            sent, got = refs[len(args) - 2 : len(args)]
             for job, (run, start, stop) in enumerate(jobs):
                 run(*refs[start:stop], results[job])
-            finish_vectors_kernel(
-                part.keep.shape[0], width, refs[len(args) - 2], refs[len(args) - 1], *results[len(jobs) :]
-            )
+            finish_vectors_kernel(part.keep.shape[0], width, sent, got, *results[len(jobs) :])
 
         done = call(kernel, outs, *args, name="finish", vmem=10)
         for weight, out in zip(WEIGHTS, done):
@@ -862,7 +848,7 @@
         vectors = [vec[0:2]] + [vec[2 + base + i] for i in (2, 0, 1)] + [vec[2 : 2 + base].reshape(-1)]
         vectors += [vec[2 + base + i] for i in (5, 3, 4)]
     return (
-        output.reshape(row_count, half, width),
+        made["output"].reshape(row_count, half, width),
         made["pooled"][None],
         made["d_input"].reshape(row_count, half, width),
         *(flats[n] for n in ("qkv", "o", "in", "out")),
@@ -870,10 +856,9 @@
     )
 
 
-def both_cores(letters):
+def as_bits(*orders):
     bits = {"x": 0, "y": 1, "1": 2, "2": 3}
-    turned = {"x": "y", "y": "x"}
-    return tuple(bits[c] for c in letters), tuple(bits[turned.get(c, c)] for c in letters)
+    return tuple(tuple(bits[c] for c in order) for order in orders)
 
 
 def solution(mesh):

time: 101 us -> 95.4 us (0.945); the launches traced: 99.2 us -> 95.2 us
  waiting for transfers between devices: 25 us -> 37.2 us
  starting transfers between devices: 34.7 us -> 25.3 us
  Pallas kernels: 38.3 us -> 31.5 us
    ppermute x20 -> x16, waiting for transfers between devices: 20.5 us -> 34.7 us  [send_to(): return lax.ppermute(x, ('dp', 'seq'), pairs)]
    ppermute x20 -> x16, starting transfers between devices: 32 us -> 22.5 us  [send_to(): return lax.ppermute(x, ('dp', 'seq'), pairs)]
    pallas_call x23, Pallas kernels: 38.3 us -> 31.5 us  [call(): pl.pallas_call(body, out_shape=list(outs), in_specs=specs, out_specs=[pl....]
    ppermute x13 -> x12, waiting for transfers between devices: 4.47 us -> 2.45 us  [swap(): return lax.ppermute(x, axis, [(0, 1), (1, 0)])]
    ppermute x13 -> x12, starting transfers between devices: 2.66 us -> 2.75 us  [swap(): return lax.ppermute(x, axis, [(0, 1), (1, 0)])]
  transfers between devices with their start and end apart: 33 -> 28, of which waited for: 14 -> 13; matrix products, arithmetic and copies ran while one was open for 0% -> 0% of each run, Pallas kernels for 27% -> 21%
where the time goes in v3:
time: 95.4 us; the launch traced here: 95.2 us
  waiting for transfers between devices  37.2 us (39%)
  Pallas kernels  31.5 us (33%)
  starting transfers between devices  25.3 us (27%)
  between operations  1.16 us (1%)
    ppermute x16, waiting for transfers between devices, send_to(): return lax.ppermute(x, ('dp', 'seq'), pairs)  34.7 us
    pallas_call x23, Pallas kernels, call(): pl.pallas_call(body, out_shape=list(outs), in_specs=specs, out_specs=[pl....  31.5 us
    ppermute x16, starting transfers between devices, send_to(): return lax.ppermute(x, ('dp', 'seq'), pairs)  22.5 us
    ppermute x12, starting transfers between devices, swap(): return lax.ppermute(x, axis, [(0, 1), (1, 0)])  2.75 us
    ppermute x12, waiting for transfers between devices, swap(): return lax.ppermute(x, axis, [(0, 1), (1, 0)])  2.45 us
  transfers between devices with their start and end apart: 28, of which 13 were waited for; matrix products, arithmetic and copies ran while one was open for 0% of the time, Pallas kernels for 21%

profile of v3, /device:TPU:0, one launch (start us, length us, event | category | flops | bytes accessed | tf_op | source)
XLA Modules:
  0.0 95.2 jit_solution(14156326106081373856)
XLA Ops:
  1.2 2.6 %project.1 = (bf16[256,768]{1,0:T(8,128)(2,1)S(1)}, bf16[3,768,384]{2,1,0:T(8,128)(2,1)S(1)}, f32[8,384]{1,0:T(8,128)S(1)}, f32[256,1152]{1,0:T(8,128)S(1)}) custom-call(bf16[256,768]{1,0:T(8,128)(2,1)} %bitcast.18, bf16[768,2304]{1,0:T(8,128)(2,1)} %refs_1_.1, bf16[2,768]{1,0:T(2,128)(2,1)} %refs_2_.1), custom_call_target="tpu_custom_call" | custom-call | flops 1100000000 | bytes 1024 | tf_op jit(solution)/shard_map/project/pallas_call | solution.py:78
  3.9 4.8 %attend.1 = (bf16[512,384]{1,0:T(8,128)(2,1)S(1)}, bf16[512,384]{1,0:T(8,128)(2,1)S(1)}, bf16[512,384]{1,0:T(8,128)(2,1)S(1)}, bf16[384,512]{1,0:T(8,128)(2,1)S(...) custom-call(s32[1,4]{1,0:T(1,128)S(1)} %copy-done.1, ...), custom_call_target="tpu_custom_call" | custom-call | flops 1100000000 | bytes 1024 | tf_op jit(solution)/shard_map/attend/pallas_call | solution.py:78
  10.5 5.6 %forward.1 = (bf16[256,768]{1,0:T(8,128)(2,1)S(1)}, bf16[256,3072]{1,0:T(8,128)(2,1)S(1)}, f32[256,3072]{1,0:T(8,128)S(1)}, f32[256,768]{1,0:T(8,128)S(1)}, f32[...) custom-call(s32[1,4]{1,0:T(1,128)S(1)} %copy-done.1, ...), custom_call_target="tpu_custom_call" | custom-call | flops 1100000000 | bytes 1024 | tf_op jit(solution)/shard_map/forward/pallas_call | solution.py:78
  16.7 3.3 %backward.1 = (bf16[256,1536]{1,0:T(8,128)(2,1)S(1)}, bf16[256,1536]{1,0:T(8,128)(2,1)S(1)}, f32[256,768]{1,0:T(8,128)S(1)}, bf16[256,768]{1,0:T(8,128)(2,1)S(1)}, f32[8,768]{1,0:T(8,128)S(1)}) custom-call(f32[256,768]{1,0:T(8,128)S(1)} %get-tuple-element.119.refs_0_, f32[256,3072]{1,0:T(8,128)S(1)} %get-tuple-element.120.refs_1_, ...), custom_call_target="tpu_custom_call" | custom-call | flops 1100000000 | bytes 1024 | tf_op jit(solution)/shard_map/backward/pallas_call | solution.py:78
  20.6 2.1 %grad_out.1 = (bf16[1536,384]{1,0:T(8,128)(2,1)S(1)}, bf16[1536,384]{1,0:T(8,128)(2,1)S(1)}) custom-call(bf16[256,3072]{1,0:T(8,128)(2,1)S(1)} %get-tuple-element.131.refs_0_, bf16[256,3072]{1,0:T(8,128)(2,1)S(1)} %collective-permute-done.3.refs_1_, bf16[256,384]{1,0:T(8,128)(2,1)S(1)} %get-tuple-element.132.refs_2_, ...), custom_call_target="tpu_custom_call" | custom-call | flops 1100000000 | bytes 1024 | tf_op jit(solution)/shard_map/grad_out/pallas_call | solution.py:78
  22.6 2.7 %collective-permute-start.11 = (bf16[1536,384]{1,0:T(8,128)(2,1)S(1)}, bf16[1536,384]{1,0:T(8,128)(2,1)S(1)}, u32[]{:S(2)}, u32[]{:S(2)}) collective-permute-start(bf16[1536,384]{1,0:T(8,128)(2,1)S(1)} %get-tuple-element.153), channel_id=1, source_target_pairs={{0,4},{1,9},{2,6},{3,11},{4,0},{5,13},{6,2},{7,15},{8,12},{9,1},{1... | collective-permute-start | bytes 3538952 | tf_op jit(solution)/shard_map/ppermute | solution.py:573
  25.5 3.6 %attend_back.1 = (bf16[512,1152]{1,0:T(8,128)(2,1)S(1)}, f32[8,384]{1,0:T(8,128)S(1)}) custom-call(bf16[256,768]{1,0:T(8,128)(2,1)S(1)} %get-tuple-element.124.refs_0_.refs_6_, bf16[256,768]{1,0:T(8,128)(2,1)S(1)} %collective-permute-done.2.refs_1_.refs_7_, bf16[768,768]{1,0:T(8,128)(2,1)S(1)} %get-tuple-element.115.refs_4_.refs_2_, ...), custom_call_target="tpu_custom_call" | custom-call | flops 1100000000 | bytes 1024 | tf_op jit(solution)/shard_map/attend_back/pallas_call | solution.py:78
  29.1 1.6 %grad_qkv.1 = (bf16[384,1152]{1,0:T(8,128)(2,1)S(1)}, bf16[416,1152]{1,0:T(8,128)(2,1)S(1)}, f32[16,768]{1,0:T(8,128)S(1)}) custom-call(bf16[256,768]{1,0:T(8,128)(2,1)S(1)} %get-tuple-element.110.refs_8_.refs_1_.refs_0_, bf16[256,768]{1,0:T(8,128)(2,1)S(1)} %collective-permute-done.refs_1_, ...), custom_call_target="tpu_custom_call" | custom-call | flops 1100000000 | bytes 1024 | tf_op jit(solution)/shard_map/grad_qkv/pallas_call | solution.py:78
  30.7 1.6 %collective-permute-start.10 = (bf16[416,1152]{1,0:T(8,128)(2,1)S(1)}, bf16[416,1152]{1,0:T(8,128)(2,1)S(1)}, u32[]{:S(2)}, u32[]{:S(2)}) collective-permute-start(bf16[416,1152]{1,0:T(8,128)(2,1)S(1)} %get-tuple-element.151), channel_id=1, source_target_pairs={{0,2},{1,3},{2,0},{3,1},{4,6},{5,7},{6,4},{7,5},{8,10},{9,11},{10,... | collective-permute-start | bytes 2875400 | tf_op jit(solution)/shard_map/ppermute | solution.py:573
  32.3 2.1 %grad_in.1 = (bf16[384,1024]{1,0:T(8,128)(2,1)S(1)}, bf16[384,1024]{1,0:T(8,128)(2,1)S(1)}, bf16[384,896]{1,0:T(8,128)(2,1)S(1)}, bf16[384,896]{1,0:T(8,128)(2,1)S(1)}) custom-call(bf16[256,768]{1,0:T(8,128)(2,1)S(1)} %get-tuple-element.123.refs_7_.refs_0_, bf16[256,768]{1,0:T(8,128)(2,1)S(1)} %collective-permute-done.5.refs_1_, ...), custom_call_target="tpu_custom_call" | custom-call | flops 1100000000 | bytes 1024 | tf_op jit(solution)/shard_map/grad_in/pallas_call | solution.py:78
  34.4 1.6 %collective-permute-start.8 = (bf16[384,1024]{1,0:T(8,128)(2,1)S(1)}, bf16[384,1024]{1,0:T(8,128)(2,1)S(1)}, u32[]{:S(2)}, u32[]{:S(2)}) collective-permute-start(bf16[384,1024]{1,0:T(8,128)(2,1)S(1)} %get-tuple-element.148), channel_id=1, source_target_pairs={{0,4},{1,3},{2,6},{3,1},{4,0},{5,7},{6,2},{7,5},{8,12},{9,11},{10,... | collective-permute-start | bytes 2359304 | tf_op jit(solution)/shard_map/ppermute | solution.py:573
  39.9 2.6 %collective-permute-start.12 = (bf16[768,384]{1,0:T(8,128)(2,1)S(1)}, bf16[768,384]{1,0:T(8,128)(2,1)S(1)}, u32[]{:S(2)}, u32[]{:S(2)}) collective-permute-start(bf16[768,384]{1,0:T(8,128)(2,1)S(1)} %get-tuple-element.160), channel_id=1, source_target_pairs={{0,8},{1,17},{2,10},{3,19},{4,12},{5,21},{6,14},{7,23},{8,0},{9,25... | collective-permute-start | bytes 1769480 | tf_op jit(solution)/shard_map/ppermute | solution.py:573
  42.5 12.3 %collective-permute-done.10.refs_0_ = bf16[416,1152]{1,0:T(8,128)(2,1)S(1)} collective-permute-done((bf16[416,1152]{1,0:T(8,128)(2,1)S(1)}, bf16[416,1152]{1,0:T(8,128)(2,1)S(1)}, u32[]{:S(2)}, u32[]{:S(2)}) %collective-permute-start.10) | collective-permute-done | bytes 958496 | tf_op jit(solution)/shard_map/ppermute | solution.py:573
  55.1 2.7 %collective-permute-start.16 = (bf16[224,1152]{1,0:T(8,128)(2,1)S(1)}, bf16[224,1152]{1,0:T(8,128)(2,1)S(1)}, u32[]{:S(2)}, u32[]{:S(2)}) collective-permute-start(bf16[224,1152]{1,0:T(8,128)(2,1)S(1)} %get-tuple-element.167), channel_id=1, source_target_pairs={{0,16},{1,5},{2,18},{3,7},{4,20},{5,1},{6,22},{7,3},{8,24},{9,13},... | collective-permute-start | bytes 1548296 | tf_op jit(solution)/shard_map/ppermute | solution.py:573
  58.1 1.6 %collective-permute-start.15 = (bf16[192,896]{1,0:T(8,128)(2,1)S(1)}, bf16[192,896]{1,0:T(8,128)(2,1)S(1)}, u32[]{:S(2)}, u32[]{:S(2)}) collective-permute-start(bf16[192,896]{1,0:T(8,128)(2,1)S(1)} %get-tuple-element.165), channel_id=1, source_target_pairs={{0,4},{1,3},{2,6},{3,1},{4,0},{5,7},{6,2},{7,5},{8,12},{9,11},{10,... | collective-permute-start | bytes 1032200 | tf_op jit(solution)/shard_map/ppermute | solution.py:573
  60.1 1.7 %finish_input.1 = (f32[8,128]{1,0:T(8,128)S(1)}, f32[256,768]{1,0:T(8,128)}, f32[4,768]{1,0:T(4,128)}, bf16[256,768]{1,0:T(8,128)(2,1)}) custom-call(s32[1,4]{1,0:T(1,128)S(1)} %copy-done.1, f32[256,768]{1,0:T(8,128)S(1)} %get-tuple-element.145.refs_2_.refs_1_, f32[264,768]{1,0:T(8,128)S(1)} %get-tuple-element.146.refs_2_, ...), custom_call_target="tpu_custom_call" | custom-call | flops 1100000000 | bytes 1024 | tf_op jit(solution)/shard_map/finish_input/pallas_call | solution.py:78
  61.8 3.0 %collective-permute-done.12.refs_0_ = bf16[768,384]{1,0:T(8,128)(2,1)S(1)} collective-permute-done((bf16[768,384]{1,0:T(8,128)(2,1)S(1)}, bf16[768,384]{1,0:T(8,128)(2,1)S(1)}, u32[]{:S(2)}, u32[]{:S(2)}) %collective-permute-start.12) | collective-permute-done | bytes 589856 | tf_op jit(solution)/shard_map/ppermute | solution.py:573
  65.0 5.8 %collective-permute-done.16.refs_0_ = bf16[224,1152]{1,0:T(8,128)(2,1)S(1)} collective-permute-done((bf16[224,1152]{1,0:T(8,128)(2,1)S(1)}, bf16[224,1152]{1,0:T(8,128)(2,1)S(1)}, u32[]{:S(2)}, u32[]{:S(2)}) %collective-permute-start.16) | collective-permute-done | bytes 516128 | tf_op jit(solution)/shard_map/ppermute | solution.py:573
  70.9 1.6 %collective-permute-start.20 = (bf16[128,1152]{1,0:T(8,128)(2,1)S(1)}, bf16[128,1152]{1,0:T(8,128)(2,1)S(1)}, u32[]{:S(2)}, u32[]{:S(2)}) collective-permute-start(bf16[128,1152]{1,0:T(8,128)(2,1)S(1)} %get-tuple-element.176), channel_id=1, source_target_pairs={{0,4},{1,9},{2,6},{3,11},{4,0},{5,13},{6,2},{7,15},{8,12},{9,1},{1... | collective-permute-start | bytes 884744 | tf_op jit(solution)/shard_map/ppermute | solution.py:573
  78.4 2.0 %collective-permute-done.18.refs_0_ = bf16[96,1024]{1,0:T(8,128)(2,1)S(1)} collective-permute-done((bf16[96,1024]{1,0:T(8,128)(2,1)S(1)}, bf16[96,1024]{1,0:T(8,128)(2,1)S(1)}, u32[]{:S(2)}, u32[]{:S(2)}) %collective-permute-start.18) | collective-permute-done | bytes 196640 | tf_op jit(solution)/shard_map/ppermute | solution.py:573
  80.4 1.6 %collective-permute-start.23 = (bf16[48,896]{1,0:T(8,128)(2,1)S(1)}, bf16[48,896]{1,0:T(8,128)(2,1)S(1)}, u32[]{:S(2)}, u32[]{:S(2)}) collective-permute-start(bf16[48,896]{1,0:T(8,128)(2,1)S(1)} %get-tuple-element.183), channel_id=1, source_target_pairs={{0,16},{1,9},{2,18},{3,11},{4,20},{5,13},{6,22},{7,15},{8,24},{9,1... | collective-permute-start | bytes 258056 | tf_op jit(solution)/shard_map/ppermute | solution.py:573
  84.0 4.0 %collective-permute-done.24.refs_0_ = bf16[80,1152]{1,0:T(8,128)(2,1)S(1)} collective-permute-done((bf16[80,1152]{1,0:T(8,128)(2,1)S(1)}, bf16[80,1152]{1,0:T(8,128)(2,1)S(1)}, u32[]{:S(2)}, u32[]{:S(2)}) %collective-permute-start.24) | collective-permute-done | bytes 184352 | tf_op jit(solution)/shard_map/ppermute | solution.py:573
  88.0 2.8 %collective-permute-done.23.refs_2_ = bf16[48,896]{1,0:T(8,128)(2,1)S(1)} collective-permute-done((bf16[48,896]{1,0:T(8,128)(2,1)S(1)}, bf16[48,896]{1,0:T(8,128)(2,1)S(1)}, u32[]{:S(2)}, u32[]{:S(2)}) %collective-permute-start.23) | collective-permute-done | bytes 86048 | tf_op jit(solution)/shard_map/ppermute | solution.py:573
  90.9 1.6 %collective-permute-done.22.refs_0_ = bf16[48,1024]{1,0:T(8,128)(2,1)S(1)} collective-permute-done((bf16[48,1024]{1,0:T(8,128)(2,1)S(1)}, bf16[48,1024]{1,0:T(8,128)(2,1)S(1)}, u32[]{:S(2)}, u32[]{:S(2)}) %collective-permute-start.22) | collective-permute-done | bytes 98336 | tf_op jit(solution)/shard_map/ppermute | solution.py:573
  (80 shorter events, 19.3 us)
Async XLA Ops:
  16.1 4.5 %collective-permute-start.3 = (bf16[256,3072]{1,0:T(8,128)(2,1)S(1)}, bf16[256,3072]{1,0:T(8,128)(2,1)S(1)}, u32[]{:S(2)}, u32[]{:S(2)}) collective-permute-start(bf16[256,3072]{1,0:T(8,128)(2,1)S(1)} %get-tuple-element.131.refs_0_), channel_id=1, source_target_pairs={{0,1},{1,0},{2,3},{3,2},{4,5},{5,4},{6,7},{7,6},{8,9},{9,8},{10,11... | collective-permute-start | bytes 4718600 | tf_op jit(solution)/shard_map/ppermute | solution.py:565
  16.3 4.2 %collective-permute-start.4 = (bf16[256,384]{1,0:T(8,128)(2,1)S(1)}, bf16[256,384]{1,0:T(8,128)(2,1)S(1)}, u32[]{:S(2)}, u32[]{:S(2)}) collective-permute-start(bf16[256,384]{1,0:T(8,128)(2,1)S(1)} %get-tuple-element.133), channel_id=1, source_target_pairs={{0,1},{1,0},{2,3},{3,2},{4,5},{5,4},{6,7},{7,6},{8,9},{9,8},{10,11... | collective-permute-start | bytes 589832 | tf_op jit(solution)/shard_map/ppermute | solution.py:565
  20.0 5.6 %collective-permute-start.2 = (bf16[256,768]{1,0:T(8,128)(2,1)S(1)}, bf16[256,768]{1,0:T(8,128)(2,1)S(1)}, u32[]{:S(2)}, u32[]{:S(2)}) collective-permute-start(bf16[256,768]{1,0:T(8,128)(2,1)S(1)} %get-tuple-element.124.refs_0_.refs_6_), channel_id=1, source_target_pairs={{0,1},{1,0},{2,3},{3,2},{4,5},{5,4},{6,7},{7,6},{8,9},{9,8},{10,11... | collective-permute-start | bytes 1179656 | tf_op jit(solution)/shard_map/ppermute | solution.py:565
  20.2 12.1 %collective-permute-start.6 = (bf16[256,1536]{1,0:T(8,128)(2,1)S(1)}, bf16[256,1536]{1,0:T(8,128)(2,1)S(1)}, u32[]{:S(2)}, u32[]{:S(2)}) collective-permute-start(bf16[256,1536]{1,0:T(8,128)(2,1)S(1)} %get-tuple-element.139), channel_id=1, source_target_pairs={{0,1},{1,0},{2,3},{3,2},{4,5},{5,4},{6,7},{7,6},{8,9},{9,8},{10,11... | collective-permute-start | bytes 2359304 | tf_op jit(solution)/shard_map/ppermute | solution.py:565
  22.6 16.9 %collective-permute-start.11 = (bf16[1536,384]{1,0:T(8,128)(2,1)S(1)}, bf16[1536,384]{1,0:T(8,128)(2,1)S(1)}, u32[]{:S(2)}, u32[]{:S(2)}) collective-permute-start(bf16[1536,384]{1,0:T(8,128)(2,1)S(1)} %get-tuple-element.153), channel_id=1, source_target_pairs={{0,4},{1,9},{2,6},{3,11},{4,0},{5,13},{6,2},{7,15},{8,12},{9,1},{1... | collective-permute-start | bytes 3538952 | tf_op jit(solution)/shard_map/ppermute | solution.py:573
  25.4 6.9 %collective-permute-start.5 = (bf16[256,768]{1,0:T(8,128)(2,1)S(1)}, bf16[256,768]{1,0:T(8,128)(2,1)S(1)}, u32[]{:S(2)}, u32[]{:S(2)}) collective-permute-start(bf16[256,768]{1,0:T(8,128)(2,1)S(1)} %get-tuple-element.123.refs_7_.refs_0_), channel_id=1, source_target_pairs={{0,1},{1,0},{2,3},{3,2},{4,5},{5,4},{6,7},{7,6},{8,9},{9,8},{10,11... | collective-permute-start | bytes 1179656 | tf_op jit(solution)/shard_map/ppermute | solution.py:565
  30.7 24.1 %collective-permute-start.10 = (bf16[416,1152]{1,0:T(8,128)(2,1)S(1)}, bf16[416,1152]{1,0:T(8,128)(2,1)S(1)}, u32[]{:S(2)}, u32[]{:S(2)}) collective-permute-start(bf16[416,1152]{1,0:T(8,128)(2,1)S(1)} %get-tuple-element.151), channel_id=1, source_target_pairs={{0,2},{1,3},{2,0},{3,1},{4,6},{5,7},{6,4},{7,5},{8,10},{9,11},{10,... | collective-permute-start | bytes 2875400 | tf_op jit(solution)/shard_map/ppermute | solution.py:573
  34.4 23.3 %collective-permute-start.8 = (bf16[384,1024]{1,0:T(8,128)(2,1)S(1)}, bf16[384,1024]{1,0:T(8,128)(2,1)S(1)}, u32[]{:S(2)}, u32[]{:S(2)}) collective-permute-start(bf16[384,1024]{1,0:T(8,128)(2,1)S(1)} %get-tuple-element.148), channel_id=1, source_target_pairs={{0,4},{1,3},{2,6},{3,1},{4,0},{5,7},{6,2},{7,5},{8,12},{9,11},{10,... | collective-permute-start | bytes 2359304 | tf_op jit(solution)/shard_map/ppermute | solution.py:573
  37.4 22.7 %collective-permute-start.7 = (f32[264,768]{1,0:T(8,128)S(1)}, f32[264,768]{1,0:T(8,128)S(1)}, u32[]{:S(2)}, u32[]{:S(2)}) collective-permute-start(f32[264,768]{1,0:T(8,128)S(1)} %get-tuple-element.146.refs_2_), channel_id=1, source_target_pairs={{0,1},{1,0},{2,3},{3,2},{4,5},{5,4},{6,7},{7,6},{8,9},{9,8},{10,11... | collective-permute-start | bytes 2433032 | tf_op jit(solution)/shard_map/ppermute | solution.py:565
  37.5 20.2 %collective-permute-start.9 = (bf16[384,896]{1,0:T(8,128)(2,1)S(1)}, bf16[384,896]{1,0:T(8,128)(2,1)S(1)}, u32[]{:S(2)}, u32[]{:S(2)}) collective-permute-start(bf16[384,896]{1,0:T(8,128)(2,1)S(1)} %get-tuple-element.149), channel_id=1, source_target_pairs={{0,8},{1,5},{2,10},{3,7},{4,12},{5,1},{6,14},{7,3},{8,0},{9,13},{1... | collective-permute-start | bytes 2064392 | tf_op jit(solution)/shard_map/ppermute | solution.py:573
  39.9 24.9 %collective-permute-start.12 = (bf16[768,384]{1,0:T(8,128)(2,1)S(1)}, bf16[768,384]{1,0:T(8,128)(2,1)S(1)}, u32[]{:S(2)}, u32[]{:S(2)}) collective-permute-start(bf16[768,384]{1,0:T(8,128)(2,1)S(1)} %get-tuple-element.160), channel_id=1, source_target_pairs={{0,8},{1,17},{2,10},{3,19},{4,12},{5,21},{6,14},{7,23},{8,0},{9,25... | collective-permute-start | bytes 1769480 | tf_op jit(solution)/shard_map/ppermute | solution.py:573
  55.1 15.7 %collective-permute-start.16 = (bf16[224,1152]{1,0:T(8,128)(2,1)S(1)}, bf16[224,1152]{1,0:T(8,128)(2,1)S(1)}, u32[]{:S(2)}, u32[]{:S(2)}) collective-permute-start(bf16[224,1152]{1,0:T(8,128)(2,1)S(1)} %get-tuple-element.167), channel_id=1, source_target_pairs={{0,16},{1,5},{2,18},{3,7},{4,20},{5,1},{6,22},{7,3},{8,24},{9,13},... | collective-permute-start | bytes 1548296 | tf_op jit(solution)/shard_map/ppermute | solution.py:573
  58.1 14.5 %collective-permute-start.15 = (bf16[192,896]{1,0:T(8,128)(2,1)S(1)}, bf16[192,896]{1,0:T(8,128)(2,1)S(1)}, u32[]{:S(2)}, u32[]{:S(2)}) collective-permute-start(bf16[192,896]{1,0:T(8,128)(2,1)S(1)} %get-tuple-element.165), channel_id=1, source_target_pairs={{0,4},{1,3},{2,6},{3,1},{4,0},{5,7},{6,2},{7,5},{8,12},{9,11},{10,... | collective-permute-start | bytes 1032200 | tf_op jit(solution)/shard_map/ppermute | solution.py:573
  59.7 12.9 %collective-permute-start.14 = (bf16[192,1024]{1,0:T(8,128)(2,1)S(1)}, bf16[192,1024]{1,0:T(8,128)(2,1)S(1)}, u32[]{:S(2)}, u32[]{:S(2)}) collective-permute-start(bf16[192,1024]{1,0:T(8,128)(2,1)S(1)} %get-tuple-element.164), channel_id=1, source_target_pairs={{0,8},{1,5},{2,10},{3,7},{4,12},{5,1},{6,14},{7,3},{8,0},{9,13},{1... | collective-permute-start | bytes 1179656 | tf_op jit(solution)/shard_map/ppermute | solution.py:573
  65.0 10.0 %collective-permute-start.13 = (bf16[384,384]{1,0:T(8,128)(2,1)S(1)}, bf16[384,384]{1,0:T(8,128)(2,1)S(1)}, u32[]{:S(2)}, u32[]{:S(2)}) collective-permute-start(bf16[384,384]{1,0:T(8,128)(2,1)S(1)} %get-tuple-element.162), channel_id=1, source_target_pairs={{0,2},{1,3},{2,0},{3,1},{4,6},{5,7},{6,4},{7,5},{8,10},{9,11},{10,... | collective-permute-start | bytes 884744 | tf_op jit(solution)/shard_map/ppermute | solution.py:573
  70.9 6.8 %collective-permute-start.20 = (bf16[128,1152]{1,0:T(8,128)(2,1)S(1)}, bf16[128,1152]{1,0:T(8,128)(2,1)S(1)}, u32[]{:S(2)}, u32[]{:S(2)}) collective-permute-start(bf16[128,1152]{1,0:T(8,128)(2,1)S(1)} %get-tuple-element.176), channel_id=1, source_target_pairs={{0,4},{1,9},{2,6},{3,11},{4,0},{5,13},{6,2},{7,15},{8,12},{9,1},{1... | collective-permute-start | bytes 884744 | tf_op jit(solution)/shard_map/ppermute | solution.py:573
  72.8 5.6 %collective-permute-start.19 = (bf16[96,896]{1,0:T(8,128)(2,1)S(1)}, bf16[96,896]{1,0:T(8,128)(2,1)S(1)}, u32[]{:S(2)}, u32[]{:S(2)}) collective-permute-start(bf16[96,896]{1,0:T(8,128)(2,1)S(1)} %get-tuple-element.174), channel_id=1, source_target_pairs={{0,2},{1,17},{2,0},{3,19},{4,6},{5,21},{6,4},{7,23},{8,10},{9,25},... | collective-permute-start | bytes 516104 | tf_op jit(solution)/shard_map/ppermute | solution.py:573
  74.3 6.1 %collective-permute-start.18 = (bf16[96,1024]{1,0:T(8,128)(2,1)S(1)}, bf16[96,1024]{1,0:T(8,128)(2,1)S(1)}, u32[]{:S(2)}, u32[]{:S(2)}) collective-permute-start(bf16[96,1024]{1,0:T(8,128)(2,1)S(1)} %get-tuple-element.173), channel_id=1, source_target_pairs={{0,2},{1,9},{2,0},{3,11},{4,6},{5,13},{6,4},{7,15},{8,10},{9,1},{1... | collective-permute-start | bytes 589832 | tf_op jit(solution)/shard_map/ppermute | solution.py:573
  75.1 8.7 %collective-permute-start.17 = (bf16[192,384]{1,0:T(8,128)(2,1)S(1)}, bf16[192,384]{1,0:T(8,128)(2,1)S(1)}, u32[]{:S(2)}, u32[]{:S(2)}) collective-permute-start(bf16[192,384]{1,0:T(8,128)(2,1)S(1)} %get-tuple-element.171), channel_id=1, source_target_pairs={{0,16},{1,5},{2,18},{3,7},{4,20},{5,1},{6,22},{7,3},{8,24},{9,13},... | collective-permute-start | bytes 442376 | tf_op jit(solution)/shard_map/ppermute | solution.py:573
  77.8 10.1 %collective-permute-start.24 = (bf16[80,1152]{1,0:T(8,128)(2,1)S(1)}, bf16[80,1152]{1,0:T(8,128)(2,1)S(1)}, u32[]{:S(2)}, u32[]{:S(2)}) collective-permute-start(bf16[80,1152]{1,0:T(8,128)(2,1)S(1)} %get-tuple-element.185), channel_id=1, source_target_pairs={{0,8},{1,17},{2,10},{3,19},{4,12},{5,21},{6,14},{7,23},{8,0},{9,25... | collective-permute-start | bytes 552968 | tf_op jit(solution)/shard_map/ppermute | solution.py:573
  80.4 10.4 %collective-permute-start.23 = (bf16[48,896]{1,0:T(8,128)(2,1)S(1)}, bf16[48,896]{1,0:T(8,128)(2,1)S(1)}, u32[]{:S(2)}, u32[]{:S(2)}) collective-permute-start(bf16[48,896]{1,0:T(8,128)(2,1)S(1)} %get-tuple-element.183), channel_id=1, source_target_pairs={{0,16},{1,9},{2,18},{3,11},{4,20},{5,13},{6,22},{7,15},{8,24},{9,1... | collective-permute-start | bytes 258056 | tf_op jit(solution)/shard_map/ppermute | solution.py:573
  82.0 10.4 %collective-permute-start.22 = (bf16[48,1024]{1,0:T(8,128)(2,1)S(1)}, bf16[48,1024]{1,0:T(8,128)(2,1)S(1)}, u32[]{:S(2)}, u32[]{:S(2)}) collective-permute-start(bf16[48,1024]{1,0:T(8,128)(2,1)S(1)} %get-tuple-element.182), channel_id=1, source_target_pairs={{0,16},{1,17},{2,18},{3,19},{4,20},{5,21},{6,22},{7,23},{8,24},{9,... | collective-permute-start | bytes 294920 | tf_op jit(solution)/shard_map/ppermute | solution.py:573
  83.9 10.2 %collective-permute-start.21 = (f32[96,384]{1,0:T(8,128)S(1)}, f32[96,384]{1,0:T(8,128)S(1)}, u32[]{:S(2)}, u32[]{:S(2)}) collective-permute-start(f32[96,384]{1,0:T(8,128)S(1)} %get-tuple-element.181), channel_id=1, source_target_pairs={{0,1},{1,0},{2,3},{3,2},{4,5},{5,4},{6,7},{7,6},{8,9},{9,8},{10,11... | collective-permute-start | bytes 442376 | tf_op jit(solution)/shard_map/ppermute | solution.py:565
  88.0 6.1 %collective-permute-start.27 = (f32[40,1152]{1,0:T(8,128)S(1)}, f32[40,1152]{1,0:T(8,128)S(1)}, u32[]{:S(2)}, u32[]{:S(2)}) collective-permute-start(f32[40,1152]{1,0:T(8,128)S(1)} %get-tuple-element.192.refs_10_), channel_id=1, source_target_pairs={{0,1},{1,0},{2,3},{3,2},{4,5},{5,4},{6,7},{7,6},{8,9},{9,8},{10,11... | collective-permute-start | bytes 552968 | tf_op jit(solution)/shard_map/ppermute | solution.py:565
  (13 other events, 53.1 us)

commit v4 on v3

--- a/solution.py
+++ b/solution.py
@@ -20,7 +20,7 @@
 KERNEL_US = 1.0
 WEIGHTS = {"out": 1, "in": 1, "qkv": 3, "o": 1}
 PARTS = {
-    "a": ("out", 0, 384, "y1x2", "12xy"),
+    "a": ("out", 0, 384, "y1x2", "12yx"),
     "b": ("in", 0, 1024, "y1x2", "xy12"),
     "c": ("in", 1024, 1536, "1yx2", "yx21"),
     "d": ("qkv", 0, 1152, "x2y1", "xy12"),
@@ -271,7 +271,7 @@
     gain = gain2[...].astype(F32)
     final = normal2 * gain + shift2[...].astype(F32)
     out_out[...] = final.astype(BF)
-    rows = lax.broadcasted_iota(jnp.int32, (half, width), 0) + s * half
+    rows = lax.broadcasted_iota(jnp.int32, (half, 1), 0) + s * half
     ids = segment_of(rows, lens)
     pool_out[...] = jnp.zeros_like(pool_out)
     for t in range(lens.shape[1]):
@@ -431,27 +431,46 @@
             spread_rows(whole_o, order, outs[2 * p], outs[2 * p + 1], slice(0, mine), to)
 
 
+USED = 12
+
+
 def pack_vectors(table, send, start):
-    high = table.astype(BF)
-    rest = (table - high.astype(F32)).astype(BF)
-    width = min(table.shape[1], send.shape[1])
-    row = start
-    for piece in (high, rest):
-        for c in range(0, table.shape[1], width):
-            send[row : row + 16, 0:width] = piece[:, c : c + width]
-            row += 16
-    return high.astype(F32) + rest.astype(F32)
+    total = table.shape[1]
+    high = table.astype(BF).astype(F32)
+    rest = (table - high).astype(BF).astype(F32)
+    half = total // 2
+    if send.shape[1] >= total + half:
+        more = jnp.concatenate([rest[4:8, half:], rest[8:USED, half:]], axis=1)
+        send[start : start + 16, 0:total] = jnp.concatenate([high[0:USED, :], more], axis=0).astype(BF)
+        side = jnp.concatenate([rest[0:USED, 0:half], rest[0:4, half:]], axis=0)
+        send[start : start + 16, total : total + half] = side.astype(BF)
+    else:
+        width = min(total, send.shape[1])
+        row = start
+        for piece in (high, rest):
+            for c in range(0, total, width):
+                send[row : row + 16, 0:width] = piece[:, c : c + width].astype(BF)
+                row += 16
+    return high + rest
 
 
 def unpack_vectors(got, start, total):
+    half = total // 2
+    if got.shape[1] >= total + half:
+        first = got[start : start + 16, 0:total].astype(F32)
+        side = got[start : start + 16, total : total + half].astype(F32)
+        right = jnp.concatenate([side[USED:, :], first[USED:, 0:half], first[USED:, half:]], axis=0)
+        rest = jnp.concatenate([side[0:USED, :], right], axis=1)
+        return jnp.concatenate([first[0:USED, :] + rest, jnp.zeros((16 - USED, total), F32)], axis=0)
     width = min(total, got.shape[1])
     count = total // width
     parts = [got[start + 16 * i : start + 16 * (i + 1), 0:width].astype(F32) for i in range(2 * count)]
     return jnp.concatenate([parts[i] + parts[count + i] for i in range(count)], axis=1)
 
 
-def vector_rows(total, cols):
-    return 32 * (total // min(total, cols))
+def vector_rows(total, cols, whole=False):
+    pieces = total // min(total, cols)
+    return 16 * pieces * (1 if whole or cols >= total + total // 2 else 2)
 
 
 def grad_qkv_kernel(parts, with_vectors, own, other, grads, vec_f, vec_b, vec_a, *outs):
@@ -598,9 +617,9 @@
         for part in self.parts:
             rows, cols = part.keep.shape
             half = rows // 2
-            extra = 0 if part.vec is None else vector_rows(part.vec.shape[1], cols)
+            extra = 0 if part.vec is None else vector_rows(part.vec.shape[1], cols, last)
             args += [part.got, part.keep]
-            outs += [sds((half, cols), dtype), sds((half + (extra // 2 if last else extra), cols), dtype)]
+            outs += [sds((half, cols), dtype), sds((half + extra, cols), dtype)]
             if last:
                 scratch.append(pltpu.VMEM((rows, cols), F32))
             if part.vec is None:

time: 95.4 us -> 94.7 us (level)
  waiting for transfers between devices: 37.2 us -> 30.1 us
  starting transfers between devices: 25.3 us -> 31.6 us
    ppermute x16, waiting for transfers between devices: 34.7 us -> 27.7 us  [send_to(): return lax.ppermute(x, ('dp', 'seq'), pairs)]
    ppermute x12, starting transfers between devices: 2.75 us -> 5.96 us  [swap(): return lax.ppermute(x, axis, [(0, 1), (1, 0)])]
    ppermute x16, starting transfers between devices: 22.5 us -> 25.7 us  [send_to(): return lax.ppermute(x, ('dp', 'seq'), pairs)]
  transfers between devices with their start and end apart: 28 -> 28, of which waited for: 13 -> 11; matrix products, arithmetic and copies ran while one was open for 0% -> 0% of each run, Pallas kernels for 21% -> 21%
where the time goes in v4:
time: 94.7 us; the launch traced here: 94.5 us
  starting transfers between devices  31.6 us (33%)
  Pallas kernels  31.5 us (33%)
  waiting for transfers between devices  30.1 us (32%)
  between operations  1.14 us (1%)
    pallas_call x23, Pallas kernels, call(): pl.pallas_call(body, out_shape=list(outs), in_specs=specs, out_specs=[pl....  31.5 us
    ppermute x16, waiting for transfers between devices, send_to(): return lax.ppermute(x, ('dp', 'seq'), pairs)  27.7 us
    ppermute x16, starting transfers between devices, send_to(): return lax.ppermute(x, ('dp', 'seq'), pairs)  25.7 us
    ppermute x12, starting transfers between devices, swap(): return lax.ppermute(x, axis, [(0, 1), (1, 0)])  5.96 us
    ppermute x12, waiting for transfers between devices, swap(): return lax.ppermute(x, axis, [(0, 1), (1, 0)])  2.45 us
  transfers between devices with their start and end apart: 28, of which 11 were waited for; matrix products, arithmetic and copies ran while one was open for 0% of the time, Pallas kernels for 21%

profile of v4, /device:TPU:0, one launch (start us, length us, event | category | flops | bytes accessed | tf_op | source)
XLA Modules:
  0.0 94.5 jit_solution(4192999053765241473)
XLA Ops:
  1.2 2.6 %project.1 = (bf16[256,768]{1,0:T(8,128)(2,1)S(1)}, bf16[3,768,384]{2,1,0:T(8,128)(2,1)S(1)}, f32[8,384]{1,0:T(8,128)S(1)}, f32[256,1152]{1,0:T(8,128)S(1)}) custom-call(bf16[256,768]{1,0:T(8,128)(2,1)} %bitcast.18, bf16[768,2304]{1,0:T(8,128)(2,1)} %refs_1_.1, bf16[2,768]{1,0:T(2,128)(2,1)} %refs_2_.1), custom_call_target="tpu_custom_call" | custom-call | flops 1100000000 | bytes 1024 | tf_op jit(solution)/shard_map/project/pallas_call | solution.py:78
  3.9 4.8 %attend.1 = (bf16[512,384]{1,0:T(8,128)(2,1)S(1)}, bf16[512,384]{1,0:T(8,128)(2,1)S(1)}, bf16[512,384]{1,0:T(8,128)(2,1)S(1)}, bf16[384,512]{1,0:T(8,128)(2,1)S(...) custom-call(s32[1,4]{1,0:T(1,128)S(1)} %copy-done.1, ...), custom_call_target="tpu_custom_call" | custom-call | flops 1100000000 | bytes 1024 | tf_op jit(solution)/shard_map/attend/pallas_call | solution.py:78
  10.5 5.6 %forward.1 = (bf16[256,768]{1,0:T(8,128)(2,1)S(1)}, bf16[256,3072]{1,0:T(8,128)(2,1)S(1)}, f32[256,3072]{1,0:T(8,128)S(1)}, f32[256,768]{1,0:T(8,128)S(1)}, f32[...) custom-call(s32[1,4]{1,0:T(1,128)S(1)} %copy-done.1, ...), custom_call_target="tpu_custom_call" | custom-call | flops 1100000000 | bytes 1024 | tf_op jit(solution)/shard_map/forward/pallas_call | solution.py:78
  16.7 3.3 %backward.1 = (bf16[256,1536]{1,0:T(8,128)(2,1)S(1)}, bf16[256,1536]{1,0:T(8,128)(2,1)S(1)}, f32[256,768]{1,0:T(8,128)S(1)}, bf16[256,768]{1,0:T(8,128)(2,1)S(1)}, f32[8,768]{1,0:T(8,128)S(1)}) custom-call(f32[256,768]{1,0:T(8,128)S(1)} %get-tuple-element.119.refs_0_, f32[256,3072]{1,0:T(8,128)S(1)} %get-tuple-element.120.refs_1_, ...), custom_call_target="tpu_custom_call" | custom-call | flops 1100000000 | bytes 1024 | tf_op jit(solution)/shard_map/backward/pallas_call | solution.py:78
  20.6 2.1 %grad_out.1 = (bf16[1536,384]{1,0:T(8,128)(2,1)S(1)}, bf16[1536,384]{1,0:T(8,128)(2,1)S(1)}) custom-call(bf16[256,3072]{1,0:T(8,128)(2,1)S(1)} %get-tuple-element.131.refs_0_, bf16[256,3072]{1,0:T(8,128)(2,1)S(1)} %collective-permute-done.3.refs_1_, bf16[256,384]{1,0:T(8,128)(2,1)S(1)} %get-tuple-element.132.refs_2_, ...), custom_call_target="tpu_custom_call" | custom-call | flops 1100000000 | bytes 1024 | tf_op jit(solution)/shard_map/grad_out/pallas_call | solution.py:78
  22.6 2.7 %collective-permute-start.11 = (bf16[1536,384]{1,0:T(8,128)(2,1)S(1)}, bf16[1536,384]{1,0:T(8,128)(2,1)S(1)}, u32[]{:S(2)}, u32[]{:S(2)}) collective-permute-start(bf16[1536,384]{1,0:T(8,128)(2,1)S(1)} %get-tuple-element.153), channel_id=1, source_target_pairs={{0,4},{1,9},{2,6},{3,11},{4,0},{5,13},{6,2},{7,15},{8,12},{9,1},{1... | collective-permute-start | bytes 3538952 | tf_op jit(solution)/shard_map/ppermute | solution.py:592
  25.5 3.6 %attend_back.1 = (bf16[512,1152]{1,0:T(8,128)(2,1)S(1)}, f32[8,384]{1,0:T(8,128)S(1)}) custom-call(bf16[256,768]{1,0:T(8,128)(2,1)S(1)} %get-tuple-element.124.refs_0_.refs_6_, bf16[256,768]{1,0:T(8,128)(2,1)S(1)} %collective-permute-done.2.refs_1_.refs_7_, bf16[768,768]{1,0:T(8,128)(2,1)S(1)} %get-tuple-element.115.refs_4_.refs_2_, ...), custom_call_target="tpu_custom_call" | custom-call | flops 1100000000 | bytes 1024 | tf_op jit(solution)/shard_map/attend_back/pallas_call | solution.py:78
  29.1 1.6 %grad_qkv.1 = (bf16[384,1152]{1,0:T(8,128)(2,1)S(1)}, bf16[400,1152]{1,0:T(8,128)(2,1)S(1)}, f32[16,768]{1,0:T(8,128)S(1)}) custom-call(bf16[256,768]{1,0:T(8,128)(2,1)S(1)} %get-tuple-element.110.refs_8_.refs_1_.refs_0_, bf16[256,768]{1,0:T(8,128)(2,1)S(1)} %collective-permute-done.refs_1_, ...), custom_call_target="tpu_custom_call" | custom-call | flops 1100000000 | bytes 1024 | tf_op jit(solution)/shard_map/grad_qkv/pallas_call | solution.py:78
  32.3 2.1 %grad_in.1 = (bf16[384,1024]{1,0:T(8,128)(2,1)S(1)}, bf16[384,1024]{1,0:T(8,128)(2,1)S(1)}, bf16[384,896]{1,0:T(8,128)(2,1)S(1)}, bf16[384,896]{1,0:T(8,128)(2,1)S(1)}) custom-call(bf16[256,768]{1,0:T(8,128)(2,1)S(1)} %get-tuple-element.123.refs_7_.refs_0_, bf16[256,768]{1,0:T(8,128)(2,1)S(1)} %collective-permute-done.5.refs_1_, ...), custom_call_target="tpu_custom_call" | custom-call | flops 1100000000 | bytes 1024 | tf_op jit(solution)/shard_map/grad_in/pallas_call | solution.py:78
  34.4 1.6 %collective-permute-start.8 = (bf16[384,1024]{1,0:T(8,128)(2,1)S(1)}, bf16[384,1024]{1,0:T(8,128)(2,1)S(1)}, u32[]{:S(2)}, u32[]{:S(2)}) collective-permute-start(bf16[384,1024]{1,0:T(8,128)(2,1)S(1)} %get-tuple-element.148), channel_id=1, source_target_pairs={{0,4},{1,3},{2,6},{3,1},{4,0},{5,7},{6,2},{7,5},{8,12},{9,11},{10,... | collective-permute-start | bytes 2359304 | tf_op jit(solution)/shard_map/ppermute | solution.py:592
  39.9 2.6 %collective-permute-start.12 = (bf16[768,384]{1,0:T(8,128)(2,1)S(1)}, bf16[768,384]{1,0:T(8,128)(2,1)S(1)}, u32[]{:S(2)}, u32[]{:S(2)}) collective-permute-start(bf16[768,384]{1,0:T(8,128)(2,1)S(1)} %get-tuple-element.160), channel_id=1, source_target_pairs={{0,8},{1,17},{2,10},{3,19},{4,12},{5,21},{6,14},{7,23},{8,0},{9,25... | collective-permute-start | bytes 1769480 | tf_op jit(solution)/shard_map/ppermute | solution.py:592
  42.5 11.6 %collective-permute-done.10.refs_0_ = bf16[400,1152]{1,0:T(8,128)(2,1)S(1)} collective-permute-done((bf16[400,1152]{1,0:T(8,128)(2,1)S(1)}, bf16[400,1152]{1,0:T(8,128)(2,1)S(1)}, u32[]{:S(2)}, u32[]{:S(2)}) %collective-permute-start.10) | collective-permute-done | bytes 921632 | tf_op jit(solution)/shard_map/ppermute | solution.py:592
  54.3 2.6 %collective-permute-start.16 = (bf16[208,1152]{1,0:T(8,128)(2,1)S(1)}, bf16[208,1152]{1,0:T(8,128)(2,1)S(1)}, u32[]{:S(2)}, u32[]{:S(2)}) collective-permute-start(bf16[208,1152]{1,0:T(8,128)(2,1)S(1)} %get-tuple-element.167), channel_id=1, source_target_pairs={{0,16},{1,5},{2,18},{3,7},{4,20},{5,1},{6,22},{7,3},{8,24},{9,13},... | collective-permute-start | bytes 1437704 | tf_op jit(solution)/shard_map/ppermute | solution.py:592
  57.3 1.6 %collective-permute-start.15 = (bf16[192,896]{1,0:T(8,128)(2,1)S(1)}, bf16[192,896]{1,0:T(8,128)(2,1)S(1)}, u32[]{:S(2)}, u32[]{:S(2)}) collective-permute-start(bf16[192,896]{1,0:T(8,128)(2,1)S(1)} %get-tuple-element.165), channel_id=1, source_target_pairs={{0,4},{1,3},{2,6},{3,1},{4,0},{5,7},{6,2},{7,5},{8,12},{9,11},{10,... | collective-permute-start | bytes 1032200 | tf_op jit(solution)/shard_map/ppermute | solution.py:592
  60.2 1.7 %finish_input.1 = (f32[8,128]{1,0:T(8,128)S(1)}, f32[256,768]{1,0:T(8,128)}, f32[4,768]{1,0:T(4,128)}, bf16[256,768]{1,0:T(8,128)(2,1)}) custom-call(s32[1,4]{1,0:T(1,128)S(1)} %copy-done.1, f32[256,768]{1,0:T(8,128)S(1)} %get-tuple-element.145.refs_2_.refs_1_, f32[264,768]{1,0:T(8,128)S(1)} %get-tuple-element.146.refs_2_, ...), custom_call_target="tpu_custom_call" | custom-call | flops 1100000000 | bytes 1024 | tf_op jit(solution)/shard_map/finish_input/pallas_call | solution.py:78
  61.8 3.8 %collective-permute-done.12.refs_0_ = bf16[768,384]{1,0:T(8,128)(2,1)S(1)} collective-permute-done((bf16[768,384]{1,0:T(8,128)(2,1)S(1)}, bf16[768,384]{1,0:T(8,128)(2,1)S(1)}, u32[]{:S(2)}, u32[]{:S(2)}) %collective-permute-start.12) | collective-permute-done | bytes 589856 | tf_op jit(solution)/shard_map/ppermute | solution.py:592
  65.8 3.4 %collective-permute-done.16.refs_0_ = bf16[208,1152]{1,0:T(8,128)(2,1)S(1)} collective-permute-done((bf16[208,1152]{1,0:T(8,128)(2,1)S(1)}, bf16[208,1152]{1,0:T(8,128)(2,1)S(1)}, u32[]{:S(2)}, u32[]{:S(2)}) %collective-permute-start.16) | collective-permute-done | bytes 479264 | tf_op jit(solution)/shard_map/ppermute | solution.py:592
  69.4 1.6 %collective-permute-start.20 = (bf16[112,1152]{1,0:T(8,128)(2,1)S(1)}, bf16[112,1152]{1,0:T(8,128)(2,1)S(1)}, u32[]{:S(2)}, u32[]{:S(2)}) collective-permute-start(bf16[112,1152]{1,0:T(8,128)(2,1)S(1)} %get-tuple-element.176), channel_id=1, source_target_pairs={{0,4},{1,9},{2,6},{3,11},{4,0},{5,13},{6,2},{7,15},{8,12},{9,1},{1... | collective-permute-start | bytes 774152 | tf_op jit(solution)/shard_map/ppermute | solution.py:592
  73.5 2.7 %collective-permute-start.17 = (bf16[192,384]{1,0:T(8,128)(2,1)S(1)}, bf16[192,384]{1,0:T(8,128)(2,1)S(1)}, u32[]{:S(2)}, u32[]{:S(2)}) collective-permute-start(bf16[192,384]{1,0:T(8,128)(2,1)S(1)} %get-tuple-element.171), channel_id=1, source_target_pairs={{0,16},{1,3},{2,18},{3,1},{4,20},{5,7},{6,22},{7,5},{8,24},{9,11},... | collective-permute-start | bytes 442376 | tf_op jit(solution)/shard_map/ppermute | solution.py:592
  76.5 1.6 %collective-permute-start.24 = (bf16[64,1152]{1,0:T(8,128)(2,1)S(1)}, bf16[64,1152]{1,0:T(8,128)(2,1)S(1)}, u32[]{:S(2)}, u32[]{:S(2)}) collective-permute-start(bf16[64,1152]{1,0:T(8,128)(2,1)S(1)} %get-tuple-element.185), channel_id=1, source_target_pairs={{0,8},{1,17},{2,10},{3,19},{4,12},{5,21},{6,14},{7,23},{8,0},{9,25... | collective-permute-start | bytes 442376 | tf_op jit(solution)/shard_map/ppermute | solution.py:592
  79.5 2.2 %collective-permute-start.23 = (bf16[48,896]{1,0:T(8,128)(2,1)S(1)}, bf16[48,896]{1,0:T(8,128)(2,1)S(1)}, u32[]{:S(2)}, u32[]{:S(2)}) collective-permute-start(bf16[48,896]{1,0:T(8,128)(2,1)S(1)} %get-tuple-element.183), channel_id=1, source_target_pairs={{0,16},{1,9},{2,18},{3,11},{4,20},{5,13},{6,22},{7,15},{8,24},{9,1... | collective-permute-start | bytes 258056 | tf_op jit(solution)/shard_map/ppermute | solution.py:592
  82.5 1.9 %collective-permute-done.17.refs_0_ = bf16[192,384]{1,0:T(8,128)(2,1)S(1)} collective-permute-done((bf16[192,384]{1,0:T(8,128)(2,1)S(1)}, bf16[192,384]{1,0:T(8,128)(2,1)S(1)}, u32[]{:S(2)}, u32[]{:S(2)}) %collective-permute-start.17) | collective-permute-done | bytes 147488 | tf_op jit(solution)/shard_map/ppermute | solution.py:592
  84.4 1.8 %collective-permute-start.21 = (f32[96,384]{1,0:T(8,128)S(1)}, f32[96,384]{1,0:T(8,128)S(1)}, u32[]{:S(2)}, u32[]{:S(2)}) collective-permute-start(f32[96,384]{1,0:T(8,128)S(1)} %get-tuple-element.181), channel_id=1, source_target_pairs={{0,1},{1,0},{2,3},{3,2},{4,5},{5,4},{6,7},{7,6},{8,9},{9,8},{10,11... | collective-permute-start | bytes 442376 | tf_op jit(solution)/shard_map/ppermute | solution.py:584
  87.9 3.9 %collective-permute-done.22.refs_0_ = bf16[48,1024]{1,0:T(8,128)(2,1)S(1)} collective-permute-done((bf16[48,1024]{1,0:T(8,128)(2,1)S(1)}, bf16[48,1024]{1,0:T(8,128)(2,1)S(1)}, u32[]{:S(2)}, u32[]{:S(2)}) %collective-permute-start.22) | collective-permute-done | bytes 98336 | tf_op jit(solution)/shard_map/ppermute | solution.py:592
  (80 shorter events, 20.3 us)
Async XLA Ops:
  16.1 4.5 %collective-permute-start.3 = (bf16[256,3072]{1,0:T(8,128)(2,1)S(1)}, bf16[256,3072]{1,0:T(8,128)(2,1)S(1)}, u32[]{:S(2)}, u32[]{:S(2)}) collective-permute-start(bf16[256,3072]{1,0:T(8,128)(2,1)S(1)} %get-tuple-element.131.refs_0_), channel_id=1, source_target_pairs={{0,1},{1,0},{2,3},{3,2},{4,5},{5,4},{6,7},{7,6},{8,9},{9,8},{10,11... | collective-permute-start | bytes 4718600 | tf_op jit(solution)/shard_map/ppermute | solution.py:584
  16.3 4.2 %collective-permute-start.4 = (bf16[256,384]{1,0:T(8,128)(2,1)S(1)}, bf16[256,384]{1,0:T(8,128)(2,1)S(1)}, u32[]{:S(2)}, u32[]{:S(2)}) collective-permute-start(bf16[256,384]{1,0:T(8,128)(2,1)S(1)} %get-tuple-element.133), channel_id=1, source_target_pairs={{0,1},{1,0},{2,3},{3,2},{4,5},{5,4},{6,7},{7,6},{8,9},{9,8},{10,11... | collective-permute-start | bytes 589832 | tf_op jit(solution)/shard_map/ppermute | solution.py:584
  20.0 5.6 %collective-permute-start.2 = (bf16[256,768]{1,0:T(8,128)(2,1)S(1)}, bf16[256,768]{1,0:T(8,128)(2,1)S(1)}, u32[]{:S(2)}, u32[]{:S(2)}) collective-permute-start(bf16[256,768]{1,0:T(8,128)(2,1)S(1)} %get-tuple-element.124.refs_0_.refs_6_), channel_id=1, source_target_pairs={{0,1},{1,0},{2,3},{3,2},{4,5},{5,4},{6,7},{7,6},{8,9},{9,8},{10,11... | collective-permute-start | bytes 1179656 | tf_op jit(solution)/shard_map/ppermute | solution.py:584
  20.2 12.1 %collective-permute-start.6 = (bf16[256,1536]{1,0:T(8,128)(2,1)S(1)}, bf16[256,1536]{1,0:T(8,128)(2,1)S(1)}, u32[]{:S(2)}, u32[]{:S(2)}) collective-permute-start(bf16[256,1536]{1,0:T(8,128)(2,1)S(1)} %get-tuple-element.139), channel_id=1, source_target_pairs={{0,1},{1,0},{2,3},{3,2},{4,5},{5,4},{6,7},{7,6},{8,9},{9,8},{10,11... | collective-permute-start | bytes 2359304 | tf_op jit(solution)/shard_map/ppermute | solution.py:584
  22.6 16.9 %collective-permute-start.11 = (bf16[1536,384]{1,0:T(8,128)(2,1)S(1)}, bf16[1536,384]{1,0:T(8,128)(2,1)S(1)}, u32[]{:S(2)}, u32[]{:S(2)}) collective-permute-start(bf16[1536,384]{1,0:T(8,128)(2,1)S(1)} %get-tuple-element.153), channel_id=1, source_target_pairs={{0,4},{1,9},{2,6},{3,11},{4,0},{5,13},{6,2},{7,15},{8,12},{9,1},{1... | collective-permute-start | bytes 3538952 | tf_op jit(solution)/shard_map/ppermute | solution.py:592
  25.4 6.9 %collective-permute-start.5 = (bf16[256,768]{1,0:T(8,128)(2,1)S(1)}, bf16[256,768]{1,0:T(8,128)(2,1)S(1)}, u32[]{:S(2)}, u32[]{:S(2)}) collective-permute-start(bf16[256,768]{1,0:T(8,128)(2,1)S(1)} %get-tuple-element.123.refs_7_.refs_0_), channel_id=1, source_target_pairs={{0,1},{1,0},{2,3},{3,2},{4,5},{5,4},{6,7},{7,6},{8,9},{9,8},{10,11... | collective-permute-start | bytes 1179656 | tf_op jit(solution)/shard_map/ppermute | solution.py:584
  30.7 23.3 %collective-permute-start.10 = (bf16[400,1152]{1,0:T(8,128)(2,1)S(1)}, bf16[400,1152]{1,0:T(8,128)(2,1)S(1)}, u32[]{:S(2)}, u32[]{:S(2)}) collective-permute-start(bf16[400,1152]{1,0:T(8,128)(2,1)S(1)} %get-tuple-element.151), channel_id=1, source_target_pairs={{0,2},{1,3},{2,0},{3,1},{4,6},{5,7},{6,4},{7,5},{8,10},{9,11},{10,... | collective-permute-start | bytes 2764808 | tf_op jit(solution)/shard_map/ppermute | solution.py:592
  34.4 22.5 %collective-permute-start.8 = (bf16[384,1024]{1,0:T(8,128)(2,1)S(1)}, bf16[384,1024]{1,0:T(8,128)(2,1)S(1)}, u32[]{:S(2)}, u32[]{:S(2)}) collective-permute-start(bf16[384,1024]{1,0:T(8,128)(2,1)S(1)} %get-tuple-element.148), channel_id=1, source_target_pairs={{0,4},{1,3},{2,6},{3,1},{4,0},{5,7},{6,2},{7,5},{8,12},{9,11},{10,... | collective-permute-start | bytes 2359304 | tf_op jit(solution)/shard_map/ppermute | solution.py:592
  37.5 22.7 %collective-permute-start.7 = (f32[264,768]{1,0:T(8,128)S(1)}, f32[264,768]{1,0:T(8,128)S(1)}, u32[]{:S(2)}, u32[]{:S(2)}) collective-permute-start(f32[264,768]{1,0:T(8,128)S(1)} %get-tuple-element.146.refs_2_), channel_id=1, source_target_pairs={{0,1},{1,0},{2,3},{3,2},{4,5},{5,4},{6,7},{7,6},{8,9},{9,8},{10,11... | collective-permute-start | bytes 2433032 | tf_op jit(solution)/shard_map/ppermute | solution.py:584
  37.5 19.4 %collective-permute-start.9 = (bf16[384,896]{1,0:T(8,128)(2,1)S(1)}, bf16[384,896]{1,0:T(8,128)(2,1)S(1)}, u32[]{:S(2)}, u32[]{:S(2)}) collective-permute-start(bf16[384,896]{1,0:T(8,128)(2,1)S(1)} %get-tuple-element.149), channel_id=1, source_target_pairs={{0,8},{1,5},{2,10},{3,7},{4,12},{5,1},{6,14},{7,3},{8,0},{9,13},{1... | collective-permute-start | bytes 2064392 | tf_op jit(solution)/shard_map/ppermute | solution.py:592
  39.9 25.7 %collective-permute-start.12 = (bf16[768,384]{1,0:T(8,128)(2,1)S(1)}, bf16[768,384]{1,0:T(8,128)(2,1)S(1)}, u32[]{:S(2)}, u32[]{:S(2)}) collective-permute-start(bf16[768,384]{1,0:T(8,128)(2,1)S(1)} %get-tuple-element.160), channel_id=1, source_target_pairs={{0,8},{1,17},{2,10},{3,19},{4,12},{5,21},{6,14},{7,23},{8,0},{9,25... | collective-permute-start | bytes 1769480 | tf_op jit(solution)/shard_map/ppermute | solution.py:592
  54.3 14.9 %collective-permute-start.16 = (bf16[208,1152]{1,0:T(8,128)(2,1)S(1)}, bf16[208,1152]{1,0:T(8,128)(2,1)S(1)}, u32[]{:S(2)}, u32[]{:S(2)}) collective-permute-start(bf16[208,1152]{1,0:T(8,128)(2,1)S(1)} %get-tuple-element.167), channel_id=1, source_target_pairs={{0,16},{1,5},{2,18},{3,7},{4,20},{5,1},{6,22},{7,3},{8,24},{9,13},... | collective-permute-start | bytes 1437704 | tf_op jit(solution)/shard_map/ppermute | solution.py:592
  57.3 13.7 %collective-permute-start.15 = (bf16[192,896]{1,0:T(8,128)(2,1)S(1)}, bf16[192,896]{1,0:T(8,128)(2,1)S(1)}, u32[]{:S(2)}, u32[]{:S(2)}) collective-permute-start(bf16[192,896]{1,0:T(8,128)(2,1)S(1)} %get-tuple-element.165), channel_id=1, source_target_pairs={{0,4},{1,3},{2,6},{3,1},{4,0},{5,7},{6,2},{7,5},{8,12},{9,11},{10,... | collective-permute-start | bytes 1032200 | tf_op jit(solution)/shard_map/ppermute | solution.py:592
  58.9 12.2 %collective-permute-start.14 = (bf16[192,1024]{1,0:T(8,128)(2,1)S(1)}, bf16[192,1024]{1,0:T(8,128)(2,1)S(1)}, u32[]{:S(2)}, u32[]{:S(2)}) collective-permute-start(bf16[192,1024]{1,0:T(8,128)(2,1)S(1)} %get-tuple-element.164), channel_id=1, source_target_pairs={{0,8},{1,5},{2,10},{3,7},{4,12},{5,1},{6,14},{7,3},{8,0},{9,13},{1... | collective-permute-start | bytes 1179656 | tf_op jit(solution)/shard_map/ppermute | solution.py:592
  65.8 7.6 %collective-permute-start.13 = (bf16[384,384]{1,0:T(8,128)(2,1)S(1)}, bf16[384,384]{1,0:T(8,128)(2,1)S(1)}, u32[]{:S(2)}, u32[]{:S(2)}) collective-permute-start(bf16[384,384]{1,0:T(8,128)(2,1)S(1)} %get-tuple-element.162), channel_id=1, source_target_pairs={{0,2},{1,5},{2,0},{3,7},{4,6},{5,1},{6,4},{7,3},{8,10},{9,13},{10,... | collective-permute-start | bytes 884744 | tf_op jit(solution)/shard_map/ppermute | solution.py:592
  69.4 7.0 %collective-permute-start.20 = (bf16[112,1152]{1,0:T(8,128)(2,1)S(1)}, bf16[112,1152]{1,0:T(8,128)(2,1)S(1)}, u32[]{:S(2)}, u32[]{:S(2)}) collective-permute-start(bf16[112,1152]{1,0:T(8,128)(2,1)S(1)} %get-tuple-element.176), channel_id=1, source_target_pairs={{0,4},{1,9},{2,6},{3,11},{4,0},{5,13},{6,2},{7,15},{8,12},{9,1},{1... | collective-permute-start | bytes 774152 | tf_op jit(solution)/shard_map/ppermute | solution.py:592
  71.3 6.8 %collective-permute-start.19 = (bf16[96,896]{1,0:T(8,128)(2,1)S(1)}, bf16[96,896]{1,0:T(8,128)(2,1)S(1)}, u32[]{:S(2)}, u32[]{:S(2)}) collective-permute-start(bf16[96,896]{1,0:T(8,128)(2,1)S(1)} %get-tuple-element.174), channel_id=1, source_target_pairs={{0,2},{1,17},{2,0},{3,19},{4,6},{5,21},{6,4},{7,23},{8,10},{9,25},... | collective-permute-start | bytes 516104 | tf_op jit(solution)/shard_map/ppermute | solution.py:592
  72.7 6.7 %collective-permute-start.18 = (bf16[96,1024]{1,0:T(8,128)(2,1)S(1)}, bf16[96,1024]{1,0:T(8,128)(2,1)S(1)}, u32[]{:S(2)}, u32[]{:S(2)}) collective-permute-start(bf16[96,1024]{1,0:T(8,128)(2,1)S(1)} %get-tuple-element.173), channel_id=1, source_target_pairs={{0,2},{1,9},{2,0},{3,11},{4,6},{5,13},{6,4},{7,15},{8,10},{9,1},{1... | collective-permute-start | bytes 589832 | tf_op jit(solution)/shard_map/ppermute | solution.py:592
  73.5 10.9 %collective-permute-start.17 = (bf16[192,384]{1,0:T(8,128)(2,1)S(1)}, bf16[192,384]{1,0:T(8,128)(2,1)S(1)}, u32[]{:S(2)}, u32[]{:S(2)}) collective-permute-start(bf16[192,384]{1,0:T(8,128)(2,1)S(1)} %get-tuple-element.171), channel_id=1, source_target_pairs={{0,16},{1,3},{2,18},{3,1},{4,20},{5,7},{6,22},{7,5},{8,24},{9,11},... | collective-permute-start | bytes 442376 | tf_op jit(solution)/shard_map/ppermute | solution.py:592
  76.5 9.7 %collective-permute-start.24 = (bf16[64,1152]{1,0:T(8,128)(2,1)S(1)}, bf16[64,1152]{1,0:T(8,128)(2,1)S(1)}, u32[]{:S(2)}, u32[]{:S(2)}) collective-permute-start(bf16[64,1152]{1,0:T(8,128)(2,1)S(1)} %get-tuple-element.185), channel_id=1, source_target_pairs={{0,8},{1,17},{2,10},{3,19},{4,12},{5,21},{6,14},{7,23},{8,0},{9,25... | collective-permute-start | bytes 442376 | tf_op jit(solution)/shard_map/ppermute | solution.py:592
  79.5 8.4 %collective-permute-start.23 = (bf16[48,896]{1,0:T(8,128)(2,1)S(1)}, bf16[48,896]{1,0:T(8,128)(2,1)S(1)}, u32[]{:S(2)}, u32[]{:S(2)}) collective-permute-start(bf16[48,896]{1,0:T(8,128)(2,1)S(1)} %get-tuple-element.183), channel_id=1, source_target_pairs={{0,16},{1,9},{2,18},{3,11},{4,20},{5,13},{6,22},{7,15},{8,24},{9,1... | collective-permute-start | bytes 258056 | tf_op jit(solution)/shard_map/ppermute | solution.py:592
  81.7 10.0 %collective-permute-start.22 = (bf16[48,1024]{1,0:T(8,128)(2,1)S(1)}, bf16[48,1024]{1,0:T(8,128)(2,1)S(1)}, u32[]{:S(2)}, u32[]{:S(2)}) collective-permute-start(bf16[48,1024]{1,0:T(8,128)(2,1)S(1)} %get-tuple-element.182), channel_id=1, source_target_pairs={{0,16},{1,17},{2,18},{3,19},{4,20},{5,21},{6,22},{7,23},{8,24},{9,... | collective-permute-start | bytes 294920 | tf_op jit(solution)/shard_map/ppermute | solution.py:592
  84.4 8.9 %collective-permute-start.21 = (f32[96,384]{1,0:T(8,128)S(1)}, f32[96,384]{1,0:T(8,128)S(1)}, u32[]{:S(2)}, u32[]{:S(2)}) collective-permute-start(f32[96,384]{1,0:T(8,128)S(1)} %get-tuple-element.181), channel_id=1, source_target_pairs={{0,1},{1,0},{2,3},{3,2},{4,5},{5,4},{6,7},{7,6},{8,9},{9,8},{10,11... | collective-permute-start | bytes 442376 | tf_op jit(solution)/shard_map/ppermute | solution.py:584
  86.3 7.0 %collective-permute-start.27 = (f32[40,1152]{1,0:T(8,128)S(1)}, f32[40,1152]{1,0:T(8,128)S(1)}, u32[]{:S(2)}, u32[]{:S(2)}) collective-permute-start(f32[40,1152]{1,0:T(8,128)S(1)} %get-tuple-element.192.refs_10_), channel_id=1, source_target_pairs={{0,1},{1,0},{2,3},{3,2},{4,5},{5,4},{6,7},{7,6},{8,9},{9,8},{10,11... | collective-permute-start | bytes 552968 | tf_op jit(solution)/shard_map/ppermute | solution.py:584
  (13 other events, 53.0 us)

commit v5 on v4

--- a/solution.py
+++ b/solution.py
@@ -257,7 +257,7 @@
     normal_out[...] = normal
     inverse_out[...] = inverse
     down_acc[...] = middle + b_out[...].astype(F32)
-    step = 1024
+    step = 1536
     for c in range(0, ff, step):
         cols = slice(c, c + step)
         upper = nn(low, w_in[:, cols]) + b_in[:, cols].astype(F32)

time: 94.7 us -> 94.6 us (level)
  no operation moved by 1% of the time
where the time goes in v5:
time: 94.6 us; the launch traced here: 94.5 us
  starting transfers between devices  31.6 us (33%)
  Pallas kernels  31.5 us (33%)
  waiting for transfers between devices  30.1 us (32%)
  between operations  1.14 us (1%)
    pallas_call x23, Pallas kernels, call(): pl.pallas_call(body, out_shape=list(outs), in_specs=specs, out_specs=[pl....  31.5 us
    ppermute x16, waiting for transfers between devices, send_to(): return lax.ppermute(x, ('dp', 'seq'), pairs)  27.7 us
    ppermute x16, starting transfers between devices, send_to(): return lax.ppermute(x, ('dp', 'seq'), pairs)  25.6 us
    ppermute x12, starting transfers between devices, swap(): return lax.ppermute(x, axis, [(0, 1), (1, 0)])  5.96 us
    ppermute x12, waiting for transfers between devices, swap(): return lax.ppermute(x, axis, [(0, 1), (1, 0)])  2.45 us
  transfers between devices with their start and end apart: 28, of which 11 were waited for; matrix products, arithmetic and copies ran while one was open for 0% of the time, Pallas kernels for 21%

profile of v5, /device:TPU:0, one launch (start us, length us, event | category | flops | bytes accessed | tf_op | source)
XLA Modules:
  0.0 94.5 jit_solution(13718843984505255673)
XLA Ops:
  1.2 2.6 %project.1 = (bf16[256,768]{1,0:T(8,128)(2,1)S(1)}, bf16[3,768,384]{2,1,0:T(8,128)(2,1)S(1)}, f32[8,384]{1,0:T(8,128)S(1)}, f32[256,1152]{1,0:T(8,128)S(1)}) custom-call(bf16[256,768]{1,0:T(8,128)(2,1)} %bitcast.18, bf16[768,2304]{1,0:T(8,128)(2,1)} %refs_1_.1, bf16[2,768]{1,0:T(2,128)(2,1)} %refs_2_.1), custom_call_target="tpu_custom_call" | custom-call | flops 1100000000 | bytes 1024 | tf_op jit(solution)/shard_map/project/pallas_call | solution.py:78
  3.9 4.8 %attend.1 = (bf16[512,384]{1,0:T(8,128)(2,1)S(1)}, bf16[512,384]{1,0:T(8,128)(2,1)S(1)}, bf16[512,384]{1,0:T(8,128)(2,1)S(1)}, bf16[384,512]{1,0:T(8,128)(2,1)S(...) custom-call(s32[1,4]{1,0:T(1,128)S(1)} %copy-done.1, ...), custom_call_target="tpu_custom_call" | custom-call | flops 1100000000 | bytes 1024 | tf_op jit(solution)/shard_map/attend/pallas_call | solution.py:78
  10.5 5.6 %forward.1 = (bf16[256,768]{1,0:T(8,128)(2,1)S(1)}, bf16[256,3072]{1,0:T(8,128)(2,1)S(1)}, f32[256,3072]{1,0:T(8,128)S(1)}, f32[256,768]{1,0:T(8,128)S(1)}, f32[...) custom-call(s32[1,4]{1,0:T(1,128)S(1)} %copy-done.1, ...), custom_call_target="tpu_custom_call" | custom-call | flops 1100000000 | bytes 1024 | tf_op jit(solution)/shard_map/forward/pallas_call | solution.py:78
  16.6 3.3 %backward.1 = (bf16[256,1536]{1,0:T(8,128)(2,1)S(1)}, bf16[256,1536]{1,0:T(8,128)(2,1)S(1)}, f32[256,768]{1,0:T(8,128)S(1)}, bf16[256,768]{1,0:T(8,128)(2,1)S(1)}, f32[8,768]{1,0:T(8,128)S(1)}) custom-call(f32[256,768]{1,0:T(8,128)S(1)} %get-tuple-element.119.refs_0_, f32[256,3072]{1,0:T(8,128)S(1)} %get-tuple-element.120.refs_1_, ...), custom_call_target="tpu_custom_call" | custom-call | flops 1100000000 | bytes 1024 | tf_op jit(solution)/shard_map/backward/pallas_call | solution.py:78
  20.5 2.1 %grad_out.1 = (bf16[1536,384]{1,0:T(8,128)(2,1)S(1)}, bf16[1536,384]{1,0:T(8,128)(2,1)S(1)}) custom-call(bf16[256,3072]{1,0:T(8,128)(2,1)S(1)} %get-tuple-element.131.refs_0_, bf16[256,3072]{1,0:T(8,128)(2,1)S(1)} %collective-permute-done.3.refs_1_, bf16[256,384]{1,0:T(8,128)(2,1)S(1)} %get-tuple-element.132.refs_2_, ...), custom_call_target="tpu_custom_call" | custom-call | flops 1100000000 | bytes 1024 | tf_op jit(solution)/shard_map/grad_out/pallas_call | solution.py:78
  22.6 2.8 %collective-permute-start.11 = (bf16[1536,384]{1,0:T(8,128)(2,1)S(1)}, bf16[1536,384]{1,0:T(8,128)(2,1)S(1)}, u32[]{:S(2)}, u32[]{:S(2)}) collective-permute-start(bf16[1536,384]{1,0:T(8,128)(2,1)S(1)} %get-tuple-element.153), channel_id=1, source_target_pairs={{0,4},{1,9},{2,6},{3,11},{4,0},{5,13},{6,2},{7,15},{8,12},{9,1},{1... | collective-permute-start | bytes 3538952 | tf_op jit(solution)/shard_map/ppermute | solution.py:592
  25.5 3.6 %attend_back.1 = (bf16[512,1152]{1,0:T(8,128)(2,1)S(1)}, f32[8,384]{1,0:T(8,128)S(1)}) custom-call(bf16[256,768]{1,0:T(8,128)(2,1)S(1)} %get-tuple-element.124.refs_0_.refs_6_, bf16[256,768]{1,0:T(8,128)(2,1)S(1)} %collective-permute-done.2.refs_1_.refs_7_, bf16[768,768]{1,0:T(8,128)(2,1)S(1)} %get-tuple-element.115.refs_4_.refs_2_, ...), custom_call_target="tpu_custom_call" | custom-call | flops 1100000000 | bytes 1024 | tf_op jit(solution)/shard_map/attend_back/pallas_call | solution.py:78
  29.1 1.6 %grad_qkv.1 = (bf16[384,1152]{1,0:T(8,128)(2,1)S(1)}, bf16[400,1152]{1,0:T(8,128)(2,1)S(1)}, f32[16,768]{1,0:T(8,128)S(1)}) custom-call(bf16[256,768]{1,0:T(8,128)(2,1)S(1)} %get-tuple-element.110.refs_8_.refs_1_.refs_0_, bf16[256,768]{1,0:T(8,128)(2,1)S(1)} %collective-permute-done.refs_1_, ...), custom_call_target="tpu_custom_call" | custom-call | flops 1100000000 | bytes 1024 | tf_op jit(solution)/shard_map/grad_qkv/pallas_call | solution.py:78
  32.3 2.1 %grad_in.1 = (bf16[384,1024]{1,0:T(8,128)(2,1)S(1)}, bf16[384,1024]{1,0:T(8,128)(2,1)S(1)}, bf16[384,896]{1,0:T(8,128)(2,1)S(1)}, bf16[384,896]{1,0:T(8,128)(2,1)S(1)}) custom-call(bf16[256,768]{1,0:T(8,128)(2,1)S(1)} %get-tuple-element.123.refs_7_.refs_0_, bf16[256,768]{1,0:T(8,128)(2,1)S(1)} %collective-permute-done.5.refs_1_, ...), custom_call_target="tpu_custom_call" | custom-call | flops 1100000000 | bytes 1024 | tf_op jit(solution)/shard_map/grad_in/pallas_call | solution.py:78
  39.8 2.6 %collective-permute-start.12 = (bf16[768,384]{1,0:T(8,128)(2,1)S(1)}, bf16[768,384]{1,0:T(8,128)(2,1)S(1)}, u32[]{:S(2)}, u32[]{:S(2)}) collective-permute-start(bf16[768,384]{1,0:T(8,128)(2,1)S(1)} %get-tuple-element.160), channel_id=1, source_target_pairs={{0,8},{1,17},{2,10},{3,19},{4,12},{5,21},{6,14},{7,23},{8,0},{9,25... | collective-permute-start | bytes 1769480 | tf_op jit(solution)/shard_map/ppermute | solution.py:592
  42.4 11.6 %collective-permute-done.10.refs_0_ = bf16[400,1152]{1,0:T(8,128)(2,1)S(1)} collective-permute-done((bf16[400,1152]{1,0:T(8,128)(2,1)S(1)}, bf16[400,1152]{1,0:T(8,128)(2,1)S(1)}, u32[]{:S(2)}, u32[]{:S(2)}) %collective-permute-start.10) | collective-permute-done | bytes 921632 | tf_op jit(solution)/shard_map/ppermute | solution.py:592
  54.3 2.6 %collective-permute-start.16 = (bf16[208,1152]{1,0:T(8,128)(2,1)S(1)}, bf16[208,1152]{1,0:T(8,128)(2,1)S(1)}, u32[]{:S(2)}, u32[]{:S(2)}) collective-permute-start(bf16[208,1152]{1,0:T(8,128)(2,1)S(1)} %get-tuple-element.167), channel_id=1, source_target_pairs={{0,16},{1,5},{2,18},{3,7},{4,20},{5,1},{6,22},{7,3},{8,24},{9,13},... | collective-permute-start | bytes 1437704 | tf_op jit(solution)/shard_map/ppermute | solution.py:592
  57.3 1.6 %collective-permute-start.15 = (bf16[192,896]{1,0:T(8,128)(2,1)S(1)}, bf16[192,896]{1,0:T(8,128)(2,1)S(1)}, u32[]{:S(2)}, u32[]{:S(2)}) collective-permute-start(bf16[192,896]{1,0:T(8,128)(2,1)S(1)} %get-tuple-element.165), channel_id=1, source_target_pairs={{0,4},{1,3},{2,6},{3,1},{4,0},{5,7},{6,2},{7,5},{8,12},{9,11},{10,... | collective-permute-start | bytes 1032200 | tf_op jit(solution)/shard_map/ppermute | solution.py:592
  60.1 1.7 %finish_input.1 = (f32[8,128]{1,0:T(8,128)S(1)}, f32[256,768]{1,0:T(8,128)}, f32[4,768]{1,0:T(4,128)}, bf16[256,768]{1,0:T(8,128)(2,1)}) custom-call(s32[1,4]{1,0:T(1,128)S(1)} %copy-done.1, f32[256,768]{1,0:T(8,128)S(1)} %get-tuple-element.145.refs_2_.refs_1_, f32[264,768]{1,0:T(8,128)S(1)} %get-tuple-element.146.refs_2_, ...), custom_call_target="tpu_custom_call" | custom-call | flops 1100000000 | bytes 1024 | tf_op jit(solution)/shard_map/finish_input/pallas_call | solution.py:78
  61.8 3.7 %collective-permute-done.12.refs_0_ = bf16[768,384]{1,0:T(8,128)(2,1)S(1)} collective-permute-done((bf16[768,384]{1,0:T(8,128)(2,1)S(1)}, bf16[768,384]{1,0:T(8,128)(2,1)S(1)}, u32[]{:S(2)}, u32[]{:S(2)}) %collective-permute-start.12) | collective-permute-done | bytes 589856 | tf_op jit(solution)/shard_map/ppermute | solution.py:592
  65.8 3.4 %collective-permute-done.16.refs_0_ = bf16[208,1152]{1,0:T(8,128)(2,1)S(1)} collective-permute-done((bf16[208,1152]{1,0:T(8,128)(2,1)S(1)}, bf16[208,1152]{1,0:T(8,128)(2,1)S(1)}, u32[]{:S(2)}, u32[]{:S(2)}) %collective-permute-start.16) | collective-permute-done | bytes 479264 | tf_op jit(solution)/shard_map/ppermute | solution.py:592
  69.3 1.6 %collective-permute-start.20 = (bf16[112,1152]{1,0:T(8,128)(2,1)S(1)}, bf16[112,1152]{1,0:T(8,128)(2,1)S(1)}, u32[]{:S(2)}, u32[]{:S(2)}) collective-permute-start(bf16[112,1152]{1,0:T(8,128)(2,1)S(1)} %get-tuple-element.176), channel_id=1, source_target_pairs={{0,4},{1,9},{2,6},{3,11},{4,0},{5,13},{6,2},{7,15},{8,12},{9,1},{1... | collective-permute-start | bytes 774152 | tf_op jit(solution)/shard_map/ppermute | solution.py:592
  73.4 2.7 %collective-permute-start.17 = (bf16[192,384]{1,0:T(8,128)(2,1)S(1)}, bf16[192,384]{1,0:T(8,128)(2,1)S(1)}, u32[]{:S(2)}, u32[]{:S(2)}) collective-permute-start(bf16[192,384]{1,0:T(8,128)(2,1)S(1)} %get-tuple-element.171), channel_id=1, source_target_pairs={{0,16},{1,3},{2,18},{3,1},{4,20},{5,7},{6,22},{7,5},{8,24},{9,11},... | collective-permute-start | bytes 442376 | tf_op jit(solution)/shard_map/ppermute | solution.py:592
  76.5 1.6 %collective-permute-start.24 = (bf16[64,1152]{1,0:T(8,128)(2,1)S(1)}, bf16[64,1152]{1,0:T(8,128)(2,1)S(1)}, u32[]{:S(2)}, u32[]{:S(2)}) collective-permute-start(bf16[64,1152]{1,0:T(8,128)(2,1)S(1)} %get-tuple-element.185), channel_id=1, source_target_pairs={{0,8},{1,17},{2,10},{3,19},{4,12},{5,21},{6,14},{7,23},{8,0},{9,25... | collective-permute-start | bytes 442376 | tf_op jit(solution)/shard_map/ppermute | solution.py:592
  79.3 2.3 %collective-permute-start.23 = (bf16[48,896]{1,0:T(8,128)(2,1)S(1)}, bf16[48,896]{1,0:T(8,128)(2,1)S(1)}, u32[]{:S(2)}, u32[]{:S(2)}) collective-permute-start(bf16[48,896]{1,0:T(8,128)(2,1)S(1)} %get-tuple-element.183), channel_id=1, source_target_pairs={{0,16},{1,9},{2,18},{3,11},{4,20},{5,13},{6,22},{7,15},{8,24},{9,1... | collective-permute-start | bytes 258056 | tf_op jit(solution)/shard_map/ppermute | solution.py:592
  82.3 2.0 %collective-permute-done.17.refs_0_ = bf16[192,384]{1,0:T(8,128)(2,1)S(1)} collective-permute-done((bf16[192,384]{1,0:T(8,128)(2,1)S(1)}, bf16[192,384]{1,0:T(8,128)(2,1)S(1)}, u32[]{:S(2)}, u32[]{:S(2)}) %collective-permute-start.17) | collective-permute-done | bytes 147488 | tf_op jit(solution)/shard_map/ppermute | solution.py:592
  84.4 1.7 %collective-permute-start.21 = (f32[96,384]{1,0:T(8,128)S(1)}, f32[96,384]{1,0:T(8,128)S(1)}, u32[]{:S(2)}, u32[]{:S(2)}) collective-permute-start(f32[96,384]{1,0:T(8,128)S(1)} %get-tuple-element.181), channel_id=1, source_target_pairs={{0,1},{1,0},{2,3},{3,2},{4,5},{5,4},{6,7},{7,6},{8,9},{9,8},{10,11... | collective-permute-start | bytes 442376 | tf_op jit(solution)/shard_map/ppermute | solution.py:584
  86.2 1.6 %collective-permute-start.27 = (f32[40,1152]{1,0:T(8,128)S(1)}, f32[40,1152]{1,0:T(8,128)S(1)}, u32[]{:S(2)}, u32[]{:S(2)}) collective-permute-start(f32[40,1152]{1,0:T(8,128)S(1)} %get-tuple-element.192.refs_10_), channel_id=1, source_target_pairs={{0,1},{1,0},{2,3},{3,2},{4,5},{5,4},{6,7},{7,6},{8,9},{9,8},{10,11... | collective-permute-start | bytes 552968 | tf_op jit(solution)/shard_map/ppermute | solution.py:584
  87.8 3.9 %collective-permute-done.22.refs_0_ = bf16[48,1024]{1,0:T(8,128)(2,1)S(1)} collective-permute-done((bf16[48,1024]{1,0:T(8,128)(2,1)S(1)}, bf16[48,1024]{1,0:T(8,128)(2,1)S(1)}, u32[]{:S(2)}, u32[]{:S(2)}) %collective-permute-start.22) | collective-permute-done | bytes 98336 | tf_op jit(solution)/shard_map/ppermute | solution.py:592
  (80 shorter events, 20.2 us)
Async XLA Ops:
  16.0 4.5 %collective-permute-start.3 = (bf16[256,3072]{1,0:T(8,128)(2,1)S(1)}, bf16[256,3072]{1,0:T(8,128)(2,1)S(1)}, u32[]{:S(2)}, u32[]{:S(2)}) collective-permute-start(bf16[256,3072]{1,0:T(8,128)(2,1)S(1)} %get-tuple-element.131.refs_0_), channel_id=1, source_target_pairs={{0,1},{1,0},{2,3},{3,2},{4,5},{5,4},{6,7},{7,6},{8,9},{9,8},{10,11... | collective-permute-start | bytes 4718600 | tf_op jit(solution)/shard_map/ppermute | solution.py:584
  16.3 4.3 %collective-permute-start.4 = (bf16[256,384]{1,0:T(8,128)(2,1)S(1)}, bf16[256,384]{1,0:T(8,128)(2,1)S(1)}, u32[]{:S(2)}, u32[]{:S(2)}) collective-permute-start(bf16[256,384]{1,0:T(8,128)(2,1)S(1)} %get-tuple-element.133), channel_id=1, source_target_pairs={{0,1},{1,0},{2,3},{3,2},{4,5},{5,4},{6,7},{7,6},{8,9},{9,8},{10,11... | collective-permute-start | bytes 589832 | tf_op jit(solution)/shard_map/ppermute | solution.py:584
  19.9 5.5 %collective-permute-start.2 = (bf16[256,768]{1,0:T(8,128)(2,1)S(1)}, bf16[256,768]{1,0:T(8,128)(2,1)S(1)}, u32[]{:S(2)}, u32[]{:S(2)}) collective-permute-start(bf16[256,768]{1,0:T(8,128)(2,1)S(1)} %get-tuple-element.124.refs_0_.refs_6_), channel_id=1, source_target_pairs={{0,1},{1,0},{2,3},{3,2},{4,5},{5,4},{6,7},{7,6},{8,9},{9,8},{10,11... | collective-permute-start | bytes 1179656 | tf_op jit(solution)/shard_map/ppermute | solution.py:584
  20.2 12.1 %collective-permute-start.6 = (bf16[256,1536]{1,0:T(8,128)(2,1)S(1)}, bf16[256,1536]{1,0:T(8,128)(2,1)S(1)}, u32[]{:S(2)}, u32[]{:S(2)}) collective-permute-start(bf16[256,1536]{1,0:T(8,128)(2,1)S(1)} %get-tuple-element.139), channel_id=1, source_target_pairs={{0,1},{1,0},{2,3},{3,2},{4,5},{5,4},{6,7},{7,6},{8,9},{9,8},{10,11... | collective-permute-start | bytes 2359304 | tf_op jit(solution)/shard_map/ppermute | solution.py:584
  22.6 16.9 %collective-permute-start.11 = (bf16[1536,384]{1,0:T(8,128)(2,1)S(1)}, bf16[1536,384]{1,0:T(8,128)(2,1)S(1)}, u32[]{:S(2)}, u32[]{:S(2)}) collective-permute-start(bf16[1536,384]{1,0:T(8,128)(2,1)S(1)} %get-tuple-element.153), channel_id=1, source_target_pairs={{0,4},{1,9},{2,6},{3,11},{4,0},{5,13},{6,2},{7,15},{8,12},{9,1},{1... | collective-permute-start | bytes 3538952 | tf_op jit(solution)/shard_map/ppermute | solution.py:592
  25.3 6.9 %collective-permute-start.5 = (bf16[256,768]{1,0:T(8,128)(2,1)S(1)}, bf16[256,768]{1,0:T(8,128)(2,1)S(1)}, u32[]{:S(2)}, u32[]{:S(2)}) collective-permute-start(bf16[256,768]{1,0:T(8,128)(2,1)S(1)} %get-tuple-element.123.refs_7_.refs_0_), channel_id=1, source_target_pairs={{0,1},{1,0},{2,3},{3,2},{4,5},{5,4},{6,7},{7,6},{8,9},{9,8},{10,11... | collective-permute-start | bytes 1179656 | tf_op jit(solution)/shard_map/ppermute | solution.py:584
  30.7 23.3 %collective-permute-start.10 = (bf16[400,1152]{1,0:T(8,128)(2,1)S(1)}, bf16[400,1152]{1,0:T(8,128)(2,1)S(1)}, u32[]{:S(2)}, u32[]{:S(2)}) collective-permute-start(bf16[400,1152]{1,0:T(8,128)(2,1)S(1)} %get-tuple-element.151), channel_id=1, source_target_pairs={{0,2},{1,3},{2,0},{3,1},{4,6},{5,7},{6,4},{7,5},{8,10},{9,11},{10,... | collective-permute-start | bytes 2764808 | tf_op jit(solution)/shard_map/ppermute | solution.py:592
  34.4 22.5 %collective-permute-start.8 = (bf16[384,1024]{1,0:T(8,128)(2,1)S(1)}, bf16[384,1024]{1,0:T(8,128)(2,1)S(1)}, u32[]{:S(2)}, u32[]{:S(2)}) collective-permute-start(bf16[384,1024]{1,0:T(8,128)(2,1)S(1)} %get-tuple-element.148), channel_id=1, source_target_pairs={{0,4},{1,3},{2,6},{3,1},{4,0},{5,7},{6,2},{7,5},{8,12},{9,11},{10,... | collective-permute-start | bytes 2359304 | tf_op jit(solution)/shard_map/ppermute | solution.py:592
  37.4 22.7 %collective-permute-start.7 = (f32[264,768]{1,0:T(8,128)S(1)}, f32[264,768]{1,0:T(8,128)S(1)}, u32[]{:S(2)}, u32[]{:S(2)}) collective-permute-start(f32[264,768]{1,0:T(8,128)S(1)} %get-tuple-element.146.refs_2_), channel_id=1, source_target_pairs={{0,1},{1,0},{2,3},{3,2},{4,5},{5,4},{6,7},{7,6},{8,9},{9,8},{10,11... | collective-permute-start | bytes 2433032 | tf_op jit(solution)/shard_map/ppermute | solution.py:584
  37.5 19.4 %collective-permute-start.9 = (bf16[384,896]{1,0:T(8,128)(2,1)S(1)}, bf16[384,896]{1,0:T(8,128)(2,1)S(1)}, u32[]{:S(2)}, u32[]{:S(2)}) collective-permute-start(bf16[384,896]{1,0:T(8,128)(2,1)S(1)} %get-tuple-element.149), channel_id=1, source_target_pairs={{0,8},{1,5},{2,10},{3,7},{4,12},{5,1},{6,14},{7,3},{8,0},{9,13},{1... | collective-permute-start | bytes 2064392 | tf_op jit(solution)/shard_map/ppermute | solution.py:592
  39.8 25.7 %collective-permute-start.12 = (bf16[768,384]{1,0:T(8,128)(2,1)S(1)}, bf16[768,384]{1,0:T(8,128)(2,1)S(1)}, u32[]{:S(2)}, u32[]{:S(2)}) collective-permute-start(bf16[768,384]{1,0:T(8,128)(2,1)S(1)} %get-tuple-element.160), channel_id=1, source_target_pairs={{0,8},{1,17},{2,10},{3,19},{4,12},{5,21},{6,14},{7,23},{8,0},{9,25... | collective-permute-start | bytes 1769480 | tf_op jit(solution)/shard_map/ppermute | solution.py:592
  54.3 14.9 %collective-permute-start.16 = (bf16[208,1152]{1,0:T(8,128)(2,1)S(1)}, bf16[208,1152]{1,0:T(8,128)(2,1)S(1)}, u32[]{:S(2)}, u32[]{:S(2)}) collective-permute-start(bf16[208,1152]{1,0:T(8,128)(2,1)S(1)} %get-tuple-element.167), channel_id=1, source_target_pairs={{0,16},{1,5},{2,18},{3,7},{4,20},{5,1},{6,22},{7,3},{8,24},{9,13},... | collective-permute-start | bytes 1437704 | tf_op jit(solution)/shard_map/ppermute | solution.py:592
  57.3 13.7 %collective-permute-start.15 = (bf16[192,896]{1,0:T(8,128)(2,1)S(1)}, bf16[192,896]{1,0:T(8,128)(2,1)S(1)}, u32[]{:S(2)}, u32[]{:S(2)}) collective-permute-start(bf16[192,896]{1,0:T(8,128)(2,1)S(1)} %get-tuple-element.165), channel_id=1, source_target_pairs={{0,4},{1,3},{2,6},{3,1},{4,0},{5,7},{6,2},{7,5},{8,12},{9,11},{10,... | collective-permute-start | bytes 1032200 | tf_op jit(solution)/shard_map/ppermute | solution.py:592
  58.9 12.1 %collective-permute-start.14 = (bf16[192,1024]{1,0:T(8,128)(2,1)S(1)}, bf16[192,1024]{1,0:T(8,128)(2,1)S(1)}, u32[]{:S(2)}, u32[]{:S(2)}) collective-permute-start(bf16[192,1024]{1,0:T(8,128)(2,1)S(1)} %get-tuple-element.164), channel_id=1, source_target_pairs={{0,8},{1,5},{2,10},{3,7},{4,12},{5,1},{6,14},{7,3},{8,0},{9,13},{1... | collective-permute-start | bytes 1179656 | tf_op jit(solution)/shard_map/ppermute | solution.py:592
  65.7 7.6 %collective-permute-start.13 = (bf16[384,384]{1,0:T(8,128)(2,1)S(1)}, bf16[384,384]{1,0:T(8,128)(2,1)S(1)}, u32[]{:S(2)}, u32[]{:S(2)}) collective-permute-start(bf16[384,384]{1,0:T(8,128)(2,1)S(1)} %get-tuple-element.162), channel_id=1, source_target_pairs={{0,2},{1,5},{2,0},{3,7},{4,6},{5,1},{6,4},{7,3},{8,10},{9,13},{10,... | collective-permute-start | bytes 884744 | tf_op jit(solution)/shard_map/ppermute | solution.py:592
  69.3 7.0 %collective-permute-start.20 = (bf16[112,1152]{1,0:T(8,128)(2,1)S(1)}, bf16[112,1152]{1,0:T(8,128)(2,1)S(1)}, u32[]{:S(2)}, u32[]{:S(2)}) collective-permute-start(bf16[112,1152]{1,0:T(8,128)(2,1)S(1)} %get-tuple-element.176), channel_id=1, source_target_pairs={{0,4},{1,9},{2,6},{3,11},{4,0},{5,13},{6,2},{7,15},{8,12},{9,1},{1... | collective-permute-start | bytes 774152 | tf_op jit(solution)/shard_map/ppermute | solution.py:592
  71.2 6.9 %collective-permute-start.19 = (bf16[96,896]{1,0:T(8,128)(2,1)S(1)}, bf16[96,896]{1,0:T(8,128)(2,1)S(1)}, u32[]{:S(2)}, u32[]{:S(2)}) collective-permute-start(bf16[96,896]{1,0:T(8,128)(2,1)S(1)} %get-tuple-element.174), channel_id=1, source_target_pairs={{0,2},{1,17},{2,0},{3,19},{4,6},{5,21},{6,4},{7,23},{8,10},{9,25},... | collective-permute-start | bytes 516104 | tf_op jit(solution)/shard_map/ppermute | solution.py:592
  72.7 6.6 %collective-permute-start.18 = (bf16[96,1024]{1,0:T(8,128)(2,1)S(1)}, bf16[96,1024]{1,0:T(8,128)(2,1)S(1)}, u32[]{:S(2)}, u32[]{:S(2)}) collective-permute-start(bf16[96,1024]{1,0:T(8,128)(2,1)S(1)} %get-tuple-element.173), channel_id=1, source_target_pairs={{0,2},{1,9},{2,0},{3,11},{4,6},{5,13},{6,4},{7,15},{8,10},{9,1},{1... | collective-permute-start | bytes 589832 | tf_op jit(solution)/shard_map/ppermute | solution.py:592
  73.4 11.0 %collective-permute-start.17 = (bf16[192,384]{1,0:T(8,128)(2,1)S(1)}, bf16[192,384]{1,0:T(8,128)(2,1)S(1)}, u32[]{:S(2)}, u32[]{:S(2)}) collective-permute-start(bf16[192,384]{1,0:T(8,128)(2,1)S(1)} %get-tuple-element.171), channel_id=1, source_target_pairs={{0,16},{1,3},{2,18},{3,1},{4,20},{5,7},{6,22},{7,5},{8,24},{9,11},... | collective-permute-start | bytes 442376 | tf_op jit(solution)/shard_map/ppermute | solution.py:592
  76.5 9.7 %collective-permute-start.24 = (bf16[64,1152]{1,0:T(8,128)(2,1)S(1)}, bf16[64,1152]{1,0:T(8,128)(2,1)S(1)}, u32[]{:S(2)}, u32[]{:S(2)}) collective-permute-start(bf16[64,1152]{1,0:T(8,128)(2,1)S(1)} %get-tuple-element.185), channel_id=1, source_target_pairs={{0,8},{1,17},{2,10},{3,19},{4,12},{5,21},{6,14},{7,23},{8,0},{9,25... | collective-permute-start | bytes 442376 | tf_op jit(solution)/shard_map/ppermute | solution.py:592
  79.3 8.5 %collective-permute-start.23 = (bf16[48,896]{1,0:T(8,128)(2,1)S(1)}, bf16[48,896]{1,0:T(8,128)(2,1)S(1)}, u32[]{:S(2)}, u32[]{:S(2)}) collective-permute-start(bf16[48,896]{1,0:T(8,128)(2,1)S(1)} %get-tuple-element.183), channel_id=1, source_target_pairs={{0,16},{1,9},{2,18},{3,11},{4,20},{5,13},{6,22},{7,15},{8,24},{9,1... | collective-permute-start | bytes 258056 | tf_op jit(solution)/shard_map/ppermute | solution.py:592
  81.6 10.1 %collective-permute-start.22 = (bf16[48,1024]{1,0:T(8,128)(2,1)S(1)}, bf16[48,1024]{1,0:T(8,128)(2,1)S(1)}, u32[]{:S(2)}, u32[]{:S(2)}) collective-permute-start(bf16[48,1024]{1,0:T(8,128)(2,1)S(1)} %get-tuple-element.182), channel_id=1, source_target_pairs={{0,16},{1,17},{2,18},{3,19},{4,20},{5,21},{6,22},{7,23},{8,24},{9,... | collective-permute-start | bytes 294920 | tf_op jit(solution)/shard_map/ppermute | solution.py:592
  84.4 8.9 %collective-permute-start.21 = (f32[96,384]{1,0:T(8,128)S(1)}, f32[96,384]{1,0:T(8,128)S(1)}, u32[]{:S(2)}, u32[]{:S(2)}) collective-permute-start(f32[96,384]{1,0:T(8,128)S(1)} %get-tuple-element.181), channel_id=1, source_target_pairs={{0,1},{1,0},{2,3},{3,2},{4,5},{5,4},{6,7},{7,6},{8,9},{9,8},{10,11... | collective-permute-start | bytes 442376 | tf_op jit(solution)/shard_map/ppermute | solution.py:584
  86.2 7.1 %collective-permute-start.27 = (f32[40,1152]{1,0:T(8,128)S(1)}, f32[40,1152]{1,0:T(8,128)S(1)}, u32[]{:S(2)}, u32[]{:S(2)}) collective-permute-start(f32[40,1152]{1,0:T(8,128)S(1)} %get-tuple-element.192.refs_10_), channel_id=1, source_target_pairs={{0,1},{1,0},{2,3},{3,2},{4,5},{5,4},{6,7},{7,6},{8,9},{9,8},{10,11... | collective-permute-start | bytes 552968 | tf_op jit(solution)/shard_map/ppermute | solution.py:584
  (13 other events, 53.0 us)
